TPU v7x, 32 devices: a whole 2x2x4 slice. The times are simulated.
32 devices in a mesh: px: 2 (over y), py: 16 (over z, x, core).
Axes of the slice: x: 2, y: 2, z: 4, core: 2. Of those that a mesh axis runs over, the one named last changes fastest.
Arguments:
- velocity: float32 [3, 128, 128, 128], P(None, 'px', 'py'), may hold values from -4 to 4
- cotangent: float32 [3, 128, 128, 128], P(None, 'px', 'py'), may hold values from -6 to 6
- weight_in: bfloat16 [32, 3, 3, 3, 3], replicated, may hold values from -0.625 to 0.625
- bias_in: float32 [32], replicated, may hold values from -3 to 3
- weight_out: bfloat16 [6, 32, 3, 3, 3], replicated, may hold values from -0.21875 to 0.21875
Outputs:
- adjoint: float32 [3, 128, 128, 128], P(None, 'px', 'py')
All inputs are finite; a program needn't handle non-finite values.
Results may differ from a plain program's by a relative error of at most 0.00041.
Values sent between devices are 32-bit elements; how exact they have to be, the bound alone decides.
A program may use at most 192 MiB of HBM per device.

v0:
```python
import math

import jax
import jax.numpy as jnp
from jax import lax
from jax.sharding import PartitionSpec as P

NX = 128
NY = 128
NZ = 128


time_step = 0.005
highest = lax.Precision.HIGHEST


def padded(block, sides, width):
    for axis, dim in sides:
        count = lax.axis_size(axis)
        forward = [(i, i + 1) for i in range(count - 1)]
        forward.append((count - 1, 0))
        backward = [(target, source) for source, target in forward]
        low = lax.ppermute(
            lax.slice_in_dim(block, block.shape[dim] - width, None, axis=dim), axis, forward
        )
        high = lax.ppermute(lax.slice_in_dim(block, 0, width, axis=dim), axis, backward)
        block = jnp.concatenate([low, block, high], axis=dim)
    return block


def shifted(source, spatial, offset, margin):
    slicers = [slice(None)]
    for position in range(1, 4):
        extent = source.shape[position]
        offset_now = offset if position == spatial else 0
        slicers.append(slice(margin + offset_now, extent - margin + offset_now))
    return source[tuple(slicers)]


def central(source, spatial, spacing):
    return (shifted(source, spatial, 1, 1) - shifted(source, spatial, -1, 1)) / (2.0 * spacing)


def sixth_order(source, spatial, spacing):
    first = shifted(source, spatial, 1, 3) - shifted(source, spatial, -1, 3)
    second = shifted(source, spatial, 2, 3) - shifted(source, spatial, -2, 3)
    third = shifted(source, spatial, 3, 3) - shifted(source, spatial, -3, 3)
    return (45.0 * first - 9.0 * second + third) / (60.0 * spacing)


def correlate(source, kernel):
    result = lax.conv_general_dilated(
        source[None],
        kernel,
        (1, 1, 1),
        "VALID",
        dimension_numbers=("NCDHW", "OIDHW", "NCDHW"),
        preferred_element_type=jnp.float32,
    )
    return result[0]


def step_adjoint(vel_ext, lam_ext, weight_in, bias_in, weight_out, spacings):
    low_velocity = vel_ext[:, 1:-1, 1:-1, 1:-1].astype(jnp.bfloat16)
    pre_act = correlate(low_velocity, weight_in) + bias_in[:, None, None, None]
    tanh_slope = 1.0 - jnp.square(jnp.tanh(pre_act))
    lam_grads = [
        [
            central(lam_ext[component : component + 1], direction + 1, spacings[direction])[0]
            for direction in range(3)
        ]
        for component in range(3)
    ]
    stress_adj = jnp.stack(
        [
            lam_grads[0][0],
            lam_grads[1][1],
            lam_grads[2][2],
            lam_grads[0][1] + lam_grads[1][0],
            lam_grads[0][2] + lam_grads[2][0],
            lam_grads[1][2] + lam_grads[2][1],
        ]
    ).astype(jnp.bfloat16)
    kernel_out = jnp.flip(weight_out, (2, 3, 4)).transpose(1, 0, 2, 3, 4)
    hidden_adj = correlate(stress_adj, kernel_out)
    pre_adj = (hidden_adj * tanh_slope).astype(jnp.bfloat16)
    kernel_in = jnp.flip(weight_in, (2, 3, 4)).transpose(1, 0, 2, 3, 4)
    closure_adj = correlate(pre_adj, kernel_in)
    lam_block = lam_ext[:, 3:-3, 3:-3, 3:-3]
    advect = sixth_order(lam_ext * vel_ext[0:1], 1, spacings[0])
    for direction in range(1, 3):
        advect = advect + sixth_order(
            lam_ext * vel_ext[direction : direction + 1], direction + 1, spacings[direction]
        )
    cross_terms = jnp.stack(
        [
            jnp.sum(lam_block * sixth_order(vel_ext, direction + 1, spacings[direction]), axis=0)
            for direction in range(3)
        ]
    )
    advect = advect - cross_terms
    return lam_block + time_step * (advect + closure_adj)


def tables(length, mode_count):
    products = (
        jnp.arange(length, dtype=jnp.int32)[:, None]
        * jnp.arange(mode_count, dtype=jnp.int32)[None, :]
        % length
    )
    phases = products.astype(jnp.float32) * (2.0 * math.pi / length)
    return (jnp.cos(phases), jnp.sin(phases))


def signed(wave_index, length):
    return jnp.where(wave_index > length // 2, wave_index - length, wave_index).astype(jnp.float32)


def body(velocity, cotangent, weight_in, bias_in, weight_out):
    mode_count = NZ
    weights_z = jnp.ones((mode_count,), jnp.float32)
    cos_z, sin_z = tables(NZ, mode_count)
    cos_y, sin_y = tables(NY, NY)
    cos_x, sin_x = tables(NX, NX)
    real_z = jnp.einsum("cxyz,zk->cxyk", cotangent, cos_z, precision=highest)
    imag_z = -jnp.einsum("cxyz,zk->cxyk", cotangent, sin_z, precision=highest)
    stacked = jnp.stack([real_z, imag_z])
    pieces = lax.all_to_all(stacked, "py", split_axis=4, concat_axis=3, tiled=True)
    real_part = jnp.einsum("cxyk,yl->ckxl", pieces[0], cos_y, precision=highest) + jnp.einsum(
        "cxyk,yl->ckxl", pieces[1], sin_y, precision=highest
    )
    imag_part = jnp.einsum("cxyk,yl->ckxl", pieces[1], cos_y, precision=highest) - jnp.einsum(
        "cxyk,yl->ckxl", pieces[0], sin_y, precision=highest
    )
    mixed_y = jnp.stack([real_part, imag_part])
    pieces = lax.all_to_all(mixed_y, "px", split_axis=4, concat_axis=3, tiled=True)
    real_part = jnp.einsum("ckxl,xm->cklm", pieces[0], cos_x, precision=highest) + jnp.einsum(
        "ckxl,xm->cklm", pieces[1], sin_x, precision=highest
    )
    imag_part = jnp.einsum("ckxl,xm->cklm", pieces[1], cos_x, precision=highest) - jnp.einsum(
        "ckxl,xm->cklm", pieces[0], sin_x, precision=highest
    )
    spectral = jnp.stack([real_part, imag_part])
    local_kz = spectral.shape[2]
    local_ky = spectral.shape[3]
    index_z = lax.axis_index("py") * local_kz + jnp.arange(local_kz, dtype=jnp.int32)
    index_y = lax.axis_index("px") * local_ky + jnp.arange(local_ky, dtype=jnp.int32)
    index_x = jnp.arange(NX, dtype=jnp.int32)
    retain = (
        (index_z != NZ // 2)[:, None, None]
        & (index_y != NY // 2)[None, :, None]
        & (index_x != NX // 2)[None, None, :]
    ).astype(jnp.float32)
    wave_z = signed(index_z, NZ)[:, None, None]
    wave_y = signed(index_y, NY)[None, :, None]
    wave_x = signed(index_x, NX)[None, None, :]
    wavenumbers = jnp.stack(jnp.broadcast_arrays(wave_x, wave_y, wave_z))
    squared = jnp.sum(wavenumbers * wavenumbers, axis=0)
    inverse = jnp.where(squared > 0, 1.0 / jnp.maximum(squared, 1.0), 0.0)
    dotted = jnp.sum(wavenumbers[None] * spectral, axis=1) * inverse
    projected = (spectral - wavenumbers[None] * dotted[:, None]) * retain
    real_x = jnp.einsum("cklm,mx->ckxl", projected[0], cos_x, precision=highest) - jnp.einsum(
        "cklm,mx->ckxl", projected[1], sin_x, precision=highest
    )
    imag_x = jnp.einsum("cklm,mx->ckxl", projected[0], sin_x, precision=highest) + jnp.einsum(
        "cklm,mx->ckxl", projected[1], cos_x, precision=highest
    )
    inverse_x = jnp.stack([real_x, imag_x])
    pieces = lax.all_to_all(inverse_x, "px", split_axis=3, concat_axis=4, tiled=True)
    real_part = jnp.einsum("ckxl,ly->cxyk", pieces[0], cos_y, precision=highest) - jnp.einsum(
        "ckxl,ly->cxyk", pieces[1], sin_y, precision=highest
    )
    imag_part = jnp.einsum("ckxl,ly->cxyk", pieces[0], sin_y, precision=highest) + jnp.einsum(
        "ckxl,ly->cxyk", pieces[1], cos_y, precision=highest
    )
    returned = jnp.stack([real_part, imag_part])
    cell_total = float(NX * NY * NZ)
    back_cos = (cos_z * weights_z[None, :]).T / cell_total
    back_sin = (sin_z * weights_z[None, :]).T / cell_total
    pieces = lax.all_to_all(returned, "py", split_axis=3, concat_axis=4, tiled=True)
    lam = jnp.einsum("cxyk,kz->cxyz", pieces[0], back_cos, precision=highest) - jnp.einsum(
        "cxyk,kz->cxyz", pieces[1], back_sin, precision=highest
    )
    stacked_fields = jnp.concatenate([velocity, lam], axis=0)
    bordered = padded(stacked_fields, (("px", 1), ("py", 2)), 3)
    bordered = jnp.concatenate([bordered[..., -3:], bordered, bordered[..., :3]], axis=3)
    spacings = (2.0 * math.pi / NX, 2.0 * math.pi / NY, 2.0 * math.pi / NZ)
    return step_adjoint(bordered[:3], bordered[3:], weight_in, bias_in, weight_out, spacings)


def solution(mesh):
    placed = (P(None, "px", "py", None), P(None, "px", "py", None), P(), P(), P())
    return jax.shard_map(
        body, mesh=mesh, in_specs=placed, out_specs=P(None, "px", "py", None), check_vma=False
    )
```

profile of v0, /device:TPU:0, one launch (start us, length us, event | category | flops | bytes accessed | tf_op | source)
XLA Modules:
  0.0 1860.4 jit_solution(9369123575079862994)
XLA Ops:
  3.4 2.3 copy.97
  5.7 4.4 reshape.204
  10.1 7.5 all-to-all-start
  18.0 31.6 %all-to-all-done = f32[16,1,24576]{2,1,0:T(1,128)S(1)} async-done(((f32[16,1,24576]{2,1,0:T(1,128)}), f32[16,1,24576]{2,1,0:T(1,128)S(1)}, u32[]{:S(2)}, u32[]{:S(2)}) %all-to-all-start) | async-done | bytes 1572896 | tf_op jit(solution)/shard_map/all_to_all | solution.py:128
  50.1 6.0 reduce
  56.1 3.5 reshape.205
  59.6 2.8 copy.159
  65.6 2.8 copy.101
  68.4 1.9 copy.102
  73.5 2.5 copy.105
  76.0 4.3 reshape.206
  80.3 3.7 all-to-all-start.1
  85.6 18.7 %all-to-all-done.1 = f32[2,1,196608]{2,1,0:T(1,128)S(1)} async-done(((f32[2,1,196608]{2,1,0:T(1,128)}), f32[2,1,196608]{2,1,0:T(1,128)S(1)}, u32[]{:S(2)}, u32[]{:S(2)}) %all-to-all-start.1) | async-done | bytes 1572896 | tf_op jit(solution)/shard_map/all_to_all | solution.py:136
  104.4 6.6 reduce.1
  110.9 4.8 reshape.207
  115.7 4.3 copy.158
  122.3 2.7 squeeze.25
  134.2 2.3 copy.107
  136.5 3.4 reshape.208
  139.9 23.0 %all_to_all.60 = f32[2,1,196608]{2,1,0:T(1,128)} all-to-all(f32[2,1,196608]{2,1,0:T(1,128)S(1)} %reshape.208), channel_id=1, replica_groups=mesh['px'=2,'py'=16] {'px'}, dimensions={0} | all-to-all | bytes 3145728 | tf_op jit(solution)/shard_map/all_to_all | solution.py:169
  162.9 6.4 reduce.2
  169.3 3.4 reshape.209
  172.7 4.3 copy.157
  178.4 2.5 squeeze.55
  182.0 1.9 fusion.131
  184.8 2.2 fusion.33
  188.1 2.3 copy.109
  190.4 4.4 reshape.210
  194.9 44.7 %all_to_all.61 = f32[16,1,24576]{2,1,0:T(1,128)S(1)} all-to-all(f32[16,1,24576]{2,1,0:T(1,128)} %reshape.210), channel_id=1, replica_groups=mesh['px'=2,'py'=16] {'py'}, dimensions={0} | all-to-all | bytes 3145728 | tf_op jit(solution)/shard_map/all_to_all | solution.py:180
  239.6 6.0 reduce.3
  245.5 3.5 reshape.211
  249.1 2.1 copy.110
  253.1 2.7 copy.114
  257.4 2.2 convolution_subtract_fusion
  261.7 3.1 collective-permute-done
  266.7 2.3 collective-permute-start.3
  270.4 6.8 collective-permute-done.3
  277.4 4.6 collective-permute-done.2
  284.2 9.7 pad_maximum_fusion
  294.8 2.0 fusion.103
  296.8 1.8 slice_bitcast_fusion.2
  298.6 2.7 copy.138
  301.3 2.6 pad.2.clone
  303.9 3.6 reshape.184
  307.5 3.1 fusion.105
  310.6 2.9 fusion.107
  313.6 4.3 fusion.109
  321.4 5.5 copy.137
  326.8 2.0 pad.clone
  328.8 5.7 reshape.179
  334.5 32.3 %copy.127 = bf16[3,68,12,1,8,17]{4,0,5,2,1,3:T(4,128)(2,1)} copy(bf16[3,68,12,1,8,17]{1,5,4,2,0,3:T(8,128)(2,1)S(1)} %copy-done.15) | data formatting | bytes 1331712 | tf_op jit(solution)/shard_map/conv_general_dilated | solution.py:52
  366.8 2.4 slice.477
  369.2 11.3 fusion.301
  380.5 66.7 %copy.123 = bf16[6,68,12,1,8,17]{0,4,5,2,1,3:T(8,128)(2,1)} copy(bf16[6,68,12,1,8,17]{1,5,4,2,0,3:T(8,128)(2,1)} %reshape.179) | data formatting | bytes 2663424 | tf_op jit(solution)/shard_map/conv_general_dilated | solution.py:52
  447.2 4.8 slice.475
  452.0 80.9 %fusion.21 = f32[66,10,8,17,32]{4,2,3,1,0:T(8,128)} fusion(bf16[32,3,3,3,3]{0,4,3,2,1:T(4,128)(2,1)S(1)} %copy-done.24, bf16[3,68,12,8,19]{3,0,4,2,1:T(4,128)(2,1)} %fusion.301), kind=kOutput, calls=%fused_computation.22 | convolution fusion | flops 465315840 | bytes 12238656 | tf_op jit(solution)/shard_map/conv_general_dilated | solution.py:52
  532.9 73.7 %select_bitcast_fusion = bf16[66,10,1,8,17,32]{5,3,4,1,0,2:T(8,128)(2,1)} fusion(pred[8,17]{0,1:T(8,128)(4,1)S(1)} %copy-done.27, f32[32]{0:T(128)S(1)} %copy-done.26, f32[66,10,8,17,32]{4,2,3,1,0:T(8,128)} %fusion.21, bf16[6,68,12,1,7,2]{0,4,5,2,1,3:T(8,128)(2,1)} %slice.475, bf16[6,68,12,1,8,17]{0,4,5,2,1,3:T(8,128)(2,1)} %copy.123, ...), kind=kOutput, calls=%fused_computation.19 | convolution fusion | flops 958075392 | bytes 18713352 | tf_op jit(solution)/shard_map/conv_general_dilated | solution.py:52
  606.6 2.6 slice.478
  609.2 1195.2 %fusion.14 = f32[64,8,8,17,3]{2,4,3,1,0:T(4,128)} fusion(bf16[66,10,1,7,2,32]{5,3,4,1,0,2:T(8,128)(2,1)S(1)} %slice.478, bf16[66,10,1,8,17,32]{5,3,4,1,0,2:T(8,128)(2,1)} %select_bitcast_fusion, bf16[32,3,3,3,3]{0,4,3,2,1:T(4,128)(2,1)S(1)} %copy-done.25), kind=kOutput, calls=%fused_computation.15 | convolution fusion | flops 380233728 | bytes 7176768 | tf_op jit(solution)/shard_map/conv_general_dilated | solution.py:52
  1804.4 15.3 copy.130
  1821.0 1.9 copy.136
  1823.0 8.0 slice_multiply_fusion.2
  1833.0 5.0 fusion.60
  1838.0 22.1 %fusion.85 = f32[3,64,8,128]{3,2,1,0:T(8,128)} fusion(f32[3,64,8,128]{3,2,1,0:T(8,128)S(1)} %copy-done.4, f32[3,70,14,134]{3,2,1,0:T(8,128)} %get-tuple-element.7, f32[3,70,14,134]{3,2,1,0:T(8,128)} %get-tuple-element.6, f32[3,70,14,134]{3,2,1,0:T(8,128)} %get-tuple-element.5, f32[1,64,8,128]{3,2,1,0:T(8,128)S(1)} %bitcast.237, ...), kind=kLoop, calls=%fused_computation.155 | loop fusion | flops 5898240 | bytes 17301504 | tf_op jit(solution)/shard_map/add | solution.py:102
  (129 shorter events, 46.9 us)
Async XLA Ops:
  0.0 1.1 copy-start
  10.1 39.5 %all-to-all-start = ((f32[16,1,24576]{2,1,0:T(1,128)}), f32[16,1,24576]{2,1,0:T(1,128)S(1)}, u32[]{:S(2)}, u32[]{:S(2)}) async-start(f32[16,1,24576]{2,1,0:T(1,128)} %reshape.204), calls=%async_computation | async-start | bytes 3145728 | tf_op jit(solution)/shard_map/all_to_all | solution.py:128
  80.3 24.1 %all-to-all-start.1 = ((f32[2,1,196608]{2,1,0:T(1,128)}), f32[2,1,196608]{2,1,0:T(1,128)S(1)}, u32[]{:S(2)}, u32[]{:S(2)}) async-start(f32[2,1,196608]{2,1,0:T(1,128)} %reshape.206), calls=%async_computation.1 | async-start | bytes 3145728 | tf_op jit(solution)/shard_map/all_to_all | solution.py:136
  128.1 1.3 copy-start.22
  128.1 1.4 copy-start.21
  255.9 3.7 copy-start.5
  259.6 24.5 %copy-start.3 = (f32[3,64,8,128]{3,2,1,0:T(8,128)}, f32[3,64,8,128]{3,2,1,0:T(8,128)S(1)}, u32[]{:S(2)}) copy-start(f32[3,64,8,128]{3,2,1,0:T(8,128)S(1)} %convolution_subtract_fusion) | copy-start | bytes 2359300
  259.6 5.2 collective-permute-start
  260.0 6.2 collective-permute-start.1
  264.8 19.3 %copy-start.16 = (f32[6,3,8,128]{3,2,1,0:T(8,128)}, f32[6,3,8,128]{3,2,1,0:T(8,128)S(1)}, u32[]{:S(2)}) copy-start(f32[6,3,8,128]{3,2,1,0:T(8,128)S(1)} %collective-permute-done) | copy-start | bytes 221188
  266.2 17.9 copy-start.18
  266.7 10.5 collective-permute-start.3
  269.0 13.0 collective-permute-start.2
  277.4 6.8 copy-start.11
  282.2 1.9 copy-start.13
  284.1 9.7 copy-start.7
  284.1 9.7 copy-start.9
  293.9 3.0 copy-start.2
  303.9 13.9 slice-start
  310.6 7.3 slice-start.1
  328.8 5.7 copy-start.15
  447.2 4.8 copy-start.24
  452.0 80.9 %copy-start.23 = (bf16[6,32,3,3,3]{1,4,3,2,0:T(4,128)(2,1)S(1)}, bf16[6,32,3,3,3]{1,4,3,2,0:T(4,128)(2,1)}, u32[]{:S(2)}) copy-start(bf16[6,32,3,3,3]{1,4,3,2,0:T(4,128)(2,1)} %param.9) | copy-start | bytes 31108
  452.0 80.9 %copy-start.26 = (f32[32]{0:T(128)S(1)}, f32[32]{0:T(128)}, u32[]{:S(2)}) copy-start(f32[32]{0:T(128)} %param.8) | copy-start | bytes 388
  452.0 80.9 %copy-start.27 = (pred[8,17]{0,1:T(8,128)(4,1)S(1)}, pred[8,17]{0,1:T(8,128)(4,1)}, u32[]{:S(2)}) copy-start(pred[8,17]{0,1:T(8,128)(4,1)} %constant.94) | copy-start | bytes 412
  606.6 2.6 copy-start.25
  1822.9 8.0 copy-start.4
  1822.9 8.0 copy-start.6
  1822.9 8.0 copy-start.12
  1822.9 8.0 copy-start.14
  1823.0 8.0 copy-start.17
  1823.0 8.0 copy-start.19
  1823.0 9.4 copy-start.10
  1831.0 2.0 copy-start.8
  1833.0 5.0 copy-start.20
  1838.0 22.1 %copy-start.1 = (f32[3,64,8,128]{3,2,1,0:T(8,128)S(1)}, f32[3,64,8,128]{3,2,1,0:T(8,128)}, u32[]{:S(2)}) copy-start(f32[3,64,8,128]{3,2,1,0:T(8,128)} %param.6) | copy-start | bytes 2359300
where the time goes:
time: 1870 us; the launch traced here: 1860 us
  matrix products  1370 us (73%)
  local copies, waits for them, and re-layouts  233 us (12%)
  other arithmetic  103 us (6%)
  blocking collectives  67.7 us (4%)
  waiting for transfers between devices  66.2 us (4%)
    conv_general_dilated x3, matrix products, correlate(): lax.conv_general_dilated(source[None], kernel, (1, 1, 1), 'VALID', dimens...  1350 us
    conv_general_dilated x8, local copies, waits for them, and re-layouts, correlate(): lax.conv_general_dilated(source[None], kernel, (1, 1, 1), 'VALID', dimens...  132 us
    all_to_all x1, blocking collectives, body(): lax.all_to_all(returned, 'py', split_axis=3, concat_axis=4, tiled=True)  44.7 us
    unnamed x71, local copies, waits for them, and re-layouts  43.7 us
  transfers between devices with their start and end apart: 6, of which 6 were waited for; matrix products, arithmetic and copies ran while one was open for 0% of the time, Pallas kernels for 0%

commit v1 on v0

v1 whole, which is shorter than its diff:
```python
import functools
import math

import jax
import jax.numpy as jnp
import numpy as np
from jax import lax
from jax.experimental import pallas as pl
from jax.experimental.pallas import tpu as pltpu
from jax.sharding import PartitionSpec as P

time_step = 0.005
high = lax.Precision.HIGH
LANES = 128
taps = ((1, 45.0), (2, -9.0), (3, 1.0))


def rows_of(ny):
    return -(-(ny + 6) // 8) * 8


def halo(block, axis, dim, width):
    count = lax.axis_size(axis)
    forward = [(i, (i + 1) % count) for i in range(count)]
    backward = [(target, source) for source, target in forward]
    low = lax.ppermute(
        lax.slice_in_dim(block, block.shape[dim] - width, None, axis=dim), axis, forward
    )
    high_side = lax.ppermute(lax.slice_in_dim(block, 0, width, axis=dim), axis, backward)
    return low, high_side


def bordered(block):
    low, up = halo(block, "py", 2, 3)
    ny = block.shape[2]
    extra = rows_of(ny) - ny - 6
    parts = [low, block, up]
    if extra:
        parts.append(jnp.zeros(block.shape[:2] + (extra,) + block.shape[3:], block.dtype))
    wide = jnp.concatenate(parts, axis=2)
    low, up = halo(wide, "px", 1, 3)
    return jnp.concatenate([low, wide, up], axis=1)


def closure_kernel(sizes, vel, lam, w1, b1, w2, w3, out, vs, ss, acc):
    nx, ny, rows, half, spacings = sizes
    vblock, sblock = 9 * rows, 18 * rows
    inv2 = [1.0 / (2.0 * h) for h in spacings]
    inv60 = [1.0 / (60.0 * h) for h in spacings]

    def zroll(value, shift):
        return pltpu.roll(value, shift % LANES, value.ndim - 1)

    def prepare(k, side):
        e = k + 1 + side * half
        lanes = slice(side * LANES, (side + 1) * LANES)
        v = vel[:, e].reshape(3 * rows, LANES)
        l = [lam[c, e] for c in range(3)]
        dx = [(lam[c, e + 1] - lam[c, e - 1]) * inv2[0] for c in range(3)]
        dy = [(pltpu.roll(l[c], rows - 1, 0) - pltpu.roll(l[c], 1, 0)) * inv2[1] for c in range(3)]
        dz = [(zroll(l[c], -1) - zroll(l[c], 1)) * inv2[2] for c in range(3)]
        s = jnp.concatenate(
            [dx[0], dy[1], dz[2], dy[0] + dx[1], dz[0] + dx[2], dz[1] + dy[2]], axis=0
        )
        for t in range(3):
            vs[pl.ds(pl.multiple_of(k * vblock + t * 3 * rows, 8), 3 * rows), lanes] = zroll(
                v, 1 - t
            ).astype(jnp.bfloat16)
            ss[pl.ds(pl.multiple_of(k * sblock + t * 6 * rows, 8), 6 * rows), lanes] = zroll(
                s, 1 - t
            ).astype(jnp.bfloat16)

    @pl.loop(0, half + 2)
    def _(k):
        prepare(k, 0)
        prepare(k, 1)

    acc[...] = jnp.zeros_like(acc)

    def step(i):
        pre = jnp.dot(
            w1[...],
            vs[pl.ds(pl.multiple_of(i * vblock, 16), 3 * vblock), :],
            preferred_element_type=jnp.float32,
        )
        hid = jnp.dot(
            w2[...],
            ss[pl.ds(pl.multiple_of(i * sblock, 16), 3 * sblock), :],
            preferred_element_type=jnp.float32,
        )
        t = jnp.tanh(pre + b1[...])
        p = (hid * (1.0 - t * t)).astype(jnp.bfloat16)
        c = jnp.dot(w3[...], p, preferred_element_type=jnp.float32)
        for d in range(3):
            acc[i + d] += c[d * 9 * ny : (d + 1) * 9 * ny]

    @pl.loop(0, half)
    def _(i):
        step(i)

    for d in range(2):
        acc[half + d, :, :LANES] += acc[d, :, LANES:]

    def finish(x, idx, side):
        e = x + 3
        lanes = slice(side * LANES, (side + 1) * LANES)
        low = [acc[idx, d * 3 * ny : (d + 1) * 3 * ny, lanes] for d in range(3)]
        closure = zroll(low[0], -1) + low[1] + zroll(low[2], 1)
        mid = slice(3, 3 + ny)
        l0 = [lam[c, e, mid] for c in range(3)]
        v0 = [vel[c, e, mid] for c in range(3)]
        total = [closure[c * ny : (c + 1) * ny] for c in range(3)]
        lz = [l0[c] * v0[2] for c in range(3)]
        for b in range(3):
            grad_flux = [0.0] * 3
            grad_vel = [0.0] * 3
            for d, weight in taps:
                for sign in (1, -1):
                    q = d * sign
                    if b == 0:
                        vq = [vel[c, e + q, mid] for c in range(3)]
                        fq = [lam[c, e + q, mid] * vq[0] for c in range(3)]
                    elif b == 1:
                        ys = slice(3 + q, 3 + q + ny)
                        vq = [vel[c, e, ys] for c in range(3)]
                        fq = [lam[c, e, ys] * vq[1] for c in range(3)]
                    else:
                        vq = [zroll(v0[c], -q) for c in range(3)]
                        fq = [zroll(lz[c], -q) for c in range(3)]
                    w = weight * sign * inv60[b]
                    for c in range(3):
                        grad_flux[c] += w * fq[c]
                        grad_vel[c] += w * vq[c]
            for c in range(3):
                total[c] += grad_flux[c]
            total[b] -= l0[0] * grad_vel[0] + l0[1] * grad_vel[1] + l0[2] * grad_vel[2]
        for c in range(3):
            out[c, x] = l0[c] + time_step * total[c]

    @pl.loop(0, half)
    def _(x):
        finish(x, x + 2, 0)

    @pl.loop(half, nx)
    def _(x):
        finish(x, x + 2 - half, 1)


def band(ny, rows, first):
    table = np.zeros((ny, 3, rows), np.float32)
    for y in range(ny):
        for d in range(3):
            table[y, d, y + d + first] = 1.0
    return jnp.asarray(table, jnp.bfloat16)


def closure_weights(weight_in, bias_in, weight_out, ny, rows):
    hid = weight_in.shape[0]
    w1 = jnp.einsum("ocxyz,pyq->opxzcq", weight_in, band(ny + 2, rows, 1))
    w1 = w1.reshape(hid * (ny + 2), 27 * rows)
    flipped = jnp.flip(weight_out, (2, 3, 4))
    w2 = jnp.einsum("ocxyz,pyq->cpxzoq", flipped, band(ny + 2, rows, 1))
    w2 = w2.reshape(hid * (ny + 2), 54 * rows)
    back = jnp.flip(band(ny, ny + 2, 0), 1)
    w3 = jnp.einsum("ocxyz,pyq->xzcpoq", weight_in, back)
    w3 = w3.reshape(27 * ny, hid * (ny + 2))
    bias = jnp.broadcast_to(bias_in[:, None], (hid, ny + 2)).reshape(hid * (ny + 2), 1)
    return w1, bias, w2, w3


def closure_step(vel_ext, lam_ext, weights, nx, ny, spacings):
    rows = vel_ext.shape[2]
    half = (nx + 2) // 2
    w1, bias, w2, w3 = weights
    kernel = functools.partial(closure_kernel, (nx, ny, rows, half, spacings))
    vm = pl.BlockSpec(memory_space=pltpu.VMEM)
    return pl.pallas_call(
        kernel,
        out_shape=jax.ShapeDtypeStruct((3, nx, ny, LANES), jnp.float32),
        in_specs=[vm] * 6,
        out_specs=vm,
        scratch_shapes=[
            pltpu.VMEM(((half + 2) * 9 * rows, 2 * LANES), jnp.bfloat16),
            pltpu.VMEM(((half + 2) * 18 * rows, 2 * LANES), jnp.bfloat16),
            pltpu.VMEM((half + 2, 9 * ny, 2 * LANES), jnp.float32),
        ],
        compiler_params=pltpu.CompilerParams(vmem_limit_bytes=50 * 2**20),
        name="closure",
    )(vel_ext, lam_ext, w1, bias, w2, w3)


def waves(length, modes):
    products = np.arange(length)[:, None] * np.arange(modes)[None, :] % length
    phases = products.astype(np.float64) * (2.0 * math.pi / length)
    return np.cos(phases), np.sin(phases)


def f32(table):
    return jnp.asarray(np.asarray(table, np.float32))


def project(re, im, index_x, index_y, index_z, sizes):
    NX, NY, NZ = sizes

    def signed(index, length):
        return jnp.where(index > length // 2, index - length, index).astype(jnp.float32)

    wx, wy, wz = signed(index_x, NX), signed(index_y, NY), signed(index_z, NZ)
    squared = wx * wx + wy * wy + wz * wz
    keep = (index_x != NX // 2) & (index_y != NY // 2) & (index_z != NZ // 2)
    inverse = jnp.where(squared > 0, 1.0 / jnp.maximum(squared, 1.0), 0.0)
    done = []
    for part in (re, im):
        dotted = (wx * part[0] + wy * part[1] + wz * part[2]) * inverse
        done.append([jnp.where(keep, part[c] - w * dotted, 0.0) for c, w in enumerate((wx, wy, wz))])
    return jnp.stack(done[0]), jnp.stack(done[1])


def einsum(*args):
    return jnp.einsum(*args, precision=high)


def mode_weights(NX, NY, NZ):
    scale = np.full((NZ // 2,), 2.0 / (NX * NY * NZ))
    scale[0] /= 2.0
    return scale


def projected_once(cotangent, sizes, npx, npy):
    NX, NY, NZ = sizes
    _, nx, ny, _ = cotangent.shape
    total = npx * npy
    nj = NZ // 2 // total
    cz, sz = waves(NZ, NZ // 2)
    cy, sy = waves(NY, NY)
    cx, sx = waves(NX, NX)
    forward_z = np.stack([cz, -sz], axis=1).reshape(NZ, 2, total, nj)
    sent = einsum("cxyz,zrdj->drcyjx", cotangent, f32(forward_z))
    sent = sent.reshape(total, 2 * 3 * ny, nj * nx)
    got = lax.all_to_all(sent, ("px", "py"), 0, 0, tiled=True)
    got = got.reshape(npx, npy, 2, 3, ny, nj, nx)
    forward_y = np.stack([np.stack([cy, -sy], 0), np.stack([sy, cy], 0)], 0)
    forward_y = forward_y.reshape(2, 2, npy, ny, NY)
    mixed = einsum("hprcyjx,rRpyl->Rcljhx", got, f32(forward_y))
    mixed = mixed.reshape(2, 3, NY, nj, NX)
    trans = einsum("Rcljx,xSm->SRcljm", mixed, f32(np.stack([cx, sx], 1)))
    re = trans[0, 0] + trans[1, 1]
    im = trans[0, 1] - trans[1, 0]
    me = lax.axis_index("px") * npy + lax.axis_index("py")
    index_z = (me * nj + jnp.arange(nj, dtype=jnp.int32))[None, :, None]
    index_y = jnp.arange(NY, dtype=jnp.int32)[:, None, None]
    index_x = jnp.arange(NX, dtype=jnp.int32)[None, None, :]
    re, im = project(re, im, index_x, index_y, index_z, sizes)
    back = einsum("Rcljm,mSx->SRcljx", jnp.stack([re, im]), f32(np.stack([cx, sx], 1)))
    re = back[0, 0] - back[1, 1]
    im = back[1, 0] + back[0, 1]
    inverse_y = np.stack([np.stack([cy, sy], 0), np.stack([-sy, cy], 0)], 0)
    inverse_y = inverse_y.reshape(2, 2, NY, npy, ny)
    sent = einsum(
        "Rcljhx,Rrlpy->hprcyjx",
        jnp.stack([re, im]).reshape(2, 3, NY, nj, npx, nx),
        f32(inverse_y),
    ).reshape(total, 2 * 3 * ny, nj * nx)
    got = lax.all_to_all(sent, ("px", "py"), 0, 0, tiled=True)
    got = got.reshape(total, 2, 3, ny, nj, nx)
    scale = mode_weights(NX, NY, NZ)
    inverse_z = np.stack([(cz * scale).T, (-sz * scale).T], 0).reshape(2, total, nj, NZ)
    return einsum("drcyjx,rdjz->cxyz", got, f32(inverse_z))


def projected_twice(cotangent, sizes, npx, npy):
    NX, NY, NZ = sizes
    cz, sz = waves(NZ, NZ // 2)
    cy, sy = map(f32, waves(NY, NY))
    cx, sx = map(f32, waves(NX, NX))
    scale = mode_weights(NX, NY, NZ)
    stacked = jnp.stack(
        [einsum("cxyz,zk->cxyk", cotangent, f32(cz)), einsum("cxyz,zk->cxyk", cotangent, f32(-sz))]
    )
    re, im = lax.all_to_all(stacked, "py", split_axis=4, concat_axis=3, tiled=True)
    pair = jnp.stack(
        [
            einsum("cxyk,yl->ckxl", re, cy) + einsum("cxyk,yl->ckxl", im, sy),
            einsum("cxyk,yl->ckxl", im, cy) - einsum("cxyk,yl->ckxl", re, sy),
        ]
    )
    re, im = lax.all_to_all(pair, "px", split_axis=4, concat_axis=3, tiled=True)
    re, im = (
        einsum("ckxl,xm->cklm", re, cx) + einsum("ckxl,xm->cklm", im, sx),
        einsum("ckxl,xm->cklm", im, cx) - einsum("ckxl,xm->cklm", re, sx),
    )
    nk, nl = re.shape[1], re.shape[2]
    index_z = (lax.axis_index("py") * nk + jnp.arange(nk, dtype=jnp.int32))[:, None, None]
    index_y = (lax.axis_index("px") * nl + jnp.arange(nl, dtype=jnp.int32))[None, :, None]
    index_x = jnp.arange(NX, dtype=jnp.int32)[None, None, :]
    re, im = project(re, im, index_x, index_y, index_z, sizes)
    pair = jnp.stack(
        [
            einsum("cklm,mx->ckxl", re, cx) - einsum("cklm,mx->ckxl", im, sx),
            einsum("cklm,mx->ckxl", re, sx) + einsum("cklm,mx->ckxl", im, cx),
        ]
    )
    re, im = lax.all_to_all(pair, "px", split_axis=3, concat_axis=4, tiled=True)
    pair = jnp.stack(
        [
            einsum("ckxl,ly->cxyk", re, cy) - einsum("ckxl,ly->cxyk", im, sy),
            einsum("ckxl,ly->cxyk", re, sy) + einsum("ckxl,ly->cxyk", im, cy),
        ]
    )
    re, im = lax.all_to_all(pair, "py", split_axis=3, concat_axis=4, tiled=True)
    return einsum("cxyk,kz->cxyz", re, f32((cz * scale).T)) - einsum(
        "cxyk,kz->cxyz", im, f32((sz * scale).T)
    )


def body(velocity, cotangent, weight_in, bias_in, weight_out):
    npx, npy = lax.axis_size("px"), lax.axis_size("py")
    _, nx, ny, NZ = velocity.shape
    sizes = (nx * npx, ny * npy, NZ)
    spacings = tuple(2.0 * math.pi / size for size in sizes)
    vel_ext = bordered(velocity)
    weights = closure_weights(weight_in, bias_in, weight_out, ny, rows_of(ny))
    if (NZ // 2) % (npx * npy) == 0:
        lam = projected_once(cotangent, sizes, npx, npy)
    else:
        lam = projected_twice(cotangent, sizes, npx, npy)
    lam_ext = bordered(lam)
    return closure_step(vel_ext, lam_ext, weights, nx, ny, spacings)


def solution(mesh):
    placed = (P(None, "px", "py", None), P(None, "px", "py", None), P(), P(), P())
    return jax.shard_map(
        body, mesh=mesh, in_specs=placed, out_specs=P(None, "px", "py", None), check_vma=False
    )
```

time: 1870 us -> 181 us (0.10)
  matrix products: 1370 us -> 14.7 us
  local copies, waits for them, and re-layouts: 233 us -> 50.6 us
  other arithmetic: 103 us -> 6.59 us
  blocking collectives: 67.7 us -> 0 us
  Pallas kernels: 0 us -> 40.3 us
  waiting for transfers between devices: 66.2 us -> 42.3 us
    conv_general_dilated x3 -> x0, matrix products: 1350 us -> none  [correlate(): lax.conv_general_dilated(source[None], kernel, (1, 1, 1), 'VALID', dimens...]
    conv_general_dilated x8 -> x0, local copies, waits for them, and re-layouts: 132 us -> none  [correlate(): lax.conv_general_dilated(source[None], kernel, (1, 1, 1), 'VALID', dimens...]
    all_to_all x2 -> x0, blocking collectives: 67.7 us -> none  [the longest x1 44.7 us: body(): lax.all_to_all(returned, 'py', split_axis=3, concat_axis=4, tiled=True)]
    unnamed x71 -> x26, local copies, waits for them, and re-layouts: 43.7 us -> 2.05 us
    pallas_call x0 -> x1, Pallas kernels: none -> 40.3 us  [closure_step(): pl.pallas_call(kernel, out_shape=jax.ShapeDtypeStruct((3, nx, ny, LANES),...]
    reshape x0 -> x9, local copies, waits for them, and re-layouts: none -> 27.6 us  [the longest x2 7.17 us: projected_once(): got = got.reshape(total, 2, 3, ny, nj, nx)]
    all_to_all x4 -> x0, other arithmetic: 24.9 us -> none  [the longest x1 6.55 us: body(): lax.all_to_all(mixed_y, 'px', split_axis=4, concat_axis=3, tiled=True)]
    add x1 -> x2, other arithmetic: 22.1 us -> 0.12 us  [the longest x1 0.08 us: project(): squared = wx * wx + wy * wy + wz * wz]
  transfers between devices with their start and end apart: 6 -> 10, of which waited for: 6 -> 3; matrix products, arithmetic and copies ran while one was open for 0% -> 26% of each run, Pallas kernels for 0% -> 0%
where the time goes in v1:
time: 181 us; the launch traced here: 178 us
  local copies, waits for them, and re-layouts  50.6 us (28%)
  waiting for transfers between devices  42.3 us (23%)
  Pallas kernels  40.3 us (22%)
  starting transfers between devices  23 us (13%)
  matrix products  14.7 us (8%)
  other arithmetic  6.59 us (4%)
    all_to_all x2, waiting for transfers between devices, projected_once(): got = lax.all_to_all(sent, ('px', 'py'), 0, 0, tiled=True)  40.8 us
    pallas_call x1, Pallas kernels, closure_step(): pl.pallas_call(kernel, out_shape=jax.ShapeDtypeStruct((3, nx, ny, LANES),...  40.3 us
    all_to_all x2, starting transfers between devices, projected_once(): got = lax.all_to_all(sent, ('px', 'py'), 0, 0, tiled=True)  10.1 us
    ppermute x4, starting transfers between devices, halo(): lax.ppermute(lax.slice_in_dim(block, 0, width, axis=dim), axis, backward)  9.94 us
    dot_general x6, matrix products, einsum(): return jnp.einsum(*args, precision=high)  9.82 us
    reshape x2, local copies, waits for them, and re-layouts, projected_once(): got = got.reshape(total, 2, 3, ny, nj, nx)  7.17 us
    transpose x1, local copies, waits for them, and re-layouts, closure_weights(): w2 = jnp.einsum('ocxyz,pyq->cpxzoq', flipped, band(ny + 2, rows, 1))  6.77 us
    reshape x1, local copies, waits for them, and re-layouts, closure_weights(): w2 = w2.reshape(hid * (ny + 2), 54 * rows)  6 us
  transfers between devices with their start and end apart: 10, of which 3 were waited for; matrix products, arithmetic and copies ran while one was open for 26% of the time, Pallas kernels for 0%

profile of v1, /device:TPU:0, one launch (start us, length us, event | category | flops | bytes accessed | tf_op | source)
XLA Modules:
  0.0 178.0 jit_solution(14470610352587677813)
XLA Ops:
  0.0 1.1 copy-done
  1.1 2.1 %convolution_bitcast_fusion.4 = f32[32,2,3,8,2,64]{5,0,3,2,4,1:T(8,128)S(1)} fusion(f32[128,2,32,2,1,1]{0,2,5,4,3,1:T(8,128)} %constant.54, f32[3,64,8,128,1,1]{3,2,1,0,5,4:T(8,128)S(1)} %bitcast.151), kind=kOutput, calls=%fused_computation.14 | convolution fusion | flops 150994944 | bytes 1638400 | tf_op jit(solution)/shard_map/cxyz,zrdj->drcyjx/dot_general | solution.py:220
  3.3 1.2 copy.31
  4.5 1.8 reshape.223
  6.2 7.3 %all-to-all-start = ((f32[32,48,128]{2,1,0:T(8,128)}), f32[32,48,128]{2,1,0:T(8,128)S(1)}, u32[]{:S(2)}, u32[]{:S(2)}) async-start(f32[32,48,128]{2,1,0:T(8,128)} %reshape.223), calls=%async_computation | async-start | bytes 1572864 | tf_op jit(solution)/shard_map/all_to_all | solution.py:240
  13.5 0.0 copy-start.7
  13.6 0.1 broadcast_and_fusion
  13.7 0.1 broadcast_add_fusion
  13.8 21.3 %all-to-all-done = f32[32,48,128]{2,1,0:T(8,128)S(1)} async-done(((f32[32,48,128]{2,1,0:T(8,128)}), f32[32,48,128]{2,1,0:T(8,128)S(1)}, u32[]{:S(2)}, u32[]{:S(2)}) %all-to-all-start) | async-done | bytes 786464 | tf_op jit(solution)/shard_map/all_to_all | solution.py:240
  35.1 0.9 reshape.224
  36.0 0.0 copy-start.5
  36.0 2.0 %fusion.6 = f32[2,3,128,2,2,64]{2,5,0,3,1,4:T(8,128)S(1)} fusion(f32[2,2,16,8,128,1,1,1]{4,2,3,0,1,7,6,5:T(8,128)S(1)} %copy-done.7, f32[2,16,2,3,8,2,64,1]{6,5,4,3,2,1,0,7:T(2,128)S(1)} %bitcast.152), kind=kOutput, calls=%fused_computation.18 | convolution fusion | flops 301989888 | bytes 1835008 | tf_op jit(solution)/shard_map/hprcyjx,rRpyl->Rcljhx/dot_general | solution.py:220
  38.0 0.1 copy.33
  38.0 0.8 convolution_bitcast_fusion.3
  39.0 0.2 and_select_fusion.5
  39.3 0.2 and_select_fusion.1
  39.4 0.1 maximum_bitcast_fusion.4
  39.5 0.8 convolution_bitcast_fusion.2
  40.3 0.0 copy-start.6
  40.4 0.1 slice_subtract_fusion
  40.4 0.8 copy-done.6
  41.3 0.8 convolution_bitcast_fusion.1
  42.1 2.4 %copy.42 = f32[2,16,2,3,8,2,64]{6,5,4,3,2,1,0:T(2,128)} copy(f32[2,16,2,3,8,2,64]{6,1,4,2,0,5,3:T(8,128)S(1)} %convolution_bitcast_fusion.1) | data formatting | bytes 1572864 | tf_op jit(solution)/shard_map/Rcljhx,Rrlpy->hprcyjx/transpose | solution.py:220
  44.5 3.1 %reshape.226 = f32[32,48,128]{2,1,0:T(8,128)} reshape(f32[2,16,2,3,8,2,64]{6,5,4,3,2,1,0:T(2,128)} %copy.42) | data formatting | bytes 1572864 | tf_op jit(solution)/shard_map/reshape | solution.py:263
  47.6 2.8 %all-to-all-start.1 = ((f32[32,48,128]{2,1,0:T(8,128)}), f32[32,48,128]{2,1,0:T(8,128)S(1)}, u32[]{:S(2)}, u32[]{:S(2)}) async-start(f32[32,48,128]{2,1,0:T(8,128)} %reshape.226), calls=%async_computation.1 | async-start | bytes 1572864 | tf_op jit(solution)/shard_map/all_to_all | solution.py:264
  50.4 1.1 fusion.33
  51.5 4.4 %collective-permute-start.1 = (f32[3,64,3,128]{3,2,1,0:T(4,128)}, f32[3,64,3,128]{3,2,1,0:T(4,128)}, u32[]{:S(2)}, u32[]{:S(2)}) collective-permute-start(f32[3,64,3,128]{3,2,1,0:T(4,128)} %get-tuple-element.18), channel_id=1, source_target_pairs={{1,0},{2,1},{3,2},{4,3},{5,4},{6,5},{7,6},{8,7},{9,8},{10,9},{11,1... | collective-permute-start | bytes 884744 | tf_op jit(solution)/shard_map/ppermute | solution.py:29
  55.9 19.6 %all-to-all-done.1 = f32[32,48,128]{2,1,0:T(8,128)S(1)} async-done(((f32[32,48,128]{2,1,0:T(8,128)}), f32[32,48,128]{2,1,0:T(8,128)S(1)}, u32[]{:S(2)}, u32[]{:S(2)}) %all-to-all-start.1) | async-done | bytes 786464 | tf_op jit(solution)/shard_map/all_to_all | solution.py:264
  75.5 2.0 %reshape.227 = f32[32,2,3,8,2,64]{5,4,3,2,1,0:T(2,128)} reshape(f32[32,48,128]{2,1,0:T(8,128)S(1)} %all-to-all-done.1) | data formatting | bytes 1572864 | tf_op jit(solution)/shard_map/reshape | solution.py:265
  77.5 5.1 %copy.64 = f32[32,2,3,8,2,64]{0,3,1,4,5,2:T(8,128)} copy(f32[32,2,3,8,2,64]{5,4,3,2,1,0:T(2,128)} %reshape.227) | data formatting | bytes 1572864 | tf_op jit(solution)/shard_map/reshape | solution.py:265
  82.6 3.3 %convolution_bitcast_fusion.7 = f32[3,64,8,128]{3,2,1,0:T(8,128)S(1)} fusion(f32[32,2,3,8,2,64]{0,3,1,4,5,2:T(8,128)} %copy.64, f32[2,32,2,128,1,1]{3,1,0,2,5,4:T(8,128)S(1)} %copy-done.9), kind=kOutput, calls=%fused_computation.17 | convolution fusion | flops 150994944 | bytes 1638400 | tf_op jit(solution)/shard_map/drcyjx,rdjz->cxyz/dot_general | solution.py:220
  85.9 0.0 copy-start.8
  85.9 0.0 copy-start.10
  86.0 1.0 fusion.32
  87.0 0.0 collective-permute-start.4
  87.0 4.4 %collective-permute-start.5 = (f32[3,64,3,128]{3,2,1,0:T(4,128)}, f32[3,64,3,128]{3,2,1,0:T(4,128)}, u32[]{:S(2)}, u32[]{:S(2)}) collective-permute-start(f32[3,64,3,128]{3,2,1,0:T(4,128)} %get-tuple-element.16), channel_id=1, source_target_pairs={{1,0},{2,1},{3,2},{4,3},{5,4},{6,5},{7,6},{8,7},{9,8},{10,9},{11,1... | collective-permute-start | bytes 884744 | tf_op jit(solution)/shard_map/ppermute | solution.py:29
  91.4 0.5 convolution_bitcast_fusion.5
  92.0 0.9 rev.8
  92.9 2.9 %convolution_bitcast_fusion = bf16[32,10,3,3,6,16]{0,5,3,2,4,1:T(8,128)(2,1)} fusion(bf16[10,3,16,1,1,1]{2,1,5,4,3,0:T(4,128)(2,1)} %constant.59, bf16[6,32,3,3,3]{1,4,3,2,0:T(4,128)(2,1)S(1)} %rev.8), kind=kOutput, calls=%fused_computation.8 | convolution fusion | flops 1658880 | bytes 564288 | tf_op jit(solution)/shard_map/ocxyz,pyq->cpxzoq/dot_general | solution.py:162
  95.8 0.0 collective-permute-done
  95.8 0.0 collective-permute-done.1
  95.8 1.5 collective-permute-done.4
  97.3 0.0 collective-permute-done.5
  97.3 0.1 broadcast.257
  97.3 0.0 copy-start.3
  97.4 0.0 copy-start.11
  97.4 2.1 %pad_maximum_fusion.2 = (f32[3,64,16,128]{3,2,1,0:T(8,128)S(1)}, f32[3,64,16,128]{3,2,1,0:T(8,128)S(1)}) fusion(f32[3,64,2,128]{3,2,1,0:T(2,128)S(1)} %broadcast.257, f32[3,64,3,128]{3,2,1,0:T(4,128)} %collective-permute-done.5, f32[3,64,8,128]{3,2,1,0:T(8,128)S(1)} %convolution_bitcast_fusion.7, f32[3,64,3,128]{3,2,1,0:T(4,128)} %collective-permute-done.4, ...), kind=kLoop, calls=%fused_computation.2 | loop fusion | flops 2359296 | bytes 6094848 | tf_op jit(solution)/shard_map/concatenate | solution.py:40
  99.5 0.7 fusion.31
  100.2 1.5 collective-permute-start.2
  101.6 0.5 collective-permute-start.3
  102.2 0.7 fusion.30
  102.8 1.5 collective-permute-start.6
  104.3 0.5 collective-permute-start.7
  104.9 1.5 convolution_bitcast_fusion.6
  106.3 6.8 %copy.48 = bf16[32,10,3,3,6,16]{5,4,3,2,1,0:T(8,128)(2,1)} copy(bf16[32,10,3,3,6,16]{0,5,3,2,4,1:T(8,128)(2,1)} %convolution_bitcast_fusion) | data formatting | bytes 1105920 | tf_op jit(solution)/shard_map/ocxyz,pyq->cpxzoq/transpose | solution.py:162
  113.1 6.0 %reshape.230.w2 = bf16[320,864]{1,0:T(8,128)(2,1)S(1)} reshape(bf16[32,10,3,3,6,16]{5,4,3,2,1,0:T(8,128)(2,1)} %copy.48) | data formatting | bytes 1105920 | tf_op jit(solution)/shard_map/reshape | solution.py:163
  119.1 3.6 %copy.46 = bf16[32,10,3,3,3,16]{5,4,3,2,1,0:T(4,128)(2,1)} copy(bf16[32,10,3,3,3,16]{0,5,3,2,4,1:T(8,128)(2,1)S(1)} %convolution_bitcast_fusion.5) | data formatting | bytes 552960 | tf_op jit(solution)/shard_map/ocxyz,pyq->opxzcq/transpose | solution.py:159
  122.8 4.6 %reshape.228.w1 = bf16[320,432]{1,0:T(8,128)(2,1)S(1)} reshape(bf16[32,10,3,3,3,16]{5,4,3,2,1,0:T(4,128)(2,1)} %copy.46) | data formatting | bytes 552960 | tf_op jit(solution)/shard_map/reshape | solution.py:160
  127.3 2.5 %copy.50 = bf16[3,3,3,8,32,10]{5,4,3,2,1,0:T(8,128)(2,1)} copy(bf16[3,3,3,8,32,10]{4,5,1,0,2,3:T(8,128)(2,1)S(1)} %copy-done.2) | data formatting | bytes 276480 | tf_op jit(solution)/shard_map/ocxyz,pyq->xzcpoq/transpose | solution.py:165
  129.8 4.1 %reshape.231.w3 = bf16[216,320]{1,0:T(8,128)(2,1)S(1)} reshape(bf16[3,3,3,8,32,10]{5,4,3,2,1,0:T(8,128)(2,1)} %copy.50) | data formatting | bytes 276480 | tf_op jit(solution)/shard_map/reshape | solution.py:166
  133.9 0.1 broadcast_in_dim.17
  134.0 0.1 reshape.251.b1
  134.1 3.6 %fusion.3 = (f32[3,70,16,128]{3,2,1,0:T(8,128)}, f32[3,70,16,128]{3,2,1,0:T(8,128)S(1)}) fusion(f32[3,64,2,128]{3,2,1,0:T(2,128)S(1)} %copy-done.4, f32[3,3,16,128]{3,2,1,0:T(8,128)} %collective-permute-done.7, f32[3,64,3,128]{3,2,1,0:T(4,128)} %collective-permute-done.5, f32[3,64,8,128]{3,2,1,0:T(8,128)S(1)} %convolution_bitcast_fusion.7, ...), kind=kLoop, calls=%fused_computation.7 | loop fusion | flops 4300800 | bytes 6684672 | tf_op jit(solution)/shard_map/concatenate | solution.py:42
  137.7 40.3 %closure.1 = f32[3,64,8,128]{3,2,1,0:T(8,128)} custom-call(f32[3,70,16,128]{3,2,1,0:T(8,128)S(1)} %get-tuple-element.22.vel, f32[3,70,16,128]{3,2,1,0:T(8,128)} %get-tuple-element.21.lam, bf16[320,432]{1,0:T(8,128)(2,1)S(1)} %reshape.228.w1, f32[320,1]{1,0:T(8,128)S(1)} %reshape.251.b1, bf16[320,864]{1,0:T(8,128)(2,1)S(1)} %reshape.230.w2, ...), custom_call_target="tpu_custom_call" | custom-call | tf_op jit(solution)/shard_map/closure/pallas_call | solution.py:177
  (31 shorter events, 0.2 us)
Async XLA Ops:
  0.0 1.1 copy-start
  6.2 28.8 %all-to-all-start = ((f32[32,48,128]{2,1,0:T(8,128)}), f32[32,48,128]{2,1,0:T(8,128)S(1)}, u32[]{:S(2)}, u32[]{:S(2)}) async-start(f32[32,48,128]{2,1,0:T(8,128)} %reshape.223), calls=%async_computation | async-start | bytes 1572864 | tf_op jit(solution)/shard_map/all_to_all | solution.py:240
  13.5 22.4 %copy-start.7 = (f32[2,2,16,8,128,1,1,1]{4,2,3,0,1,7,6,5:T(8,128)S(1)}, f32[2,2,16,8,128,1,1,1]{4,2,3,0,1,7,6,5:T(8,128)}, u32[]{:S(2)}) copy-start(f32[2,2,16,8,128,1,1,1]{4,2,3,0,1,7,6,5:T(8,128)} %constant.55) | copy-start | bytes 786436
  36.0 2.1 %copy-start.5 = (f32[128,2,128,1,1,1]{2,0,1,5,4,3:T(8,128)S(1)}, f32[128,2,128,1,1,1]{2,0,1,5,4,3:T(8,128)}, u32[]{:S(2)}) copy-start(f32[128,2,128,1,1,1]{2,0,1,5,4,3:T(8,128)} %constant.56) | copy-start | bytes 393220
  40.3 1.0 copy-start.6
  44.5 5.9 %copy-start.1 = (f32[3,64,8,128]{3,2,1,0:T(8,128)S(1)}, f32[3,64,8,128]{3,2,1,0:T(8,128)}, u32[]{:S(2)}) copy-start(f32[3,64,8,128]{3,2,1,0:T(8,128)} %param.14) | copy-start | bytes 2359300
  47.6 27.9 %all-to-all-start.1 = ((f32[32,48,128]{2,1,0:T(8,128)}), f32[32,48,128]{2,1,0:T(8,128)S(1)}, u32[]{:S(2)}, u32[]{:S(2)}) async-start(f32[32,48,128]{2,1,0:T(8,128)} %reshape.226), calls=%async_computation.1 | async-start | bytes 1572864 | tf_op jit(solution)/shard_map/all_to_all | solution.py:264
  51.5 44.3 %collective-permute-start = (f32[3,64,3,128]{3,2,1,0:T(4,128)}, f32[3,64,3,128]{3,2,1,0:T(4,128)}, u32[]{:S(2)}, u32[]{:S(2)}) collective-permute-start(f32[3,64,3,128]{3,2,1,0:T(4,128)} %get-tuple-element.17), channel_id=1, source_target_pairs={{0,1},{1,2},{2,3},{3,4},{4,5},{5,6},{6,7},{7,8},{8,9},{9,10},{10,1... | collective-permute-start | bytes 884744 | tf_op jit(solution)/shard_map/ppermute | solution.py:26
  51.5 44.3 %collective-permute-start.1 = (f32[3,64,3,128]{3,2,1,0:T(4,128)}, f32[3,64,3,128]{3,2,1,0:T(4,128)}, u32[]{:S(2)}, u32[]{:S(2)}) collective-permute-start(f32[3,64,3,128]{3,2,1,0:T(4,128)} %get-tuple-element.18), channel_id=1, source_target_pairs={{1,0},{2,1},{3,2},{4,3},{5,4},{6,5},{7,6},{8,7},{9,8},{10,9},{11,1... | collective-permute-start | bytes 884744 | tf_op jit(solution)/shard_map/ppermute | solution.py:29
  77.5 5.1 %copy-start.9 = (f32[2,32,2,128,1,1]{3,1,0,2,5,4:T(8,128)S(1)}, f32[2,32,2,128,1,1]{3,1,0,2,5,4:T(8,128)}, u32[]{:S(2)}) copy-start(f32[2,32,2,128,1,1]{3,1,0,2,5,4:T(8,128)} %constant.58) | copy-start | bytes 196612
  85.9 5.5 %copy-start.8 = (bf16[32,3,3,3,3]{0,4,3,2,1:T(4,128)(2,1)S(1)}, bf16[32,3,3,3,3]{0,4,3,2,1:T(4,128)(2,1)}, u32[]{:S(2)}) copy-start(bf16[32,3,3,3,3]{0,4,3,2,1:T(4,128)(2,1)} %param.16) | copy-start | bytes 15556
  85.9 5.5 %copy-start.10 = (bf16[10,3,16,1,1,1]{2,1,5,4,3,0:T(4,128)(2,1)S(1)}, bf16[10,3,16,1,1,1]{2,1,5,4,3,0:T(4,128)(2,1)}, u32[]{:S(2)}) copy-start(bf16[10,3,16,1,1,1]{2,1,5,4,3,0:T(4,128)(2,1)} %constant.59) | copy-start | bytes 2884
  87.0 10.3 %collective-permute-start.4 = (f32[3,64,3,128]{3,2,1,0:T(4,128)}, f32[3,64,3,128]{3,2,1,0:T(4,128)}, u32[]{:S(2)}, u32[]{:S(2)}) collective-permute-start(f32[3,64,3,128]{3,2,1,0:T(4,128)} %get-tuple-element.15), channel_id=1, source_target_pairs={{0,1},{1,2},{2,3},{3,4},{4,5},{5,6},{6,7},{7,8},{8,9},{9,10},{10,1... | collective-permute-start | bytes 884744 | tf_op jit(solution)/shard_map/ppermute | solution.py:26
  87.0 10.3 %collective-permute-start.5 = (f32[3,64,3,128]{3,2,1,0:T(4,128)}, f32[3,64,3,128]{3,2,1,0:T(4,128)}, u32[]{:S(2)}, u32[]{:S(2)}) collective-permute-start(f32[3,64,3,128]{3,2,1,0:T(4,128)} %get-tuple-element.16), channel_id=1, source_target_pairs={{1,0},{2,1},{3,2},{4,3},{5,4},{6,5},{7,6},{8,7},{9,8},{10,9},{11,1... | collective-permute-start | bytes 884744 | tf_op jit(solution)/shard_map/ppermute | solution.py:29
  97.3 2.1 %copy-start.3 = (f32[3,64,2,128]{3,2,1,0:T(2,128)}, f32[3,64,2,128]{3,2,1,0:T(2,128)S(1)}, u32[]{:S(2)}) copy-start(f32[3,64,2,128]{3,2,1,0:T(2,128)S(1)} %broadcast.257) | copy-start | bytes 589828
  97.4 7.5 %copy-start.11 = (bf16[8,3,10,1,1,1]{2,1,5,4,3,0:T(4,128)(2,1)S(1)}, bf16[8,3,10,1,1,1]{2,1,5,4,3,0:T(4,128)(2,1)}, u32[]{:S(2)}) copy-start(bf16[8,3,10,1,1,1]{2,1,5,4,3,0:T(4,128)(2,1)} %constant.60) | copy-start | bytes 1444
  100.2 33.9 %collective-permute-start.2 = (f32[3,3,16,128]{3,2,1,0:T(8,128)}, f32[3,3,16,128]{3,2,1,0:T(8,128)}, u32[]{:S(2)}, u32[]{:S(2)}) collective-permute-start(f32[3,3,16,128]{3,2,1,0:T(8,128)} %get-tuple-element.13), channel_id=1, source_target_pairs={{0,16},{16,0},{1,17},{17,1},{2,18},{18,2},{3,19},{19,3},{4,20},{20... | collective-permute-start | bytes 221192 | tf_op jit(solution)/shard_map/ppermute | solution.py:26
  101.6 32.5 %collective-permute-start.3 = (f32[3,3,16,128]{3,2,1,0:T(8,128)}, f32[3,3,16,128]{3,2,1,0:T(8,128)}, u32[]{:S(2)}, u32[]{:S(2)}) collective-permute-start(f32[3,3,16,128]{3,2,1,0:T(8,128)} %get-tuple-element.14), channel_id=1, source_target_pairs={{16,0},{0,16},{17,1},{1,17},{18,2},{2,18},{19,3},{3,19},{20,4},{4,... | collective-permute-start | bytes 221192 | tf_op jit(solution)/shard_map/ppermute | solution.py:29
  102.8 31.3 %collective-permute-start.6 = (f32[3,3,16,128]{3,2,1,0:T(8,128)}, f32[3,3,16,128]{3,2,1,0:T(8,128)}, u32[]{:S(2)}, u32[]{:S(2)}) collective-permute-start(f32[3,3,16,128]{3,2,1,0:T(8,128)} %get-tuple-element.9), channel_id=1, source_target_pairs={{0,16},{16,0},{1,17},{17,1},{2,18},{18,2},{3,19},{19,3},{4,20},{20... | collective-permute-start | bytes 221192 | tf_op jit(solution)/shard_map/ppermute | solution.py:26
  104.3 29.8 %collective-permute-start.7 = (f32[3,3,16,128]{3,2,1,0:T(8,128)}, f32[3,3,16,128]{3,2,1,0:T(8,128)}, u32[]{:S(2)}, u32[]{:S(2)}) collective-permute-start(f32[3,3,16,128]{3,2,1,0:T(8,128)} %get-tuple-element.10), channel_id=1, source_target_pairs={{16,0},{0,16},{17,1},{1,17},{18,2},{2,18},{19,3},{3,19},{20,4},{4,... | collective-permute-start | bytes 221192 | tf_op jit(solution)/shard_map/ppermute | solution.py:29
  122.8 4.6 %copy-start.2 = (bf16[3,3,3,8,32,10]{4,5,1,0,2,3:T(8,128)(2,1)S(1)}, bf16[3,3,3,8,32,10]{4,5,1,0,2,3:T(8,128)(2,1)}, u32[]{:S(2)}) copy-start(bf16[3,3,3,8,32,10]{4,5,1,0,2,3:T(8,128)(2,1)} %convolution_bitcast_fusion.6) | copy-start | bytes 414724
  129.8 4.1 %copy-start.12 = (f32[32]{0:T(128)S(1)}, f32[32]{0:T(128)}, u32[]{:S(2)}) copy-start(f32[32]{0:T(128)} %param.17) | copy-start | bytes 388
  129.8 4.3 %copy-start.4 = (f32[3,64,2,128]{3,2,1,0:T(2,128)S(1)}, f32[3,64,2,128]{3,2,1,0:T(2,128)}, u32[]{:S(2)}) copy-start(f32[3,64,2,128]{3,2,1,0:T(2,128)} %copy-done.3) | copy-start | bytes 589828

commit v2 on v1

--- a/solution.py
+++ b/solution.py
@@ -42,61 +42,107 @@
     return jnp.concatenate([low, wide, up], axis=1)
 
 
-def closure_kernel(sizes, vel, lam, w1, b1, w2, w3, out, vs, ss, acc):
+def zroll(value, shift):
+    return pltpu.roll(value, shift % LANES, value.ndim - 1)
+
+
+def many(count, size, run):
+    if count % size:
+        size = 1
+
+    @pl.loop(0, count // size)
+    def _(block):
+        for piece in range(size):
+            run(block * size + piece)
+
+
+def velocity_kernel(sizes, vel, w1, b1, slope, grads, vs):
     nx, ny, rows, half, spacings = sizes
-    vblock, sblock = 9 * rows, 18 * rows
-    inv2 = [1.0 / (2.0 * h) for h in spacings]
-    inv60 = [1.0 / (60.0 * h) for h in spacings]
-
-    def zroll(value, shift):
-        return pltpu.roll(value, shift % LANES, value.ndim - 1)
-
-    def prepare(k, side):
-        e = k + 1 + side * half
-        lanes = slice(side * LANES, (side + 1) * LANES)
-        v = vel[:, e].reshape(3 * rows, LANES)
-        l = [lam[c, e] for c in range(3)]
-        dx = [(lam[c, e + 1] - lam[c, e - 1]) * inv2[0] for c in range(3)]
-        dy = [(pltpu.roll(l[c], rows - 1, 0) - pltpu.roll(l[c], 1, 0)) * inv2[1] for c in range(3)]
-        dz = [(zroll(l[c], -1) - zroll(l[c], 1)) * inv2[2] for c in range(3)]
-        s = jnp.concatenate(
-            [dx[0], dy[1], dz[2], dy[0] + dx[1], dz[0] + dx[2], dz[1] + dy[2]], axis=0
-        )
-        for t in range(3):
-            vs[pl.ds(pl.multiple_of(k * vblock + t * 3 * rows, 8), 3 * rows), lanes] = zroll(
-                v, 1 - t
-            ).astype(jnp.bfloat16)
-            ss[pl.ds(pl.multiple_of(k * sblock + t * 6 * rows, 8), 6 * rows), lanes] = zroll(
-                s, 1 - t
-            ).astype(jnp.bfloat16)
-
-    @pl.loop(0, half + 2)
-    def _(k):
-        prepare(k, 0)
-        prepare(k, 1)
-
-    acc[...] = jnp.zeros_like(acc)
+    vblock, out_rows = 9 * rows, w1.shape[0]
+
+    def prepare(k):
+        for side in range(2):
+            v = vel[:, k + 1 + side * half].reshape(3 * rows, LANES)
+            for t in range(3):
+                start = pl.multiple_of(k * vblock + t * 3 * rows, 16)
+                vs[pl.ds(start, 3 * rows), side * LANES : (side + 1) * LANES] = zroll(
+                    v, 1 - t
+                ).astype(jnp.bfloat16)
+
+    many(half + 2, 5, prepare)
 
     def step(i):
         pre = jnp.dot(
-            w1[...],
+            w1[:, : 3 * vblock],
             vs[pl.ds(pl.multiple_of(i * vblock, 16), 3 * vblock), :],
             preferred_element_type=jnp.float32,
         )
+        t = jnp.tanh(pre + b1[...])
+        slope[pl.ds(pl.multiple_of(i * out_rows, 16), out_rows), :] = (1.0 - t * t).astype(
+            jnp.bfloat16
+        )
+
+    many(half, 3, step)
+
+    def gradient(x):
+        e = x + 3
+        mid = slice(3, 3 + ny)
+        for c in range(3):
+            v0 = vel[c, e, mid]
+            for b in range(3):
+                total = 0.0
+                for d, weight in taps:
+                    if b == 0:
+                        pair = vel[c, e + d, mid] - vel[c, e - d, mid]
+                    elif b == 1:
+                        pair = vel[c, e, 3 + d : 3 + d + ny] - vel[c, e, 3 - d : 3 - d + ny]
+                    else:
+                        pair = zroll(v0, -d) - zroll(v0, d)
+                    total += (weight / (60.0 * spacings[b])) * pair
+                grads[3 * b + c, x] = total
+
+    many(nx, 2, gradient)
+
+
+def closure_kernel(sizes, vel, lam, slope, grads, w2, w3, out, ss, acc):
+    nx, ny, rows, half, spacings = sizes
+    sblock, hid_rows = 18 * rows, w2.shape[0]
+    inv2 = [1.0 / (2.0 * h) for h in spacings]
+
+    def prepare(k):
+        for side in range(2):
+            e = k + 1 + side * half
+            lanes = slice(side * LANES, (side + 1) * LANES)
+            l = [lam[c, e] for c in range(3)]
+            dx = [(lam[c, e + 1] - lam[c, e - 1]) * inv2[0] for c in range(3)]
+            dy = [
+                (pltpu.roll(l[c], rows - 1, 0) - pltpu.roll(l[c], 1, 0)) * inv2[1]
+                for c in range(3)
+            ]
+            dz = [(zroll(l[c], -1) - zroll(l[c], 1)) * inv2[2] for c in range(3)]
+            s = jnp.concatenate(
+                [dx[0], dy[1], dz[2], dy[0] + dx[1], dz[0] + dx[2], dz[1] + dy[2]], axis=0
+            )
+            for t in range(3):
+                start = pl.multiple_of(k * sblock + t * 6 * rows, 16)
+                ss[pl.ds(start, 6 * rows), lanes] = zroll(s, 1 - t).astype(jnp.bfloat16)
+        acc[k] = jnp.zeros(acc.shape[1:], acc.dtype)
+
+    many(half + 2, 5, prepare)
+
+    def step(i):
         hid = jnp.dot(
-            w2[...],
+            w2[:, : 3 * sblock],
             ss[pl.ds(pl.multiple_of(i * sblock, 16), 3 * sblock), :],
             preferred_element_type=jnp.float32,
         )
-        t = jnp.tanh(pre + b1[...])
-        p = (hid * (1.0 - t * t)).astype(jnp.bfloat16)
+        part = slope[pl.ds(pl.multiple_of(i * hid_rows, 16), hid_rows), :]
+        p = (hid * part.astype(jnp.float32)).astype(jnp.bfloat16)
         c = jnp.dot(w3[...], p, preferred_element_type=jnp.float32)
         for d in range(3):
             acc[i + d] += c[d * 9 * ny : (d + 1) * 9 * ny]
 
-    @pl.loop(0, half)
-    def _(i):
-        step(i)
+    many(half, 3, step)
 
     for d in range(2):
         acc[half + d, :, :LANES] += acc[d, :, LANES:]
@@ -108,85 +154,119 @@
         closure = zroll(low[0], -1) + low[1] + zroll(low[2], 1)
         mid = slice(3, 3 + ny)
         l0 = [lam[c, e, mid] for c in range(3)]
-        v0 = [vel[c, e, mid] for c in range(3)]
-        total = [closure[c * ny : (c + 1) * ny] for c in range(3)]
-        lz = [l0[c] * v0[2] for c in range(3)]
-        for b in range(3):
-            grad_flux = [0.0] * 3
-            grad_vel = [0.0] * 3
+        vz = vel[2, e, mid]
+        for c in range(3):
+            total = closure[c * ny : (c + 1) * ny]
+            lz = l0[c] * vz
             for d, weight in taps:
-                for sign in (1, -1):
-                    q = d * sign
-                    if b == 0:
-                        vq = [vel[c, e + q, mid] for c in range(3)]
-                        fq = [lam[c, e + q, mid] * vq[0] for c in range(3)]
-                    elif b == 1:
-                        ys = slice(3 + q, 3 + q + ny)
-                        vq = [vel[c, e, ys] for c in range(3)]
-                        fq = [lam[c, e, ys] * vq[1] for c in range(3)]
-                    else:
-                        vq = [zroll(v0[c], -q) for c in range(3)]
-                        fq = [zroll(lz[c], -q) for c in range(3)]
-                    w = weight * sign * inv60[b]
-                    for c in range(3):
-                        grad_flux[c] += w * fq[c]
-                        grad_vel[c] += w * vq[c]
-            for c in range(3):
-                total[c] += grad_flux[c]
-            total[b] -= l0[0] * grad_vel[0] + l0[1] * grad_vel[1] + l0[2] * grad_vel[2]
-        for c in range(3):
-            out[c, x] = l0[c] + time_step * total[c]
-
-    @pl.loop(0, half)
-    def _(x):
-        finish(x, x + 2, 0)
-
-    @pl.loop(half, nx)
-    def _(x):
-        finish(x, x + 2 - half, 1)
-
-
-def band(ny, rows, first):
-    table = np.zeros((ny, 3, rows), np.float32)
-    for y in range(ny):
-        for d in range(3):
-            table[y, d, y + d + first] = 1.0
-    return jnp.asarray(table, jnp.bfloat16)
-
-
-def closure_weights(weight_in, bias_in, weight_out, ny, rows):
-    hid = weight_in.shape[0]
-    w1 = jnp.einsum("ocxyz,pyq->opxzcq", weight_in, band(ny + 2, rows, 1))
-    w1 = w1.reshape(hid * (ny + 2), 27 * rows)
-    flipped = jnp.flip(weight_out, (2, 3, 4))
-    w2 = jnp.einsum("ocxyz,pyq->cpxzoq", flipped, band(ny + 2, rows, 1))
-    w2 = w2.reshape(hid * (ny + 2), 54 * rows)
-    back = jnp.flip(band(ny, ny + 2, 0), 1)
-    w3 = jnp.einsum("ocxyz,pyq->xzcpoq", weight_in, back)
-    w3 = w3.reshape(27 * ny, hid * (ny + 2))
-    bias = jnp.broadcast_to(bias_in[:, None], (hid, ny + 2)).reshape(hid * (ny + 2), 1)
-    return w1, bias, w2, w3
-
-
-def closure_step(vel_ext, lam_ext, weights, nx, ny, spacings):
+                fx = lam[c, e + d, mid] * vel[0, e + d, mid] - lam[c, e - d, mid] * vel[0, e - d, mid]
+                up, down = slice(3 + d, 3 + d + ny), slice(3 - d, 3 - d + ny)
+                fy = lam[c, e, up] * vel[1, e, up] - lam[c, e, down] * vel[1, e, down]
+                fz = zroll(lz, -d) - zroll(lz, d)
+                for b, pair in enumerate((fx, fy, fz)):
+                    total += (weight / (60.0 * spacings[b])) * pair
+            for a in range(3):
+                total -= l0[a] * grads[3 * c + a, x]
+            out[c, x] = l0[c] + time_step * total
+
+    many(half, 3, lambda x: finish(x, x + 2, 0))
+    many(nx - half, 2, lambda x: finish(x + half, x + 2, 1))
+
+
+def lane_padded(size):
+    return -(-size // LANES) * LANES
+
+
+def banded_table(channels, ny, rows):
+    table = np.zeros((channels, 3, 3, 3, ny + 2, 3, 3, channels, rows), np.float32)
+    for c in range(channels):
+        for x in range(3):
+            for d in range(3):
+                for z in range(3):
+                    for p in range(ny + 2):
+                        table[c, x, d, z, p, x, z, c, p + d + 1] = 1.0
+    table = table.reshape(27 * channels, ny + 2, 9 * channels * rows)
+    extra = lane_padded(table.shape[2]) - table.shape[2]
+    return np.pad(table, ((0, 0), (0, 0), (0, extra)))
+
+
+def returned_table(channels, ny):
+    table = np.zeros((channels, 3, 3, 3, ny + 2, 3, 3, channels, ny), np.float32)
+    for c in range(channels):
+        for x in range(3):
+            for d in range(3):
+                for z in range(3):
+                    for y in range(ny):
+                        table[c, x, d, z, y + 2 - d, x, z, c, y] = 1.0
+    table = table.reshape(27 * channels, ny + 2, 9 * channels * ny)
+    extra = lane_padded(table.shape[2]) - table.shape[2]
+    return np.pad(table, ((0, 0), (0, 0), (0, extra)))
+
+
+def spread(weight, table):
+    flat = table.reshape(table.shape[0], -1)
+    wide = jnp.dot(
+        weight, jnp.asarray(flat, jnp.bfloat16), preferred_element_type=jnp.float32
+    ).astype(jnp.bfloat16)
+    columns = table.shape[2]
+    return jnp.concatenate(
+        [wide[:, p * columns : (p + 1) * columns] for p in range(table.shape[1])], axis=0
+    )
+
+
+def input_weights(weight_in, bias_in, ny, rows):
+    hid, comp = weight_in.shape[:2]
+    w1 = spread(weight_in.reshape(hid, -1), banded_table(comp, ny, rows))
+    return w1, jnp.tile(bias_in, ny + 2)[:, None]
+
+
+def output_weights(weight_in, weight_out, ny, rows):
+    hid, comp = weight_in.shape[:2]
+    flipped = jnp.flip(weight_out, (2, 3, 4)).transpose(1, 0, 2, 3, 4).reshape(hid, -1)
+    w2 = spread(flipped, banded_table(weight_out.shape[0], ny, rows))
+    w3 = spread(weight_in.reshape(hid, -1), returned_table(comp, ny)).T[: 9 * comp * ny]
+    return w2, w3
+
+
+def velocity_step(vel_ext, w1, bias, nx, ny, spacings):
     rows = vel_ext.shape[2]
     half = (nx + 2) // 2
-    w1, bias, w2, w3 = weights
-    kernel = functools.partial(closure_kernel, (nx, ny, rows, half, spacings))
     vm = pl.BlockSpec(memory_space=pltpu.VMEM)
     return pl.pallas_call(
-        kernel,
+        functools.partial(velocity_kernel, (nx, ny, rows, half, spacings)),
+        out_shape=(
+            jax.ShapeDtypeStruct((half * w1.shape[0], 2 * LANES), jnp.bfloat16),
+            jax.ShapeDtypeStruct((9, nx, ny, LANES), jnp.float32),
+        ),
+        in_specs=[vm] * 3,
+        out_specs=(vm, vm),
+        scratch_shapes=[pltpu.VMEM(((half + 2) * 9 * rows, 2 * LANES), jnp.bfloat16)],
+        compiler_params=pltpu.CompilerParams(vmem_limit_bytes=40 * 2**20),
+        cost_estimate=pl.CostEstimate(
+            flops=2 * half * w1.shape[0] * w1.shape[1] * 2 * LANES,
+            bytes_accessed=12 * 2**20,
+            transcendentals=half * w1.shape[0] * 2 * LANES,
+        ),
+        name="velocity",
+    )(vel_ext, w1, bias)
+
+
+def closure_step(vel_ext, lam_ext, slope, grads, w2, w3, nx, ny, spacings):
+    rows = vel_ext.shape[2]
+    half = (nx + 2) // 2
+    vm = pl.BlockSpec(memory_space=pltpu.VMEM)
+    return pl.pallas_call(
+        functools.partial(closure_kernel, (nx, ny, rows, half, spacings)),
         out_shape=jax.ShapeDtypeStruct((3, nx, ny, LANES), jnp.float32),
         in_specs=[vm] * 6,
         out_specs=vm,
         scratch_shapes=[
-            pltpu.VMEM(((half + 2) * 9 * rows, 2 * LANES), jnp.bfloat16),
             pltpu.VMEM(((half + 2) * 18 * rows, 2 * LANES), jnp.bfloat16),
             pltpu.VMEM((half + 2, 9 * ny, 2 * LANES), jnp.float32),
         ],
         compiler_params=pltpu.CompilerParams(vmem_limit_bytes=50 * 2**20),
         name="closure",
-    )(vel_ext, lam_ext, w1, bias, w2, w3)
+    )(vel_ext, lam_ext, slope, grads, w2, w3)
 
 
 def waves(length, modes):
@@ -226,7 +306,7 @@
     return scale
 
 
-def projected_once(cotangent, sizes, npx, npy):
+def projected_once(cotangent, sizes, npx, npy, others, beside_first, beside_second):
     NX, NY, NZ = sizes
     _, nx, ny, _ = cotangent.shape
     total = npx * npy
@@ -237,7 +317,9 @@
     forward_z = np.stack([cz, -sz], axis=1).reshape(NZ, 2, total, nj)
     sent = einsum("cxyz,zrdj->drcyjx", cotangent, f32(forward_z))
     sent = sent.reshape(total, 2 * 3 * ny, nj * nx)
+    sent, others = lax.optimization_barrier((sent, others))
     got = lax.all_to_all(sent, ("px", "py"), 0, 0, tiled=True)
+    got, first = lax.optimization_barrier((got, beside_first(*others)))
     got = got.reshape(npx, npy, 2, 3, ny, nj, nx)
     forward_y = np.stack([np.stack([cy, -sy], 0), np.stack([sy, cy], 0)], 0)
     forward_y = forward_y.reshape(2, 2, npy, ny, NY)
@@ -261,11 +343,13 @@
         jnp.stack([re, im]).reshape(2, 3, NY, nj, npx, nx),
         f32(inverse_y),
     ).reshape(total, 2 * 3 * ny, nj * nx)
+    sent, first = lax.optimization_barrier((sent, first))
     got = lax.all_to_all(sent, ("px", "py"), 0, 0, tiled=True)
+    got, second = lax.optimization_barrier((got, beside_second(first)))
     got = got.reshape(total, 2, 3, ny, nj, nx)
     scale = mode_weights(NX, NY, NZ)
     inverse_z = np.stack([(cz * scale).T, (-sz * scale).T], 0).reshape(2, total, nj, NZ)
-    return einsum("drcyjx,rdjz->cxyz", got, f32(inverse_z))
+    return einsum("drcyjx,rdjz->cxyz", got, f32(inverse_z)), second
 
 
 def projected_twice(cotangent, sizes, npx, npy):
@@ -318,14 +402,26 @@
     _, nx, ny, NZ = velocity.shape
     sizes = (nx * npx, ny * npy, NZ)
     spacings = tuple(2.0 * math.pi / size for size in sizes)
-    vel_ext = bordered(velocity)
-    weights = closure_weights(weight_in, bias_in, weight_out, ny, rows_of(ny))
+    rows = rows_of(ny)
+
+    def beside_first(velocity, weight_in, bias_in, weight_out):
+        w1, bias = input_weights(weight_in, bias_in, ny, rows)
+        w2, w3 = output_weights(weight_in, weight_out, ny, rows)
+        return bordered(velocity), w1, bias, w2, w3
+
+    def beside_second(first):
+        vel_ext, w1, bias, w2, w3 = first
+        slope, grads = velocity_step(vel_ext, w1, bias, nx, ny, spacings)
+        return vel_ext, slope, grads, w2, w3
+
+    others = (velocity, weight_in, bias_in, weight_out)
     if (NZ // 2) % (npx * npy) == 0:
-        lam = projected_once(cotangent, sizes, npx, npy)
+        lam, second = projected_once(cotangent, sizes, npx, npy, others, beside_first, beside_second)
     else:
         lam = projected_twice(cotangent, sizes, npx, npy)
-    lam_ext = bordered(lam)
-    return closure_step(vel_ext, lam_ext, weights, nx, ny, spacings)
+        second = beside_second(beside_first(*others))
+    vel_ext, slope, grads, w2, w3 = second
+    return closure_step(vel_ext, bordered(lam), slope, grads, w2, w3, nx, ny, spacings)
 
 
 def solution(mesh):

time: 181 us -> 156 us (0.86)
  local copies, waits for them, and re-layouts: 50.6 us -> 34.6 us
  waiting for transfers between devices: 42.3 us -> 27.2 us
  Pallas kernels: 40.3 us -> 43.5 us
  starting transfers between devices: 23 us -> 25.1 us
    all_to_all x2, waiting for transfers between devices: 40.8 us -> 6.94 us  [projected_once(): got = lax.all_to_all(sent, ('px', 'py'), 0, 0, tiled=True)]
    ppermute x4, waiting for transfers between devices: 1.52 us -> 17.8 us  [halo(): lax.ppermute(lax.slice_in_dim(block, block.shape[dim] - width, None, axis...]
    reshape x4 -> x2, local copies, waits for them, and re-layouts: 14.8 us -> 0.06 us  [the longest x1 0.04 us: output_weights(): jnp.flip(weight_out, (2, 3, 4)).transpose(1, 0, 2, 3, 4).reshape(hid, -1)]
    transpose x3 -> x0, local copies, waits for them, and re-layouts: 12.9 us -> none  [the longest x1 6.77 us: closure_weights(): w2 = jnp.einsum('ocxyz,pyq->cpxzoq', flipped, band(ny + 2, rows, 1))]
    unnamed x26 -> x58, local copies, waits for them, and re-layouts: 2.05 us -> 8.37 us
    pallas_call x1 -> x2, Pallas kernels: 40.3 us -> 43.5 us  [the longest x1 34.1 us: closure_step(): pl.pallas_call(functools.partial(closure_kernel, (nx, ny, rows, half, spa...]
    ppermute x4, waiting for transfers between devices: 0.01 us -> 2.51 us  [halo(): lax.ppermute(lax.slice_in_dim(block, 0, width, axis=dim), axis, backward)]
    reshape x1, local copies, waits for them, and re-layouts: 0.88 us -> 3.24 us  [projected_once(): got = got.reshape(npx, npy, 2, 3, ny, nj, nx)]
  transfers between devices with their start and end apart: 10 -> 10, of which waited for: 3 -> 7; matrix products, arithmetic and copies ran while one was open for 26% -> 8% of each run, Pallas kernels for 0% -> 6%
where the time goes in v2:
time: 156 us; the launch traced here: 154 us
  Pallas kernels  43.5 us (28%)
  local copies, waits for them, and re-layouts  34.6 us (22%)
  waiting for transfers between devices  27.2 us (17%)
  starting transfers between devices  25.1 us (16%)
  matrix products  15.8 us (10%)
  other arithmetic  7.16 us (5%)
    pallas_call x1, Pallas kernels, closure_step(): pl.pallas_call(functools.partial(closure_kernel, (nx, ny, rows, half, spa...  34.1 us
    ppermute x4, waiting for transfers between devices, halo(): lax.ppermute(lax.slice_in_dim(block, block.shape[dim] - width, None, axis...  17.8 us
    all_to_all x2, starting transfers between devices, projected_once(): got = lax.all_to_all(sent, ('px', 'py'), 0, 0, tiled=True)  12 us
    dot_general x6, matrix products, einsum(): return jnp.einsum(*args, precision=high)  11.3 us
    ppermute x4, starting transfers between devices, halo(): lax.ppermute(lax.slice_in_dim(block, 0, width, axis=dim), axis, backward)  10.2 us
    pallas_call x1, Pallas kernels, velocity_step(): pl.pallas_call(functools.partial(velocity_kernel, (nx, ny, rows, half, sp...  9.42 us
    unnamed x58, local copies, waits for them, and re-layouts  8.37 us
    reshape x2, local copies, waits for them, and re-layouts, projected_once(): got = got.reshape(total, 2, 3, ny, nj, nx)  8.36 us
  transfers between devices with their start and end apart: 10, of which 7 were waited for; matrix products, arithmetic and copies ran while one was open for 8% of the time, Pallas kernels for 6%

profile of v2, /device:TPU:0, one launch (start us, length us, event | category | flops | bytes accessed | tf_op | source)
XLA Modules:
  0.0 153.9 jit_solution(4916781802980978500)
XLA Ops:
  0.0 1.1 copy-done
  1.1 2.1 %convolution_bitcast_fusion.3 = f32[32,2,3,8,2,64]{5,0,3,2,4,1:T(8,128)S(1)} fusion(f32[128,2,32,2,1,1]{0,2,5,4,3,1:T(8,128)} %constant.56, f32[3,64,8,128,1,1]{3,2,1,0,5,4:T(8,128)S(1)} %bitcast.137), kind=kOutput, calls=%fused_computation.16 | convolution fusion | flops 150994944 | bytes 1638400 | tf_op jit(solution)/shard_map/cxyz,zrdj->drcyjx/dot_general | solution.py:300
  3.3 2.4 %copy.26 = f32[32,2,3,8,2,64]{5,4,3,2,1,0:T(2,128)} copy(f32[32,2,3,8,2,64]{5,0,3,2,4,1:T(8,128)S(1)} %convolution_bitcast_fusion.3) | data formatting | bytes 1572864 | tf_op jit(solution)/shard_map/cxyz,zrdj->drcyjx/transpose | solution.py:300
  5.7 3.1 %reshape.218 = f32[32,48,128]{2,1,0:T(8,128)} reshape(f32[32,2,3,8,2,64]{5,4,3,2,1,0:T(2,128)} %copy.26) | data formatting | bytes 1572864 | tf_op jit(solution)/shard_map/reshape | solution.py:319
  8.8 7.4 %all-to-all-start = ((f32[32,48,128]{2,1,0:T(8,128)}), f32[32,48,128]{2,1,0:T(8,128)}, u32[]{:S(2)}, u32[]{:S(2)}) async-start(f32[32,48,128]{2,1,0:T(8,128)} %reshape.218), calls=%async_computation | async-start | bytes 1572864 | tf_op jit(solution)/shard_map/all_to_all | solution.py:321
  16.2 1.0 fusion.27
  17.2 0.2 collective-permute-start
  17.4 4.3 %collective-permute-start.1 = (f32[3,64,3,128]{3,2,1,0:T(4,128)}, f32[3,64,3,128]{3,2,1,0:T(4,128)}, u32[]{:S(2)}, u32[]{:S(2)}) collective-permute-start(f32[3,64,3,128]{3,2,1,0:T(4,128)} %get-tuple-element.68), channel_id=1, source_target_pairs={{1,0},{2,1},{3,2},{4,3},{5,4},{6,5},{7,6},{8,7},{9,8},{10,9},{11,1... | collective-permute-start | bytes 884744 | tf_op jit(solution)/shard_map/ppermute | solution.py:29
  21.7 0.7 broadcast_and_fusion
  22.4 0.7 broadcast_add_fusion
  23.1 0.1 broadcast_in_dim_tile.3
  23.2 0.1 rev.4
  23.3 1.5 convolution_convert_fusion.1
  25.0 0.7 copy-done.3
  25.7 2.7 %convolution_convert_fusion = bf16[32,8960]{1,0:T(8,128)(2,1)S(1)} fusion(bf16[32,162]{0,1:T(8,128)(2,1)S(1)} %reshape.220, bf16[162,8960]{1,0:T(8,128)(2,1)} %constant.48.clone), kind=kOutput, calls=%fused_computation | convolution fusion | flops 93184000 | bytes 3486848 | tf_op jit(solution)/shard_map/dot_general | solution.py:208
  28.5 0.4 convolution_convert_fusion.2
  28.9 0.8 fusion.28
  29.7 1.3 concatenate.26
  31.0 7.6 %collective-permute-done = f32[3,64,3,128]{3,2,1,0:T(4,128)S(1)} collective-permute-done((f32[3,64,3,128]{3,2,1,0:T(4,128)}, f32[3,64,3,128]{3,2,1,0:T(4,128)S(1)}, u32[]{:S(2)}, u32[]{:S(2)}) %collective-permute-start) | collective-permute-done | bytes 294944 | tf_op jit(solution)/shard_map/ppermute | solution.py:26
  38.6 0.1 broadcast.259
  38.7 0.0 copy-start.6
  38.7 1.6 %pad_maximum_fusion.3 = f32[3,64,16,128]{3,2,1,0:T(8,128)S(1)} fusion(f32[3,64,2,128]{3,2,1,0:T(2,128)S(1)} %broadcast.259, f32[3,64,3,128]{3,2,1,0:T(4,128)} %collective-permute-done.1, f32[3,64,8,128]{3,2,1,0:T(8,128)S(1)} %copy-done.5, f32[3,64,3,128]{3,2,1,0:T(4,128)S(1)} %collective-permute-done), kind=kLoop, calls=%fused_computation.6 | loop fusion | flops 1179648 | bytes 3145728 | tf_op jit(solution)/shard_map/concatenate | solution.py:40
  40.3 1.6 %collective-permute-start.2 = (f32[3,3,16,128]{3,2,1,0:T(8,128)S(1)}, f32[3,3,16,128]{3,2,1,0:T(8,128)S(1)}, u32[]{:S(2)}, u32[]{:S(2)}) collective-permute-start(f32[3,3,16,128]{3,2,1,0:T(8,128)S(1)} %get-tuple-element.63), channel_id=1, source_target_pairs={{0,16},{16,0},{1,17},{17,1},{2,18},{18,2},{3,19},{19,3},{4,20},{20... | collective-permute-start | bytes 221192 | tf_op jit(solution)/shard_map/ppermute | solution.py:26
  41.8 0.5 collective-permute-start.3
  42.4 2.3 %collective-permute-done.2 = f32[3,3,16,128]{3,2,1,0:T(8,128)S(1)} collective-permute-done((f32[3,3,16,128]{3,2,1,0:T(8,128)S(1)}, f32[3,3,16,128]{3,2,1,0:T(8,128)S(1)}, u32[]{:S(2)}, u32[]{:S(2)}) %collective-permute-start.2) | collective-permute-done | bytes 73760 | tf_op jit(solution)/shard_map/ppermute | solution.py:26
  44.7 1.5 collective-permute-done.3
  46.2 1.5 fusion.1.vel
  47.7 0.0 copy-start.13
  47.8 3.2 %reshape.221 = f32[2,16,2,3,8,2,64]{6,5,4,3,2,1,0:T(2,128)} reshape(f32[32,48,128]{2,1,0:T(8,128)} %all-to-all-done) | data formatting | bytes 1572864 | tf_op jit(solution)/shard_map/reshape | solution.py:323
  51.0 3.4 %fusion.6 = f32[2,3,128,2,2,64]{2,5,0,3,1,4:T(8,128)S(1)} fusion(f32[2,2,16,8,128,1,1,1]{4,2,3,0,1,7,6,5:T(8,128)S(1)} %copy-done.13, f32[2,16,2,3,8,2,64,1]{6,5,4,3,2,1,0,7:T(2,128)} %bitcast.138), kind=kOutput, calls=%fused_computation.18 | convolution fusion | flops 301989888 | bytes 1835008 | tf_op jit(solution)/shard_map/hprcyjx,rRpyl->Rcljhx/dot_general | solution.py:300
  54.4 0.1 copy.29
  54.5 0.8 convolution_bitcast_fusion.2
  55.5 0.7 copy-done.14
  56.2 0.2 and_select_fusion.5
  56.4 0.2 and_select_fusion.1
  56.6 0.1 maximum_bitcast_fusion.4
  56.7 0.8 convolution_bitcast_fusion.1
  57.5 0.0 copy-start.12
  57.5 0.1 slice_subtract_fusion
  57.6 0.8 copy-done.12
  58.4 0.8 convolution_bitcast_fusion
  59.2 2.4 %copy.38 = f32[2,16,2,3,8,2,64]{6,5,4,3,2,1,0:T(2,128)} copy(f32[2,16,2,3,8,2,64]{6,1,4,2,0,5,3:T(8,128)S(1)} %convolution_bitcast_fusion) | data formatting | bytes 1572864 | tf_op jit(solution)/shard_map/Rcljhx,Rrlpy->hprcyjx/transpose | solution.py:300
  61.6 3.0 %reshape.223 = f32[32,48,128]{2,1,0:T(8,128)} reshape(f32[2,16,2,3,8,2,64]{6,5,4,3,2,1,0:T(2,128)} %copy.38) | data formatting | bytes 1572864 | tf_op jit(solution)/shard_map/reshape | solution.py:345
  64.7 4.6 %all-to-all-start.1 = ((f32[32,48,128]{2,1,0:T(8,128)}), f32[32,48,128]{2,1,0:T(8,128)}, u32[]{:S(2)}, u32[]{:S(2)}) async-start(f32[32,48,128]{2,1,0:T(8,128)} %reshape.223), calls=%async_computation.1 | async-start | bytes 1572864 | tf_op jit(solution)/shard_map/all_to_all | solution.py:347
  69.3 0.1 copy.39.b1
  69.4 1.0 copy-done.4
  70.4 9.4 %velocity.1 = (bf16[10560,256]{1,0:T(8,128)(2,1)S(1)}, f32[9,64,8,128]{3,2,1,0:T(8,128)S(1)}) custom-call(f32[3,70,16,128]{3,2,1,0:T(8,128)S(1)} %fusion.1.vel, bf16[320,512]{1,0:T(8,128)(2,1)S(1)} %copy-done.4, f32[320,1]{1,0:T(8,128)S(1)} %copy.39.b1), custom_call_target="tpu_custom_call" | custom-call | flops 2768240640 | bytes 12582912 | tf_op jit(solution)/shard_map/velocity/pallas_call | solution.py:235
  79.8 2.4 %copy-done.1 = bf16[10560,256]{1,0:T(8,128)(2,1)} copy-done((bf16[10560,256]{1,0:T(8,128)(2,1)}, bf16[10560,256]{1,0:T(8,128)(2,1)S(1)}, u32[]{:S(2)}) %copy-start.1) | copy-done | bytes 5406744
  82.2 1.4 copy-done.2
  83.6 6.9 %all-to-all-done.1 = f32[32,48,128]{2,1,0:T(8,128)} async-done(((f32[32,48,128]{2,1,0:T(8,128)}), f32[32,48,128]{2,1,0:T(8,128)}, u32[]{:S(2)}, u32[]{:S(2)}) %all-to-all-start.1) | async-done | bytes 786464 | tf_op jit(solution)/shard_map/all_to_all | solution.py:347
  90.6 3.2 %reshape.224 = f32[32,2,3,8,2,64]{5,4,3,2,1,0:T(2,128)} reshape(f32[32,48,128]{2,1,0:T(8,128)} %all-to-all-done.1) | data formatting | bytes 1572864 | tf_op jit(solution)/shard_map/reshape | solution.py:349
  93.8 5.1 %copy.55 = f32[32,2,3,8,2,64]{0,3,1,4,5,2:T(8,128)} copy(f32[32,2,3,8,2,64]{5,4,3,2,1,0:T(2,128)} %reshape.224) | data formatting | bytes 1572864 | tf_op jit(solution)/shard_map/reshape | solution.py:349
  98.9 3.3 %convolution_bitcast_fusion.4 = f32[3,64,8,128]{3,2,1,0:T(8,128)S(1)} fusion(f32[32,2,3,8,2,64]{0,3,1,4,5,2:T(8,128)} %copy.55, f32[2,32,2,128,1,1]{3,1,0,2,5,4:T(8,128)S(1)} %copy-done.16), kind=kOutput, calls=%fused_computation.17 | convolution fusion | flops 150994944 | bytes 1638400 | tf_op jit(solution)/shard_map/drcyjx,rdjz->cxyz/dot_general | solution.py:300
  102.2 0.1 fusion.26
  102.4 0.1 collective-permute-start.4
  102.4 4.4 %collective-permute-start.5 = (f32[3,64,3,128]{3,2,1,0:T(4,128)S(1)}, f32[3,64,3,128]{3,2,1,0:T(4,128)S(1)}, u32[]{:S(2)}, u32[]{:S(2)}) collective-permute-start(f32[3,64,3,128]{3,2,1,0:T(4,128)S(1)} %get-tuple-element.66), channel_id=1, source_target_pairs={{1,0},{2,1},{3,2},{4,3},{5,4},{6,5},{7,6},{8,7},{9,8},{10,9},{11,1... | collective-permute-start | bytes 884744 | tf_op jit(solution)/shard_map/ppermute | solution.py:29
  106.9 5.6 %collective-permute-done.4 = f32[3,64,3,128]{3,2,1,0:T(4,128)S(1)} collective-permute-done((f32[3,64,3,128]{3,2,1,0:T(4,128)S(1)}, f32[3,64,3,128]{3,2,1,0:T(4,128)S(1)}, u32[]{:S(2)}, u32[]{:S(2)}) %collective-permute-start.4) | collective-permute-done | bytes 294944 | tf_op jit(solution)/shard_map/ppermute | solution.py:26
  112.4 0.4 pad_maximum_fusion.2
  112.8 1.1 collective-permute-start.6
  113.9 1.0 collective-permute-start.7
  114.9 2.3 %collective-permute-done.6 = f32[3,3,16,128]{3,2,1,0:T(8,128)S(1)} collective-permute-done((f32[3,3,16,128]{3,2,1,0:T(8,128)S(1)}, f32[3,3,16,128]{3,2,1,0:T(8,128)S(1)}, u32[]{:S(2)}, u32[]{:S(2)}) %collective-permute-start.6) | collective-permute-done | bytes 73760 | tf_op jit(solution)/shard_map/ppermute | solution.py:26
  117.2 1.0 collective-permute-done.7
  118.3 1.6 %fusion.3.lam = f32[3,70,16,128]{3,2,1,0:T(8,128)} fusion(f32[3,64,2,128]{3,2,1,0:T(2,128)S(1)} %copy-done.8, f32[3,3,16,128]{3,2,1,0:T(8,128)S(1)} %collective-permute-done.7, f32[3,64,3,128]{3,2,1,0:T(4,128)S(1)} %collective-permute-done.5, f32[3,64,8,128]{3,2,1,0:T(8,128)S(1)} %convolution_bitcast_fusion.4, ...), kind=kLoop, calls=%fused_computation.10 | loop fusion | flops 2150400 | bytes 3440640 | tf_op jit(solution)/shard_map/concatenate | solution.py:42
  119.9 34.1 %closure.1 = f32[3,64,8,128]{3,2,1,0:T(8,128)} custom-call(f32[3,70,16,128]{3,2,1,0:T(8,128)S(1)} %fusion.1.vel, f32[3,70,16,128]{3,2,1,0:T(8,128)} %fusion.3.lam, bf16[10560,256]{1,0:T(8,128)(2,1)} %copy-done.1, f32[9,64,8,128]{3,2,1,0:T(8,128)} %copy-done.2, bf16[320,896]{1,0:T(8,128)(2,1)S(1)} %slice_dynamic-update-slice_fusion.w2, ...), custom_call_target="tpu_custom_call" | custom-call | tf_op jit(solution)/shard_map/closure/pallas_call | solution.py:258
  (68 shorter events, 0.5 us)
Async XLA Ops:
  0.0 1.1 copy-start
  5.7 10.5 %copy-start.5 = (f32[3,64,8,128]{3,2,1,0:T(8,128)S(1)}, f32[3,64,8,128]{3,2,1,0:T(8,128)}, u32[]{:S(2)}) copy-start(f32[3,64,8,128]{3,2,1,0:T(8,128)} %param.14) | copy-start | bytes 2359300
  8.7 14.3 %copy-start.19 = (f32[32]{0:T(128)S(1)}, f32[32]{0:T(128)}, u32[]{:S(2)}) copy-start(f32[32]{0:T(128)} %param.17) | copy-start | bytes 388
  8.7 14.4 %copy-start.18 = (bf16[32,3,3,3,3]{0,4,3,2,1:T(4,128)(2,1)S(1)}, bf16[32,3,3,3,3]{0,4,3,2,1:T(4,128)(2,1)}, u32[]{:S(2)}) copy-start(bf16[32,3,3,3,3]{0,4,3,2,1:T(4,128)(2,1)} %param.16) | copy-start | bytes 15556
  8.8 14.4 %copy-start.17 = (bf16[6,32,3,3,3]{1,4,3,2,0:T(4,128)(2,1)S(1)}, bf16[6,32,3,3,3]{1,4,3,2,0:T(4,128)(2,1)}, u32[]{:S(2)}) copy-start(bf16[6,32,3,3,3]{1,4,3,2,0:T(4,128)(2,1)} %param.18) | copy-start | bytes 31108
  8.8 39.0 %all-to-all-start = ((f32[32,48,128]{2,1,0:T(8,128)}), f32[32,48,128]{2,1,0:T(8,128)}, u32[]{:S(2)}, u32[]{:S(2)}) async-start(f32[32,48,128]{2,1,0:T(8,128)} %reshape.218), calls=%async_computation | async-start | bytes 1572864 | tf_op jit(solution)/shard_map/all_to_all | solution.py:321
  17.2 21.4 %collective-permute-start = (f32[3,64,3,128]{3,2,1,0:T(4,128)}, f32[3,64,3,128]{3,2,1,0:T(4,128)S(1)}, u32[]{:S(2)}, u32[]{:S(2)}) collective-permute-start(f32[3,64,3,128]{3,2,1,0:T(4,128)} %get-tuple-element.67), channel_id=1, source_target_pairs={{0,1},{1,2},{2,3},{3,4},{4,5},{5,6},{6,7},{7,8},{8,9},{9,10},{10,1... | collective-permute-start | bytes 884744 | tf_op jit(solution)/shard_map/ppermute | solution.py:26
  17.4 21.2 %collective-permute-start.1 = (f32[3,64,3,128]{3,2,1,0:T(4,128)}, f32[3,64,3,128]{3,2,1,0:T(4,128)}, u32[]{:S(2)}, u32[]{:S(2)}) collective-permute-start(f32[3,64,3,128]{3,2,1,0:T(4,128)} %get-tuple-element.68), channel_id=1, source_target_pairs={{1,0},{2,1},{3,2},{4,3},{5,4},{6,5},{7,6},{8,7},{9,8},{10,9},{11,1... | collective-permute-start | bytes 884744 | tf_op jit(solution)/shard_map/ppermute | solution.py:29
  25.0 0.7 copy-start.3
  25.7 2.8 %copy-start.11 = (bf16[81,2560]{1,0:T(8,128)(2,1)S(1)}, bf16[81,2560]{1,0:T(8,128)(2,1)}, u32[]{:S(2)}) copy-start(bf16[81,2560]{1,0:T(8,128)(2,1)} %constant.49.clone) | copy-start | bytes 1244164
  38.6 1.6 %copy-start.9 = (f32[3,64,3,128]{3,2,1,0:T(4,128)}, f32[3,64,3,128]{3,2,1,0:T(4,128)S(1)}, u32[]{:S(2)}) copy-start(f32[3,64,3,128]{3,2,1,0:T(4,128)S(1)} %collective-permute-done) | copy-start | bytes 884740
  38.7 7.5 %copy-start.7 = (f32[3,64,2,128]{3,2,1,0:T(2,128)}, f32[3,64,2,128]{3,2,1,0:T(2,128)S(1)}, u32[]{:S(2)}) copy-start(f32[3,64,2,128]{3,2,1,0:T(2,128)S(1)} %broadcast.259) | copy-start | bytes 589828
  38.7 7.5 %copy-start.6 = (f32[3,64,8,128]{3,2,1,0:T(8,128)S(1)}, f32[3,64,8,128]{3,2,1,0:T(8,128)}, u32[]{:S(2)}) copy-start(f32[3,64,8,128]{3,2,1,0:T(8,128)} %param.14) | copy-start | bytes 2359300
  40.3 4.4 %collective-permute-start.2 = (f32[3,3,16,128]{3,2,1,0:T(8,128)S(1)}, f32[3,3,16,128]{3,2,1,0:T(8,128)S(1)}, u32[]{:S(2)}, u32[]{:S(2)}) collective-permute-start(f32[3,3,16,128]{3,2,1,0:T(8,128)S(1)} %get-tuple-element.63), channel_id=1, source_target_pairs={{0,16},{16,0},{1,17},{17,1},{2,18},{18,2},{3,19},{19,3},{4,20},{20... | collective-permute-start | bytes 221192 | tf_op jit(solution)/shard_map/ppermute | solution.py:26
  41.8 4.4 %collective-permute-start.3 = (f32[3,3,16,128]{3,2,1,0:T(8,128)S(1)}, f32[3,3,16,128]{3,2,1,0:T(8,128)S(1)}, u32[]{:S(2)}, u32[]{:S(2)}) collective-permute-start(f32[3,3,16,128]{3,2,1,0:T(8,128)S(1)} %get-tuple-element.64), channel_id=1, source_target_pairs={{16,0},{0,16},{17,1},{1,17},{18,2},{2,18},{19,3},{3,19},{20,4},{4,... | collective-permute-start | bytes 221192 | tf_op jit(solution)/shard_map/ppermute | solution.py:29
  47.7 3.3 %copy-start.13 = (f32[2,2,16,8,128,1,1,1]{4,2,3,0,1,7,6,5:T(8,128)S(1)}, f32[2,2,16,8,128,1,1,1]{4,2,3,0,1,7,6,5:T(8,128)}, u32[]{:S(2)}) copy-start(f32[2,2,16,8,128,1,1,1]{4,2,3,0,1,7,6,5:T(8,128)} %constant.57) | copy-start | bytes 786436
  51.0 3.5 %copy-start.10 = (f32[128,2,128,1,1,1]{2,0,1,5,4,3:T(8,128)S(1)}, f32[128,2,128,1,1,1]{2,0,1,5,4,3:T(8,128)}, u32[]{:S(2)}) copy-start(f32[128,2,128,1,1,1]{2,0,1,5,4,3:T(8,128)} %constant.58) | copy-start | bytes 393220
  55.3 0.8 copy-start.14
  55.3 0.8 copy-start.15
  57.5 1.0 copy-start.12
  64.7 25.9 %all-to-all-start.1 = ((f32[32,48,128]{2,1,0:T(8,128)}), f32[32,48,128]{2,1,0:T(8,128)}, u32[]{:S(2)}, u32[]{:S(2)}) async-start(f32[32,48,128]{2,1,0:T(8,128)} %reshape.223), calls=%async_computation.1 | async-start | bytes 1572864 | tf_op jit(solution)/shard_map/all_to_all | solution.py:347
  69.4 1.0 copy-start.4
  79.8 2.4 %copy-start.1 = (bf16[10560,256]{1,0:T(8,128)(2,1)}, bf16[10560,256]{1,0:T(8,128)(2,1)S(1)}, u32[]{:S(2)}) copy-start(bf16[10560,256]{1,0:T(8,128)(2,1)S(1)} %get-tuple-element.51.slope) | copy-start | bytes 16220164
  82.2 1.4 copy-start.2
  93.8 5.2 %copy-start.16 = (f32[2,32,2,128,1,1]{3,1,0,2,5,4:T(8,128)S(1)}, f32[2,32,2,128,1,1]{3,1,0,2,5,4:T(8,128)}, u32[]{:S(2)}) copy-start(f32[2,32,2,128,1,1]{3,1,0,2,5,4:T(8,128)} %constant.60) | copy-start | bytes 196612
  102.2 10.2 %copy-start.8 = (f32[3,64,2,128]{3,2,1,0:T(2,128)S(1)}, f32[3,64,2,128]{3,2,1,0:T(2,128)}, u32[]{:S(2)}) copy-start(f32[3,64,2,128]{3,2,1,0:T(2,128)} %copy-done.7) | copy-start | bytes 589828
  102.4 10.1 %collective-permute-start.4 = (f32[3,64,3,128]{3,2,1,0:T(4,128)S(1)}, f32[3,64,3,128]{3,2,1,0:T(4,128)S(1)}, u32[]{:S(2)}, u32[]{:S(2)}) collective-permute-start(f32[3,64,3,128]{3,2,1,0:T(4,128)S(1)} %get-tuple-element.65), channel_id=1, source_target_pairs={{0,1},{1,2},{2,3},{3,4},{4,5},{5,6},{6,7},{7,8},{8,9},{9,10},{10,1... | collective-permute-start | bytes 884744 | tf_op jit(solution)/shard_map/ppermute | solution.py:26
  102.4 10.0 %collective-permute-start.5 = (f32[3,64,3,128]{3,2,1,0:T(4,128)S(1)}, f32[3,64,3,128]{3,2,1,0:T(4,128)S(1)}, u32[]{:S(2)}, u32[]{:S(2)}) collective-permute-start(f32[3,64,3,128]{3,2,1,0:T(4,128)S(1)} %get-tuple-element.66), channel_id=1, source_target_pairs={{1,0},{2,1},{3,2},{4,3},{5,4},{6,5},{7,6},{8,7},{9,8},{10,9},{11,1... | collective-permute-start | bytes 884744 | tf_op jit(solution)/shard_map/ppermute | solution.py:29
  112.8 4.4 %collective-permute-start.6 = (f32[3,3,16,128]{3,2,1,0:T(8,128)S(1)}, f32[3,3,16,128]{3,2,1,0:T(8,128)S(1)}, u32[]{:S(2)}, u32[]{:S(2)}) collective-permute-start(f32[3,3,16,128]{3,2,1,0:T(8,128)S(1)} %get-tuple-element.59), channel_id=1, source_target_pairs={{0,16},{16,0},{1,17},{17,1},{2,18},{18,2},{3,19},{19,3},{4,20},{20... | collective-permute-start | bytes 221192 | tf_op jit(solution)/shard_map/ppermute | solution.py:26
  113.9 4.4 %collective-permute-start.7 = (f32[3,3,16,128]{3,2,1,0:T(8,128)S(1)}, f32[3,3,16,128]{3,2,1,0:T(8,128)S(1)}, u32[]{:S(2)}, u32[]{:S(2)}) collective-permute-start(f32[3,3,16,128]{3,2,1,0:T(8,128)S(1)} %get-tuple-element.60), channel_id=1, source_target_pairs={{16,0},{0,16},{17,1},{1,17},{18,2},{2,18},{19,3},{3,19},{20,4},{4,... | collective-permute-start | bytes 221192 | tf_op jit(solution)/shard_map/ppermute | solution.py:29

commit v3 on v2

--- a/solution.py
+++ b/solution.py
@@ -3,6 +3,7 @@
 
 import jax
 import jax.numpy as jnp
+import ml_dtypes
 import numpy as np
 from jax import lax
 from jax.experimental import pallas as pl
@@ -31,7 +32,10 @@
 
 
 def bordered(block):
-    low, up = halo(block, "py", 2, 3)
+    return bordered_rest(block, *halo(block, "py", 2, 3))
+
+
+def bordered_rest(block, low, up):
     ny = block.shape[2]
     extra = rows_of(ny) - ny - 6
     parts = [low, block, up]
@@ -306,6 +310,104 @@
     return scale
 
 
+def halves(table):
+    table = np.asarray(table, np.float32)
+    first = table.astype(ml_dtypes.bfloat16)
+    second = (table - first.astype(np.float32)).astype(ml_dtypes.bfloat16)
+    return jnp.asarray(np.stack([first, second]))
+
+
+def cut(value):
+    first = value.astype(jnp.bfloat16)
+    return first, (value - first.astype(jnp.float32)).astype(jnp.bfloat16)
+
+
+def dot3(left, right, dims=((1,), (0,))):
+    def one(a, b):
+        return lax.dot_general(a, b, (dims, ((), ())), preferred_element_type=jnp.float32)
+
+    return one(left[0], right[0]) + (one(left[0], right[1]) + one(left[1], right[0]))
+
+
+def forward_kernel(sizes, cot, table, sent):
+    total, nj, nx, ny = sizes
+    left = (table[0], table[1])
+    for c in range(3):
+        planes = []
+        for y in range(ny):
+            modes = dot3(left, cut(cot[c, :, y, :]), ((1,), (1,)))
+            rows = 2 * total
+            planes.append(
+                jnp.concatenate([modes[j * rows : (j + 1) * rows] for j in range(nj)], axis=1)
+            )
+        block = jnp.swapaxes(jnp.stack(planes), 0, 1)
+        sent[:, :, c] = block.reshape(total, 2, ny, nj * nx)
+
+
+def backward_kernel(sizes, got, table, lam):
+    total, nj, nx, ny = sizes
+    right = (table[0], table[1])
+    for c in range(3):
+        block = got[:, :, c].reshape(2 * total, ny, nj * nx)
+        block = jnp.swapaxes(block, 0, 1)
+        for y in range(ny):
+            modes = jnp.concatenate(
+                [block[y][:, j * nx : (j + 1) * nx] for j in range(nj)], axis=0
+            )
+            lam[c, :, y, :] = dot3(cut(modes), right, ((0,), (0,)))
+
+
+def middle_kernel(sizes, got, lanes, fy, fx, bx, by, sent):
+    npx, npy, ny, NY, wide = sizes
+    rows = 2 * npy * ny
+    per = wide // npx
+
+    def table(ref):
+        return ref[0], ref[1]
+
+    modes = []
+    for c in range(3):
+        block = jnp.concatenate(
+            [got[h * npy : (h + 1) * npy, :, c].reshape(rows, per) for h in range(npx)], axis=1
+        )
+        mixed = dot3(table(fy), cut(block))
+        both = dot3(cut(mixed), table(fx))
+        re = both[:NY, :wide] + both[NY:, wide:]
+        im = both[NY:, :wide] - both[:NY, wide:]
+        modes.append((re, im))
+    ky = lax.broadcasted_iota(jnp.int32, (NY, wide), 0)
+    wy = jnp.where(ky > NY // 2, ky - NY, ky).astype(jnp.float32)
+    wx, wz = lanes[0:1], lanes[1:2]
+    keep = jnp.where(ky == NY // 2, 0.0, 1.0) * lanes[2:3]
+    squared = wx * wx + wy * wy + wz * wz
+    inverse = jnp.where(squared > 0, 1.0 / jnp.maximum(squared, 1.0), 0.0)
+    dotted = [
+        (wx * modes[0][r] + wy * modes[1][r] + wz * modes[2][r]) * inverse for r in range(2)
+    ]
+    for c, w in enumerate((wx, wy, wz)):
+        pair = jnp.concatenate([(modes[c][r] - w * dotted[r]) * keep for r in range(2)], axis=0)
+        both = dot3(cut(pair), table(bx))
+        re = both[:NY, :wide] - both[NY:, wide:]
+        im = both[NY:, :wide] + both[:NY, wide:]
+        back = dot3(table(by), cut(jnp.concatenate([re, im], axis=0)))
+        for h in range(npx):
+            sent[h * npy : (h + 1) * npy, :, c] = back[:, h * per : (h + 1) * per].reshape(
+                npy, 2, ny, per
+            )
+
+
+def local_call(kernel, shape, name, *operands):
+    vm = pl.BlockSpec(memory_space=pltpu.VMEM)
+    return pl.pallas_call(
+        kernel,
+        out_shape=jax.ShapeDtypeStruct(shape, jnp.float32),
+        in_specs=[vm] * len(operands),
+        out_specs=vm,
+        compiler_params=pltpu.CompilerParams(vmem_limit_bytes=40 * 2**20),
+        name=name,
+    )(*operands)
+
+
 def projected_once(cotangent, sizes, npx, npy, others, beside_first, beside_second):
     NX, NY, NZ = sizes
     _, nx, ny, _ = cotangent.shape
@@ -314,42 +416,61 @@
     cz, sz = waves(NZ, NZ // 2)
     cy, sy = waves(NY, NY)
     cx, sx = waves(NX, NX)
-    forward_z = np.stack([cz, -sz], axis=1).reshape(NZ, 2, total, nj)
-    sent = einsum("cxyz,zrdj->drcyjx", cotangent, f32(forward_z))
-    sent = sent.reshape(total, 2 * 3 * ny, nj * nx)
+    shape = (total, 2, 3, ny, nj * nx)
+    forward_z = np.stack([cz, -sz], 0).reshape(2, NZ, total, nj)
+    forward_z = forward_z.transpose(3, 2, 0, 1).reshape(NZ, NZ)
+    sent = local_call(
+        functools.partial(forward_kernel, (total, nj, nx, ny)),
+        shape,
+        "forward",
+        cotangent,
+        halves(forward_z),
+    )
     sent, others = lax.optimization_barrier((sent, others))
     got = lax.all_to_all(sent, ("px", "py"), 0, 0, tiled=True)
-    got, first = lax.optimization_barrier((got, beside_first(*others)))
-    got = got.reshape(npx, npy, 2, 3, ny, nj, nx)
+    first, halo_first = beside_first(*others)
+    got, first = lax.optimization_barrier((got, first))
     forward_y = np.stack([np.stack([cy, -sy], 0), np.stack([sy, cy], 0)], 0)
-    forward_y = forward_y.reshape(2, 2, npy, ny, NY)
-    mixed = einsum("hprcyjx,rRpyl->Rcljhx", got, f32(forward_y))
-    mixed = mixed.reshape(2, 3, NY, nj, NX)
-    trans = einsum("Rcljx,xSm->SRcljm", mixed, f32(np.stack([cx, sx], 1)))
-    re = trans[0, 0] + trans[1, 1]
-    im = trans[0, 1] - trans[1, 0]
+    forward_y = forward_y.reshape(2, 2, npy, ny, NY).transpose(1, 4, 2, 0, 3)
+    eye = np.eye(nj)
+    forward_x = np.stack([cx, sx], 0).reshape(2, npx, nx, NX)
+    forward_x = np.einsum("shxm,jk->hjxskm", forward_x, eye)
+    backward_x = np.stack([cx, sx], 0).reshape(2, NX, npx, nx)
+    backward_x = np.einsum("smhx,jk->jmshkx", backward_x, eye)
+    backward_y = np.stack([np.stack([cy, sy], 0), np.stack([-sy, cy], 0)], 0)
+    backward_y = backward_y.reshape(2, 2, NY, npy, ny).transpose(3, 1, 4, 0, 2)
+    wide = nj * NX
     me = lax.axis_index("px") * npy + lax.axis_index("py")
-    index_z = (me * nj + jnp.arange(nj, dtype=jnp.int32))[None, :, None]
-    index_y = jnp.arange(NY, dtype=jnp.int32)[:, None, None]
-    index_x = jnp.arange(NX, dtype=jnp.int32)[None, None, :]
-    re, im = project(re, im, index_x, index_y, index_z, sizes)
-    back = einsum("Rcljm,mSx->SRcljx", jnp.stack([re, im]), f32(np.stack([cx, sx], 1)))
-    re = back[0, 0] - back[1, 1]
-    im = back[1, 0] + back[0, 1]
-    inverse_y = np.stack([np.stack([cy, sy], 0), np.stack([-sy, cy], 0)], 0)
-    inverse_y = inverse_y.reshape(2, 2, NY, npy, ny)
-    sent = einsum(
-        "Rcljhx,Rrlpy->hprcyjx",
-        jnp.stack([re, im]).reshape(2, 3, NY, nj, npx, nx),
-        f32(inverse_y),
-    ).reshape(total, 2 * 3 * ny, nj * nx)
-    sent, first = lax.optimization_barrier((sent, first))
+    lane = jnp.arange(wide, dtype=jnp.int32)
+    index_x, index_z = lane % NX, me * nj + lane // NX
+    wave_x = jnp.where(index_x > NX // 2, index_x - NX, index_x).astype(jnp.float32)
+    keep = ((index_x != NX // 2) & (index_z != NZ // 2)).astype(jnp.float32)
+    lanes = jnp.stack([wave_x, index_z.astype(jnp.float32), keep])
+    sent = local_call(
+        functools.partial(middle_kernel, (npx, npy, ny, NY, wide)),
+        shape,
+        "middle",
+        got,
+        lanes,
+        halves(forward_y.reshape(2 * NY, 2 * NY)),
+        halves(forward_x.reshape(wide, 2 * wide)),
+        halves(backward_x.reshape(wide, 2 * wide)),
+        halves(backward_y.reshape(2 * NY, 2 * NY)),
+    )
+    sent, first, halo_first = lax.optimization_barrier((sent, first, halo_first))
     got = lax.all_to_all(sent, ("px", "py"), 0, 0, tiled=True)
-    got, second = lax.optimization_barrier((got, beside_second(first)))
-    got = got.reshape(total, 2, 3, ny, nj, nx)
+    got, second = lax.optimization_barrier((got, beside_second(first, halo_first)))
     scale = mode_weights(NX, NY, NZ)
-    inverse_z = np.stack([(cz * scale).T, (-sz * scale).T], 0).reshape(2, total, nj, NZ)
-    return einsum("drcyjx,rdjz->cxyz", got, f32(inverse_z)), second
+    backward_z = np.stack([(cz * scale).T, (-sz * scale).T], 0).reshape(2, total, nj, NZ)
+    backward_z = backward_z.transpose(2, 1, 0, 3).reshape(NZ, NZ)
+    lam = local_call(
+        functools.partial(backward_kernel, (total, nj, nx, ny)),
+        cotangent.shape,
+        "backward",
+        got,
+        halves(backward_z),
+    )
+    return lam, second
 
 
 def projected_twice(cotangent, sizes, npx, npy):
@@ -407,19 +528,20 @@
     def beside_first(velocity, weight_in, bias_in, weight_out):
         w1, bias = input_weights(weight_in, bias_in, ny, rows)
         w2, w3 = output_weights(weight_in, weight_out, ny, rows)
-        return bordered(velocity), w1, bias, w2, w3
-
-    def beside_second(first):
-        vel_ext, w1, bias, w2, w3 = first
+        return (w1, bias, w2, w3), (velocity,) + halo(velocity, "py", 2, 3)
+
+    def beside_second(first, halo_first):
+        w1, bias, w2, w3 = first
+        vel_ext = bordered_rest(*halo_first)
         slope, grads = velocity_step(vel_ext, w1, bias, nx, ny, spacings)
         return vel_ext, slope, grads, w2, w3
 
     others = (velocity, weight_in, bias_in, weight_out)
-    if (NZ // 2) % (npx * npy) == 0:
+    if (NZ // 2) % (npx * npy) == 0 and nx * (NZ // 2) % (npx * npy * LANES) == 0 and ny % 8 == 0:
         lam, second = projected_once(cotangent, sizes, npx, npy, others, beside_first, beside_second)
     else:
         lam = projected_twice(cotangent, sizes, npx, npy)
-        second = beside_second(beside_first(*others))
+        second = beside_second(*beside_first(*others))
     vel_ext, slope, grads, w2, w3 = second
     return closure_step(vel_ext, bordered(lam), slope, grads, w2, w3, nx, ny, spacings)
 

time: 156 us -> 128 us (0.82)
  local copies, waits for them, and re-layouts: 34.6 us -> 18.5 us
  matrix products: 15.8 us -> 4.18 us
  Pallas kernels: 43.5 us -> 53 us
  waiting for transfers between devices: 27.2 us -> 20.6 us
  other arithmetic: 7.16 us -> 5.49 us
    reshape x5 -> x0, local copies, waits for them, and re-layouts: 17.7 us -> none  [the longest x2 8.36 us: projected_once(): got = got.reshape(total, 2, 3, ny, nj, nx)]
    dot_general x6 -> x0, matrix products: 11.3 us -> none  [einsum(): return jnp.einsum(*args, precision=high)]
    pallas_call x0 -> x3, Pallas kernels: none -> 9.43 us  [local_call(): pl.pallas_call(kernel, out_shape=jax.ShapeDtypeStruct(shape, jnp.float32)...]
    unnamed x58, local copies, waits for them, and re-layouts: 8.37 us -> 14.1 us
    ppermute x4, waiting for transfers between devices: 17.8 us -> 12.6 us  [halo(): lax.ppermute(lax.slice_in_dim(block, block.shape[dim] - width, None, axis...]
    transpose x3 -> x0, local copies, waits for them, and re-layouts: 4.86 us -> none  [einsum(): return jnp.einsum(*args, precision=high)]
    all_to_all x2, waiting for transfers between devices: 6.94 us -> 4.22 us  [projected_once(): got = lax.all_to_all(sent, ('px', 'py'), 0, 0, tiled=True)]
    all_to_all x2, starting transfers between devices: 12 us -> 10.1 us  [projected_once(): got = lax.all_to_all(sent, ('px', 'py'), 0, 0, tiled=True)]
  transfers between devices with their start and end apart: 10 -> 10, of which waited for: 7 -> 6; matrix products, arithmetic and copies ran while one was open for 8% -> 15% of each run, Pallas kernels for 6% -> 11%
where the time goes in v3:
time: 128 us; the launch traced here: 126 us
  Pallas kernels  53 us (41%)
  starting transfers between devices  23.7 us (19%)
  waiting for transfers between devices  20.6 us (16%)
  local copies, waits for them, and re-layouts  18.5 us (14%)
  other arithmetic  5.49 us (4%)
  matrix products  4.18 us (3%)
    pallas_call x1, Pallas kernels, closure_step(): pl.pallas_call(functools.partial(closure_kernel, (nx, ny, rows, half, spa...  34.1 us
    unnamed x58, local copies, waits for them, and re-layouts  14.1 us
    ppermute x4, waiting for transfers between devices, halo(): lax.ppermute(lax.slice_in_dim(block, block.shape[dim] - width, None, axis...  12.6 us
    ppermute x4, starting transfers between devices, halo(): lax.ppermute(lax.slice_in_dim(block, 0, width, axis=dim), axis, backward)  11.4 us
    all_to_all x2, starting transfers between devices, projected_once(): got = lax.all_to_all(sent, ('px', 'py'), 0, 0, tiled=True)  10.1 us
    pallas_call x3, Pallas kernels, local_call(): pl.pallas_call(kernel, out_shape=jax.ShapeDtypeStruct(shape, jnp.float32)...  9.43 us
    pallas_call x1, Pallas kernels, velocity_step(): pl.pallas_call(functools.partial(velocity_kernel, (nx, ny, rows, half, sp...  9.42 us
    all_to_all x2, waiting for transfers between devices, projected_once(): got = lax.all_to_all(sent, ('px', 'py'), 0, 0, tiled=True)  4.22 us
  transfers between devices with their start and end apart: 10, of which 6 were waited for; matrix products, arithmetic and copies ran while one was open for 15% of the time, Pallas kernels for 11%

profile of v3, /device:TPU:0, one launch (start us, length us, event | category | flops | bytes accessed | tf_op | source)
XLA Modules:
  0.0 125.8 jit_solution(11440410753006581690)
XLA Ops:
  0.0 1.1 copy-done.2
  1.1 0.8 copy-done.8
  2.0 3.4 %forward.1 = f32[32,2,3,8,128]{4,3,2,1,0:T(8,128)} custom-call(f32[3,64,8,128]{3,2,1,0:T(8,128)S(1)} %copy-done.2, bf16[2,128,128]{2,1,0:T(8,128)(2,1)S(1)} %copy-done.8), custom_call_target="tpu_custom_call" | custom-call | tf_op jit(solution)/shard_map/forward/pallas_call | solution.py:401
  5.4 7.3 %all-to-all-start = ((f32[32,2,3,8,128]{4,3,2,1,0:T(8,128)}), f32[32,2,3,8,128]{4,3,2,1,0:T(8,128)S(1)}, u32[]{:S(2)}, u32[]{:S(2)}) async-start(f32[32,2,3,8,128]{4,3,2,1,0:T(8,128)} %forward.1), calls=%async_computation | async-start | bytes 1572864 | tf_op jit(solution)/shard_map/all_to_all | solution.py:430
  12.7 0.0 copy-done.11
  12.7 1.0 fusion.10
  13.7 4.3 %collective-permute-start.1 = (f32[3,64,3,128]{3,2,1,0:T(4,128)}, f32[3,64,3,128]{3,2,1,0:T(4,128)}, u32[]{:S(2)}, u32[]{:S(2)}) collective-permute-start(f32[3,64,3,128]{3,2,1,0:T(4,128)} %get-tuple-element.63), channel_id=1, source_target_pairs={{1,0},{2,1},{3,2},{4,3},{5,4},{6,5},{7,6},{8,7},{9,8},{10,9},{11,1... | collective-permute-start | bytes 884744 | tf_op jit(solution)/shard_map/ppermute | solution.py:30
  18.0 0.0 collective-permute-start
  18.0 0.0 copy-done.18
  18.1 0.1 rev.4
  18.2 0.3 convolution_convert_fusion.1
  18.7 0.7 copy-done.9
  19.4 3.5 %convolution_convert_fusion = bf16[32,8960]{1,0:T(8,128)(2,1)} fusion(bf16[32,162]{0,1:T(8,128)(2,1)S(1)} %reshape.90, bf16[162,8960]{1,0:T(8,128)(2,1)} %constant.73.clone), kind=kOutput, calls=%fused_computation | convolution fusion | flops 93184000 | bytes 3486848 | tf_op jit(solution)/shard_map/dot_general | solution.py:212
  22.9 0.8 slice_dynamic-update-slice_fusion.9
  23.8 0.8 slice_dynamic-update-slice_fusion.8
  24.6 0.8 slice_dynamic-update-slice_fusion.7
  25.4 0.8 slice_dynamic-update-slice_fusion.6
  26.2 0.4 convolution_convert_fusion.2
  26.6 0.0 copy-start.3
  26.6 0.0 copy-start.4
  26.7 0.0 copy-start.5
  26.7 0.0 copy-start.6
  26.7 0.7 fusion.11
  27.5 0.1 broadcast_in_dim_tile.3
  27.5 1.2 concatenate.23
  28.8 0.8 slice_dynamic-update-slice_fusion.5
  29.6 0.8 slice_dynamic-update-slice_fusion.4
  30.4 0.8 slice_dynamic-update-slice_fusion.3
  31.3 0.8 slice_dynamic-update-slice_fusion.2
  32.1 0.8 slice_dynamic-update-slice_fusion.1
  32.9 0.8 slice_dynamic-update-slice_fusion.w2
  33.8 4.2 %all-to-all-done.got = f32[32,2,3,8,128]{4,3,2,1,0:T(8,128)S(1)} async-done(((f32[32,2,3,8,128]{4,3,2,1,0:T(8,128)}), f32[32,2,3,8,128]{4,3,2,1,0:T(8,128)S(1)}, u32[]{:S(2)}, u32[]{:S(2)}) %all-to-all-start) | async-done | bytes 786464 | tf_op jit(solution)/shard_map/all_to_all | solution.py:430
  38.0 4.5 %middle.1 = f32[32,2,3,8,128]{4,3,2,1,0:T(8,128)} custom-call(f32[32,2,3,8,128]{4,3,2,1,0:T(8,128)S(1)} %all-to-all-done.got, f32[3,256]{1,0:T(4,128)S(1)} %pad_maximum_fusion.4.lanes, bf16[2,256,256]{2,1,0:T(8,128)(2,1)S(1)} %copy-done.6, bf16[2,256,512]{2,1,0:T(8,128)(2,1)S(1)} %copy-done.4, bf16[2,256,512]{2,1,0:T(8,128)(2,1)S(1)} %copy-done.3, ...), custom_call_target="tpu_custom_call" | custom-call | tf_op jit(solution)/shard_map/middle/pallas_call | solution.py:401
  42.5 0.0 collective-permute-done.1
  42.5 0.0 collective-permute-done
  42.5 2.8 %all-to-all-start.1 = ((f32[32,2,3,8,128]{4,3,2,1,0:T(8,128)}), f32[32,2,3,8,128]{4,3,2,1,0:T(8,128)S(1)}, u32[]{:S(2)}, u32[]{:S(2)}) async-start(f32[32,2,3,8,128]{4,3,2,1,0:T(8,128)} %middle.1), calls=%async_computation.1 | async-start | bytes 1572864 | tf_op jit(solution)/shard_map/all_to_all | solution.py:461
  45.2 0.1 broadcast.160
  45.3 1.6 %pad_maximum_fusion.3 = f32[3,64,16,128]{3,2,1,0:T(8,128)S(1)} fusion(f32[3,64,2,128]{3,2,1,0:T(2,128)S(1)} %broadcast.160, f32[3,64,3,128]{3,2,1,0:T(4,128)} %collective-permute-done.1, f32[3,64,8,128]{3,2,1,0:T(8,128)S(1)} %copy-done.12, f32[3,64,3,128]{3,2,1,0:T(4,128)} %collective-permute-done), kind=kLoop, calls=%fused_computation.6 | loop fusion | flops 1179648 | bytes 3145728 | tf_op jit(solution)/shard_map/concatenate | solution.py:44
  46.9 1.7 %collective-permute-start.2 = (f32[3,3,16,128]{3,2,1,0:T(8,128)S(1)}, f32[3,3,16,128]{3,2,1,0:T(8,128)S(1)}, u32[]{:S(2)}, u32[]{:S(2)}) collective-permute-start(f32[3,3,16,128]{3,2,1,0:T(8,128)S(1)} %get-tuple-element.59), channel_id=1, source_target_pairs={{0,16},{16,0},{1,17},{17,1},{2,18},{18,2},{3,19},{19,3},{4,20},{20... | collective-permute-start | bytes 221192 | tf_op jit(solution)/shard_map/ppermute | solution.py:27
  48.6 0.4 collective-permute-start.3
  49.0 0.1 copy.17.b1
  49.1 0.0 copy-start.10
  49.2 4.9 %collective-permute-done.2 = f32[3,3,16,128]{3,2,1,0:T(8,128)S(1)} collective-permute-done((f32[3,3,16,128]{3,2,1,0:T(8,128)S(1)}, f32[3,3,16,128]{3,2,1,0:T(8,128)S(1)}, u32[]{:S(2)}, u32[]{:S(2)}) %collective-permute-start.2) | collective-permute-done | bytes 73760 | tf_op jit(solution)/shard_map/ppermute | solution.py:27
  54.1 3.1 %collective-permute-done.3 = f32[3,3,16,128]{3,2,1,0:T(8,128)} collective-permute-done((f32[3,3,16,128]{3,2,1,0:T(8,128)S(1)}, f32[3,3,16,128]{3,2,1,0:T(8,128)}, u32[]{:S(2)}, u32[]{:S(2)}) %collective-permute-start.3) | collective-permute-done | bytes 73760 | tf_op jit(solution)/shard_map/ppermute | solution.py:30
  57.1 1.9 %fusion.1.vel = f32[3,70,16,128]{3,2,1,0:T(8,128)S(1)} fusion(f32[3,64,2,128]{3,2,1,0:T(2,128)} %copy-done.13, f32[3,3,16,128]{3,2,1,0:T(8,128)} %collective-permute-done.3, f32[3,64,3,128]{3,2,1,0:T(4,128)} %collective-permute-done.1, f32[3,64,8,128]{3,2,1,0:T(8,128)} %param.14, f32[3,64,3,128]{3,2,1,0:T(4,128)} %collective-permute-done, ...), kind=kLoop, calls=%fused_computation.8 | loop fusion | flops 2150400 | bytes 3440640 | tf_op jit(solution)/shard_map/concatenate | solution.py:46
  59.0 0.0 copy-start.7
  59.0 9.4 %velocity.1 = (bf16[10560,256]{1,0:T(8,128)(2,1)S(1)}, f32[9,64,8,128]{3,2,1,0:T(8,128)S(1)}) custom-call(f32[3,70,16,128]{3,2,1,0:T(8,128)S(1)} %fusion.1.vel, bf16[320,512]{1,0:T(8,128)(2,1)S(1)} %copy-done.10, f32[320,1]{1,0:T(8,128)S(1)} %copy.17.b1), custom_call_target="tpu_custom_call" | custom-call | flops 2768240640 | bytes 12582912 | tf_op jit(solution)/shard_map/velocity/pallas_call | solution.py:239
  68.5 0.0 copy-start
  68.5 2.4 %copy-done = bf16[10560,256]{1,0:T(8,128)(2,1)} copy-done((bf16[10560,256]{1,0:T(8,128)(2,1)}, bf16[10560,256]{1,0:T(8,128)(2,1)S(1)}, u32[]{:S(2)}) %copy-start) | copy-done | bytes 5406744
  70.8 1.4 %copy-done.1 = f32[9,64,8,128]{3,2,1,0:T(8,128)} copy-done((f32[9,64,8,128]{3,2,1,0:T(8,128)}, f32[9,64,8,128]{3,2,1,0:T(8,128)S(1)}, u32[]{:S(2)}) %copy-start.1) | copy-done | bytes 2359320
  72.3 0.0 all-to-all-done.1.got
  72.3 1.5 %backward.1 = f32[3,64,8,128]{3,2,1,0:T(8,128)S(1)} custom-call(f32[32,2,3,8,128]{4,3,2,1,0:T(8,128)S(1)} %all-to-all-done.1.got, bf16[2,128,128]{2,1,0:T(8,128)(2,1)S(1)} %copy-done.7), custom_call_target="tpu_custom_call" | custom-call | tf_op jit(solution)/shard_map/backward/pallas_call | solution.py:401
  73.8 0.1 fusion.9
  74.0 0.1 collective-permute-start.4
  74.0 5.1 %collective-permute-start.5 = (f32[3,64,3,128]{3,2,1,0:T(4,128)S(1)}, f32[3,64,3,128]{3,2,1,0:T(4,128)S(1)}, u32[]{:S(2)}, u32[]{:S(2)}) collective-permute-start(f32[3,64,3,128]{3,2,1,0:T(4,128)S(1)} %get-tuple-element.62), channel_id=1, source_target_pairs={{1,0},{2,1},{3,2},{4,3},{5,4},{6,5},{7,6},{8,7},{9,8},{10,9},{11,1... | collective-permute-start | bytes 884744 | tf_op jit(solution)/shard_map/ppermute | solution.py:30
  79.1 5.3 %collective-permute-done.4 = f32[3,64,3,128]{3,2,1,0:T(4,128)S(1)} collective-permute-done((f32[3,64,3,128]{3,2,1,0:T(4,128)S(1)}, f32[3,64,3,128]{3,2,1,0:T(4,128)S(1)}, u32[]{:S(2)}, u32[]{:S(2)}) %collective-permute-start.4) | collective-permute-done | bytes 294944 | tf_op jit(solution)/shard_map/ppermute | solution.py:27
  84.4 0.0 collective-permute-done.5
  84.4 0.4 pad_maximum_fusion.2
  84.8 0.5 collective-permute-start.6
  85.3 1.6 %collective-permute-start.7 = (f32[3,3,16,128]{3,2,1,0:T(8,128)S(1)}, f32[3,3,16,128]{3,2,1,0:T(8,128)S(1)}, u32[]{:S(2)}, u32[]{:S(2)}) collective-permute-start(f32[3,3,16,128]{3,2,1,0:T(8,128)S(1)} %get-tuple-element.58), channel_id=1, source_target_pairs={{16,0},{0,16},{17,1},{1,17},{18,2},{2,18},{19,3},{3,19},{20,4},{4,... | collective-permute-start | bytes 221192 | tf_op jit(solution)/shard_map/ppermute | solution.py:30
  86.9 2.3 %collective-permute-done.6 = f32[3,3,16,128]{3,2,1,0:T(8,128)S(1)} collective-permute-done((f32[3,3,16,128]{3,2,1,0:T(8,128)S(1)}, f32[3,3,16,128]{3,2,1,0:T(8,128)S(1)}, u32[]{:S(2)}, u32[]{:S(2)}) %collective-permute-start.6) | collective-permute-done | bytes 73760 | tf_op jit(solution)/shard_map/ppermute | solution.py:27
  89.3 0.8 collective-permute-done.7
  90.0 1.6 %fusion.3.lam = f32[3,70,16,128]{3,2,1,0:T(8,128)} fusion(f32[3,64,2,128]{3,2,1,0:T(2,128)S(1)} %copy-done.14, f32[3,3,16,128]{3,2,1,0:T(8,128)S(1)} %collective-permute-done.7, f32[3,64,3,128]{3,2,1,0:T(4,128)S(1)} %collective-permute-done.5, f32[3,64,8,128]{3,2,1,0:T(8,128)S(1)} %backward.1, f32[3,64,3,128]{3,2,1,0:T(4,128)S(1)} %collective-permute-done.4, ...), kind=kLoop, calls=%fused_computation.10 | loop fusion | flops 2150400 | bytes 3440640 | tf_op jit(solution)/shard_map/concatenate | solution.py:46
  91.7 34.1 %closure.1 = f32[3,64,8,128]{3,2,1,0:T(8,128)} custom-call(f32[3,70,16,128]{3,2,1,0:T(8,128)S(1)} %fusion.1.vel, f32[3,70,16,128]{3,2,1,0:T(8,128)} %fusion.3.lam, bf16[10560,256]{1,0:T(8,128)(2,1)} %copy-done, f32[9,64,8,128]{3,2,1,0:T(8,128)} %copy-done.1, bf16[320,896]{1,0:T(8,128)(2,1)S(1)} %slice_dynamic-update-slice_fusion.w2, ...), custom_call_target="tpu_custom_call" | custom-call | tf_op jit(solution)/shard_map/closure/pallas_call | solution.py:262
  (45 shorter events, 0.2 us)
Async XLA Ops:
  0.0 1.1 copy-start.2
  1.1 0.8 copy-start.8
  2.0 10.7 %copy-start.11 = (f32[3,64,8,128]{3,2,1,0:T(8,128)S(1)}, f32[3,64,8,128]{3,2,1,0:T(8,128)}, u32[]{:S(2)}) copy-start(f32[3,64,8,128]{3,2,1,0:T(8,128)} %param.14) | copy-start | bytes 2359300
  5.4 12.6 %copy-start.18 = (bf16[32,3,3,3,3]{0,4,3,2,1:T(4,128)(2,1)S(1)}, bf16[32,3,3,3,3]{0,4,3,2,1:T(4,128)(2,1)}, u32[]{:S(2)}) copy-start(bf16[32,3,3,3,3]{0,4,3,2,1:T(4,128)(2,1)} %param.16) | copy-start | bytes 15556
  5.4 12.7 %copy-start.17 = (bf16[6,32,3,3,3]{1,4,3,2,0:T(4,128)(2,1)S(1)}, bf16[6,32,3,3,3]{1,4,3,2,0:T(4,128)(2,1)}, u32[]{:S(2)}) copy-start(bf16[6,32,3,3,3]{1,4,3,2,0:T(4,128)(2,1)} %param.18) | copy-start | bytes 31108
  5.4 12.8 %copy-start.15 = (bf16[81,5120]{1,0:T(8,128)(2,1)S(1)}, bf16[81,5120]{1,0:T(8,128)(2,1)}, u32[]{:S(2)}) copy-start(bf16[81,5120]{1,0:T(8,128)(2,1)} %constant.72.clone) | copy-start | bytes 2488324
  5.4 32.6 %all-to-all-start = ((f32[32,2,3,8,128]{4,3,2,1,0:T(8,128)}), f32[32,2,3,8,128]{4,3,2,1,0:T(8,128)S(1)}, u32[]{:S(2)}, u32[]{:S(2)}) async-start(f32[32,2,3,8,128]{4,3,2,1,0:T(8,128)} %forward.1), calls=%async_computation | async-start | bytes 1572864 | tf_op jit(solution)/shard_map/all_to_all | solution.py:430
  13.7 28.7 %collective-permute-start.1 = (f32[3,64,3,128]{3,2,1,0:T(4,128)}, f32[3,64,3,128]{3,2,1,0:T(4,128)}, u32[]{:S(2)}, u32[]{:S(2)}) collective-permute-start(f32[3,64,3,128]{3,2,1,0:T(4,128)} %get-tuple-element.63), channel_id=1, source_target_pairs={{1,0},{2,1},{3,2},{4,3},{5,4},{6,5},{7,6},{8,7},{9,8},{10,9},{11,1... | collective-permute-start | bytes 884744 | tf_op jit(solution)/shard_map/ppermute | solution.py:30
  18.0 24.4 %collective-permute-start = (f32[3,64,3,128]{3,2,1,0:T(4,128)}, f32[3,64,3,128]{3,2,1,0:T(4,128)}, u32[]{:S(2)}, u32[]{:S(2)}) collective-permute-start(f32[3,64,3,128]{3,2,1,0:T(4,128)} %get-tuple-element.64), channel_id=1, source_target_pairs={{0,1},{1,2},{2,3},{3,4},{4,5},{5,6},{6,7},{7,8},{8,9},{9,10},{10,1... | collective-permute-start | bytes 884744 | tf_op jit(solution)/shard_map/ppermute | solution.py:27
  18.7 0.7 copy-start.9
  19.4 6.8 %copy-start.16 = (bf16[81,2560]{1,0:T(8,128)(2,1)S(1)}, bf16[81,2560]{1,0:T(8,128)(2,1)}, u32[]{:S(2)}) copy-start(bf16[81,2560]{1,0:T(8,128)(2,1)} %constant.74.clone) | copy-start | bytes 1244164
  22.9 4.5 %copy-start.19 = (f32[32]{0:T(128)S(1)}, f32[32]{0:T(128)}, u32[]{:S(2)}) copy-start(f32[32]{0:T(128)} %param.17) | copy-start | bytes 388
  26.6 11.3 %copy-start.3 = (bf16[2,256,512]{2,1,0:T(8,128)(2,1)S(1)}, bf16[2,256,512]{2,1,0:T(8,128)(2,1)}, u32[]{:S(2)}) copy-start(bf16[2,256,512]{2,1,0:T(8,128)(2,1)} %constant.77.clone.bx) | copy-start | bytes 1572868
  26.6 11.3 %copy-start.4 = (bf16[2,256,512]{2,1,0:T(8,128)(2,1)S(1)}, bf16[2,256,512]{2,1,0:T(8,128)(2,1)}, u32[]{:S(2)}) copy-start(bf16[2,256,512]{2,1,0:T(8,128)(2,1)} %constant.76.clone.fx) | copy-start | bytes 1572868
  26.7 11.3 %copy-start.5 = (bf16[2,256,256]{2,1,0:T(8,128)(2,1)S(1)}, bf16[2,256,256]{2,1,0:T(8,128)(2,1)}, u32[]{:S(2)}) copy-start(bf16[2,256,256]{2,1,0:T(8,128)(2,1)} %constant.78.clone.by) | copy-start | bytes 786436
  26.7 11.3 %copy-start.6 = (bf16[2,256,256]{2,1,0:T(8,128)(2,1)S(1)}, bf16[2,256,256]{2,1,0:T(8,128)(2,1)}, u32[]{:S(2)}) copy-start(bf16[2,256,256]{2,1,0:T(8,128)(2,1)} %constant.75.clone.fy) | copy-start | bytes 786436
  42.5 2.9 %copy-start.12 = (f32[3,64,8,128]{3,2,1,0:T(8,128)S(1)}, f32[3,64,8,128]{3,2,1,0:T(8,128)}, u32[]{:S(2)}) copy-start(f32[3,64,8,128]{3,2,1,0:T(8,128)} %param.14) | copy-start | bytes 2359300
  42.5 29.8 %all-to-all-start.1 = ((f32[32,2,3,8,128]{4,3,2,1,0:T(8,128)}), f32[32,2,3,8,128]{4,3,2,1,0:T(8,128)S(1)}, u32[]{:S(2)}, u32[]{:S(2)}) async-start(f32[32,2,3,8,128]{4,3,2,1,0:T(8,128)} %middle.1), calls=%async_computation.1 | async-start | bytes 1572864 | tf_op jit(solution)/shard_map/all_to_all | solution.py:461
  45.3 8.8 %copy-start.13 = (f32[3,64,2,128]{3,2,1,0:T(2,128)}, f32[3,64,2,128]{3,2,1,0:T(2,128)S(1)}, u32[]{:S(2)}) copy-start(f32[3,64,2,128]{3,2,1,0:T(2,128)S(1)} %broadcast.160) | copy-start | bytes 589828
  46.9 7.2 %collective-permute-start.2 = (f32[3,3,16,128]{3,2,1,0:T(8,128)S(1)}, f32[3,3,16,128]{3,2,1,0:T(8,128)S(1)}, u32[]{:S(2)}, u32[]{:S(2)}) collective-permute-start(f32[3,3,16,128]{3,2,1,0:T(8,128)S(1)} %get-tuple-element.59), channel_id=1, source_target_pairs={{0,16},{16,0},{1,17},{17,1},{2,18},{18,2},{3,19},{19,3},{4,20},{20... | collective-permute-start | bytes 221192 | tf_op jit(solution)/shard_map/ppermute | solution.py:27
  48.6 8.5 %collective-permute-start.3 = (f32[3,3,16,128]{3,2,1,0:T(8,128)S(1)}, f32[3,3,16,128]{3,2,1,0:T(8,128)}, u32[]{:S(2)}, u32[]{:S(2)}) collective-permute-start(f32[3,3,16,128]{3,2,1,0:T(8,128)S(1)} %get-tuple-element.60), channel_id=1, source_target_pairs={{16,0},{0,16},{17,1},{1,17},{18,2},{2,18},{19,3},{3,19},{20,4},{4,... | collective-permute-start | bytes 221192 | tf_op jit(solution)/shard_map/ppermute | solution.py:30
  49.1 9.9 %copy-start.10 = (bf16[320,512]{1,0:T(8,128)(2,1)S(1)}, bf16[320,512]{1,0:T(8,128)(2,1)}, u32[]{:S(2)}) copy-start(bf16[320,512]{1,0:T(8,128)(2,1)} %copy-done.9) | copy-start | bytes 983044
  59.0 13.2 %copy-start.7 = (bf16[2,128,128]{2,1,0:T(8,128)(2,1)S(1)}, bf16[2,128,128]{2,1,0:T(8,128)(2,1)}, u32[]{:S(2)}) copy-start(bf16[2,128,128]{2,1,0:T(8,128)(2,1)} %constant.79.clone.table) | copy-start | bytes 196612
  68.5 2.4 %copy-start = (bf16[10560,256]{1,0:T(8,128)(2,1)}, bf16[10560,256]{1,0:T(8,128)(2,1)S(1)}, u32[]{:S(2)}) copy-start(bf16[10560,256]{1,0:T(8,128)(2,1)S(1)} %get-tuple-element.53.slope) | copy-start | bytes 16220164
  70.8 1.4 %copy-start.1 = (f32[9,64,8,128]{3,2,1,0:T(8,128)}, f32[9,64,8,128]{3,2,1,0:T(8,128)S(1)}, u32[]{:S(2)}) copy-start(f32[9,64,8,128]{3,2,1,0:T(8,128)S(1)} %get-tuple-element.54.grads) | copy-start | bytes 7077892
  72.3 12.2 %copy-start.14 = (f32[3,64,2,128]{3,2,1,0:T(2,128)S(1)}, f32[3,64,2,128]{3,2,1,0:T(2,128)}, u32[]{:S(2)}) copy-start(f32[3,64,2,128]{3,2,1,0:T(2,128)} %copy-done.13) | copy-start | bytes 589828
  74.0 10.5 %collective-permute-start.4 = (f32[3,64,3,128]{3,2,1,0:T(4,128)S(1)}, f32[3,64,3,128]{3,2,1,0:T(4,128)S(1)}, u32[]{:S(2)}, u32[]{:S(2)}) collective-permute-start(f32[3,64,3,128]{3,2,1,0:T(4,128)S(1)} %get-tuple-element.61), channel_id=1, source_target_pairs={{0,1},{1,2},{2,3},{3,4},{4,5},{5,6},{6,7},{7,8},{8,9},{9,10},{10,1... | collective-permute-start | bytes 884744 | tf_op jit(solution)/shard_map/ppermute | solution.py:27
  74.0 10.4 %collective-permute-start.5 = (f32[3,64,3,128]{3,2,1,0:T(4,128)S(1)}, f32[3,64,3,128]{3,2,1,0:T(4,128)S(1)}, u32[]{:S(2)}, u32[]{:S(2)}) collective-permute-start(f32[3,64,3,128]{3,2,1,0:T(4,128)S(1)} %get-tuple-element.62), channel_id=1, source_target_pairs={{1,0},{2,1},{3,2},{4,3},{5,4},{6,5},{7,6},{8,7},{9,8},{10,9},{11,1... | collective-permute-start | bytes 884744 | tf_op jit(solution)/shard_map/ppermute | solution.py:30
  84.8 4.4 %collective-permute-start.6 = (f32[3,3,16,128]{3,2,1,0:T(8,128)S(1)}, f32[3,3,16,128]{3,2,1,0:T(8,128)S(1)}, u32[]{:S(2)}, u32[]{:S(2)}) collective-permute-start(f32[3,3,16,128]{3,2,1,0:T(8,128)S(1)} %get-tuple-element.57), channel_id=1, source_target_pairs={{0,16},{16,0},{1,17},{17,1},{2,18},{18,2},{3,19},{19,3},{4,20},{20... | collective-permute-start | bytes 221192 | tf_op jit(solution)/shard_map/ppermute | solution.py:27
  85.3 4.7 %collective-permute-start.7 = (f32[3,3,16,128]{3,2,1,0:T(8,128)S(1)}, f32[3,3,16,128]{3,2,1,0:T(8,128)S(1)}, u32[]{:S(2)}, u32[]{:S(2)}) collective-permute-start(f32[3,3,16,128]{3,2,1,0:T(8,128)S(1)} %get-tuple-element.58), channel_id=1, source_target_pairs={{16,0},{0,16},{17,1},{1,17},{18,2},{2,18},{19,3},{3,19},{20,4},{4,... | collective-permute-start | bytes 221192 | tf_op jit(solution)/shard_map/ppermute | solution.py:30

commit v4 on v3

--- a/solution.py
+++ b/solution.py
@@ -31,17 +31,17 @@
     return low, high_side
 
 
-def bordered(block):
-    return bordered_rest(block, *halo(block, "py", 2, 3))
-
-
-def bordered_rest(block, low, up):
+def widened(block, low, up):
     ny = block.shape[2]
     extra = rows_of(ny) - ny - 6
-    parts = [low, block, up]
+    parts = [block, up]
     if extra:
         parts.append(jnp.zeros(block.shape[:2] + (extra,) + block.shape[3:], block.dtype))
-    wide = jnp.concatenate(parts, axis=2)
+    return jnp.concatenate(parts + [low], axis=2)
+
+
+def bordered(block):
+    wide = widened(block, *halo(block, "py", 2, 3))
     low, up = halo(wide, "px", 1, 3)
     return jnp.concatenate([low, wide, up], axis=1)
 
@@ -90,18 +90,17 @@
 
     def gradient(x):
         e = x + 3
-        mid = slice(3, 3 + ny)
         for c in range(3):
-            v0 = vel[c, e, mid]
+            wide = vel[c, e]
             for b in range(3):
                 total = 0.0
                 for d, weight in taps:
                     if b == 0:
-                        pair = vel[c, e + d, mid] - vel[c, e - d, mid]
+                        pair = vel[c, e + d, :ny] - vel[c, e - d, :ny]
                     elif b == 1:
-                        pair = vel[c, e, 3 + d : 3 + d + ny] - vel[c, e, 3 - d : 3 - d + ny]
+                        pair = (pltpu.roll(wide, rows - d, 0) - pltpu.roll(wide, d, 0))[:ny]
                     else:
-                        pair = zroll(v0, -d) - zroll(v0, d)
+                        pair = zroll(wide[:ny], -d) - zroll(wide[:ny], d)
                     total += (weight / (60.0 * spacings[b])) * pair
                 grads[3 * b + c, x] = total
 
@@ -156,16 +155,18 @@
         lanes = slice(side * LANES, (side + 1) * LANES)
         low = [acc[idx, d * 3 * ny : (d + 1) * 3 * ny, lanes] for d in range(3)]
         closure = zroll(low[0], -1) + low[1] + zroll(low[2], 1)
-        mid = slice(3, 3 + ny)
-        l0 = [lam[c, e, mid] for c in range(3)]
-        vz = vel[2, e, mid]
+        wide = [lam[c, e] for c in range(3)]
+        l0 = [value[:ny] for value in wide]
+        vy = vel[1, e]
+        vz = vel[2, e, :ny]
+        vx = {q: vel[0, e + q, :ny] for d, _ in taps for q in (d, -d)}
         for c in range(3):
             total = closure[c * ny : (c + 1) * ny]
+            ly = wide[c] * vy
             lz = l0[c] * vz
             for d, weight in taps:
-                fx = lam[c, e + d, mid] * vel[0, e + d, mid] - lam[c, e - d, mid] * vel[0, e - d, mid]
-                up, down = slice(3 + d, 3 + d + ny), slice(3 - d, 3 - d + ny)
-                fy = lam[c, e, up] * vel[1, e, up] - lam[c, e, down] * vel[1, e, down]
+                fx = lam[c, e + d, :ny] * vx[d] - lam[c, e - d, :ny] * vx[-d]
+                fy = (pltpu.roll(ly, rows - d, 0) - pltpu.roll(ly, d, 0))[:ny]
                 fz = zroll(lz, -d) - zroll(lz, d)
                 for b, pair in enumerate((fx, fy, fz)):
                     total += (weight / (60.0 * spacings[b])) * pair
@@ -188,7 +189,7 @@
             for d in range(3):
                 for z in range(3):
                     for p in range(ny + 2):
-                        table[c, x, d, z, p, x, z, c, p + d + 1] = 1.0
+                        table[c, x, d, z, p, x, z, c, (p + d - 2) % rows] = 1.0
     table = table.reshape(27 * channels, ny + 2, 9 * channels * rows)
     extra = lane_padded(table.shape[2]) - table.shape[2]
     return np.pad(table, ((0, 0), (0, 0), (0, extra)))
@@ -245,7 +246,7 @@
         in_specs=[vm] * 3,
         out_specs=(vm, vm),
         scratch_shapes=[pltpu.VMEM(((half + 2) * 9 * rows, 2 * LANES), jnp.bfloat16)],
-        compiler_params=pltpu.CompilerParams(vmem_limit_bytes=40 * 2**20),
+        compiler_params=pltpu.CompilerParams(vmem_limit_bytes=20 * 2**20),
         cost_estimate=pl.CostEstimate(
             flops=2 * half * w1.shape[0] * w1.shape[1] * 2 * LANES,
             bytes_accessed=12 * 2**20,
@@ -268,7 +269,7 @@
             pltpu.VMEM(((half + 2) * 18 * rows, 2 * LANES), jnp.bfloat16),
             pltpu.VMEM((half + 2, 9 * ny, 2 * LANES), jnp.float32),
         ],
-        compiler_params=pltpu.CompilerParams(vmem_limit_bytes=50 * 2**20),
+        compiler_params=pltpu.CompilerParams(vmem_limit_bytes=28 * 2**20),
         name="closure",
     )(vel_ext, lam_ext, slope, grads, w2, w3)
 
@@ -528,11 +529,13 @@
     def beside_first(velocity, weight_in, bias_in, weight_out):
         w1, bias = input_weights(weight_in, bias_in, ny, rows)
         w2, w3 = output_weights(weight_in, weight_out, ny, rows)
-        return (w1, bias, w2, w3), (velocity,) + halo(velocity, "py", 2, 3)
+        wide = widened(velocity, *halo(velocity, "py", 2, 3))
+        return (w1, bias, w2, w3, wide), halo(wide, "px", 1, 3)
 
     def beside_second(first, halo_first):
-        w1, bias, w2, w3 = first
-        vel_ext = bordered_rest(*halo_first)
+        w1, bias, w2, w3, wide = first
+        low, up = halo_first
+        vel_ext = jnp.concatenate([low, wide, up], axis=1)
         slope, grads = velocity_step(vel_ext, w1, bias, nx, ny, spacings)
         return vel_ext, slope, grads, w2, w3
 

time: 128 us -> 120 us (0.938); the launches traced: 126 us -> 120 us
  waiting for transfers between devices: 20.6 us -> 33.9 us
  local copies, waits for them, and re-layouts: 18.5 us -> 9.31 us
  Pallas kernels: 53 us -> 49.1 us
  other arithmetic: 5.49 us -> 2.41 us
  starting transfers between devices: 23.7 us -> 21.3 us
    ppermute x4, waiting for transfers between devices: 3.86 us -> 14 us  [halo(): lax.ppermute(lax.slice_in_dim(block, 0, width, axis=dim), axis, backward)]
    unnamed x58 -> x70, local copies, waits for them, and re-layouts: 14.1 us -> 7.52 us
    ppermute x4, starting transfers between devices: 11.4 us -> 6.75 us  [halo(): lax.ppermute(lax.slice_in_dim(block, 0, width, axis=dim), axis, backward)]
    pallas_call x1, Pallas kernels: 34.1 us -> 30.2 us  [closure_step(): pl.pallas_call(functools.partial(closure_kernel, (nx, ny, rows, half, spa...]
    all_to_all x2, waiting for transfers between devices: 4.22 us -> 7.31 us  [projected_once(): got = lax.all_to_all(sent, ('px', 'py'), 0, 0, tiled=True)]
    concatenate x4 -> x3, other arithmetic: 5.46 us -> 2.39 us  [the longest x2 2.08 us: widened(): return jnp.concatenate(parts + [low], axis=2)]
    all_to_all x2, starting transfers between devices: 10.1 us -> 12.3 us  [projected_once(): got = lax.all_to_all(sent, ('px', 'py'), 0, 0, tiled=True)]
    concatenate x3, local copies, waits for them, and re-layouts: 2.03 us -> 0.27 us  [spread(): jnp.concatenate([wide[:, p * columns:(p + 1) * columns] for p in range(ta...]
  transfers between devices with their start and end apart: 10 -> 10, of which waited for: 6 -> 7; matrix products, arithmetic and copies ran while one was open for 15% -> 6% of each run, Pallas kernels for 11% -> 12%
where the time goes in v4:
time: 120 us
  Pallas kernels  49.1 us (41%)
  waiting for transfers between devices  33.9 us (28%)
  starting transfers between devices  21.3 us (18%)
  local copies, waits for them, and re-layouts  9.31 us (8%)
  matrix products  3.37 us (3%)
  other arithmetic  2.41 us (2%)
    pallas_call x1, Pallas kernels, closure_step(): pl.pallas_call(functools.partial(closure_kernel, (nx, ny, rows, half, spa...  30.2 us
    ppermute x4, waiting for transfers between devices, halo(): lax.ppermute(lax.slice_in_dim(block, 0, width, axis=dim), axis, backward)  14 us
    ppermute x4, waiting for transfers between devices, halo(): lax.ppermute(lax.slice_in_dim(block, block.shape[dim] - width, None, axis...  12.6 us
    all_to_all x2, starting transfers between devices, projected_once(): got = lax.all_to_all(sent, ('px', 'py'), 0, 0, tiled=True)  12.3 us
    pallas_call x1, Pallas kernels, velocity_step(): pl.pallas_call(functools.partial(velocity_kernel, (nx, ny, rows, half, sp...  9.49 us
    pallas_call x3, Pallas kernels, local_call(): pl.pallas_call(kernel, out_shape=jax.ShapeDtypeStruct(shape, jnp.float32)...  9.42 us
    unnamed x70, local copies, waits for them, and re-layouts  7.52 us
    all_to_all x2, waiting for transfers between devices, projected_once(): got = lax.all_to_all(sent, ('px', 'py'), 0, 0, tiled=True)  7.31 us
  transfers between devices with their start and end apart: 10, of which 7 were waited for; matrix products, arithmetic and copies ran while one was open for 6% of the time, Pallas kernels for 12%

profile of v4, /device:TPU:0, one launch (start us, length us, event | category | flops | bytes accessed | tf_op | source)
XLA Modules:
  0.0 119.9 jit_solution(15225477508499094268)
XLA Ops:
  0.0 1.1 copy-done.4
  1.1 0.8 copy-done.12
  2.0 3.4 %forward.1 = f32[32,2,3,8,128]{4,3,2,1,0:T(8,128)} custom-call(f32[3,64,8,128]{3,2,1,0:T(8,128)S(1)} %copy-done.4, bf16[2,128,128]{2,1,0:T(8,128)(2,1)S(1)} %copy-done.12), custom_call_target="tpu_custom_call" | custom-call | tf_op jit(solution)/shard_map/forward/pallas_call | solution.py:402
  5.4 7.3 %all-to-all-start = ((f32[32,2,3,8,128]{4,3,2,1,0:T(8,128)}), f32[32,2,3,8,128]{4,3,2,1,0:T(8,128)S(1)}, u32[]{:S(2)}, u32[]{:S(2)}) async-start(f32[32,2,3,8,128]{4,3,2,1,0:T(8,128)} %forward.1), calls=%async_computation | async-start | bytes 1572864 | tf_op jit(solution)/shard_map/all_to_all | solution.py:431
  12.7 0.0 copy-done.19
  12.7 0.9 fusion.8
  13.6 4.3 %collective-permute-start = (f32[3,64,3,128]{3,2,1,0:T(4,128)}, f32[3,64,3,128]{3,2,1,0:T(4,128)}, u32[]{:S(2)}, u32[]{:S(2)}) collective-permute-start(f32[3,64,3,128]{3,2,1,0:T(4,128)} %get-tuple-element.65), channel_id=1, source_target_pairs={{1,0},{2,1},{3,2},{4,3},{5,4},{6,5},{7,6},{8,7},{9,8},{10,9},{11,1... | collective-permute-start | bytes 884744 | tf_op jit(solution)/shard_map/ppermute | solution.py:30
  17.9 0.0 collective-permute-start.1
  17.9 0.0 copy-done.23
  17.9 0.0 copy-done.22
  17.9 0.1 rev.4
  18.1 0.0 copy-done.20
  18.1 0.3 convolution_convert_fusion.1
  18.5 0.0 copy-start.13
  18.5 0.7 copy-done.13
  19.3 2.7 %convolution_convert_fusion = bf16[32,8960]{1,0:T(8,128)(2,1)S(1)} fusion(bf16[32,162]{0,1:T(8,128)(2,1)S(1)} %reshape.90, bf16[162,8960]{1,0:T(8,128)(2,1)} %constant.73.clone), kind=kOutput, calls=%fused_computation | convolution fusion | flops 93184000 | bytes 3486848 | tf_op jit(solution)/shard_map/dot_general | solution.py:213
  22.0 0.0 copy-done.21
  22.0 0.4 convolution_convert_fusion.2
  22.5 0.1 copy-done.24
  22.6 0.1 broadcast_in_dim_tile.3
  22.7 0.2 concatenate.23
  23.0 0.0 copy-start.5
  23.0 7.5 %collective-permute-done = f32[3,64,3,128]{3,2,1,0:T(4,128)} collective-permute-done((f32[3,64,3,128]{3,2,1,0:T(4,128)}, f32[3,64,3,128]{3,2,1,0:T(4,128)}, u32[]{:S(2)}, u32[]{:S(2)}) %collective-permute-start) | collective-permute-done | bytes 294944 | tf_op jit(solution)/shard_map/ppermute | solution.py:30
  30.5 4.8 %collective-permute-done.1 = f32[3,64,3,128]{3,2,1,0:T(4,128)} collective-permute-done((f32[3,64,3,128]{3,2,1,0:T(4,128)S(1)}, f32[3,64,3,128]{3,2,1,0:T(4,128)}, u32[]{:S(2)}, u32[]{:S(2)}) %collective-permute-start.1) | collective-permute-done | bytes 294944 | tf_op jit(solution)/shard_map/ppermute | solution.py:27
  35.4 0.1 broadcast.158
  35.4 0.0 copy-start.17
  35.5 0.0 copy-start.7
  35.5 0.0 copy-start.8
  35.5 0.0 copy-start.9
  35.5 0.0 copy-start.10
  35.5 1.8 %fusion = f32[3,64,16,128]{3,2,1,0:T(8,128)S(1)} fusion(f32[3,64,2,128]{3,2,1,0:T(2,128)S(1)} %broadcast.158, f32[3,64,3,128]{3,2,1,0:T(4,128)} %collective-permute-done.1, f32[3,64,3,128]{3,2,1,0:T(4,128)} %collective-permute-done, f32[3,64,8,128]{3,2,1,0:T(8,128)} %param.14), kind=kLoop, calls=%fused_computation.6 | loop fusion | flops 1179648 | bytes 3145728 | tf_op jit(solution)/shard_map/concatenate | solution.py:40
  37.3 0.0 copy-done.5
  37.3 0.0 copy-start.15
  37.4 1.6 %collective-permute-start.3 = (f32[3,3,16,128]{3,2,1,0:T(8,128)S(1)}, f32[3,3,16,128]{3,2,1,0:T(8,128)S(1)}, u32[]{:S(2)}, u32[]{:S(2)}) collective-permute-start(f32[3,3,16,128]{3,2,1,0:T(8,128)S(1)} %get-tuple-element.61), channel_id=1, source_target_pairs={{16,0},{0,16},{17,1},{1,17},{18,2},{2,18},{19,3},{3,19},{20,4},{4,... | collective-permute-start | bytes 221192 | tf_op jit(solution)/shard_map/ppermute | solution.py:30
  38.9 0.5 collective-permute-start.2
  39.5 0.0 all-to-all-done.got
  39.5 4.5 %middle.1 = f32[32,2,3,8,128]{4,3,2,1,0:T(8,128)} custom-call(f32[32,2,3,8,128]{4,3,2,1,0:T(8,128)S(1)} %all-to-all-done.got, f32[3,256]{1,0:T(4,128)S(1)} %pad_maximum_fusion.3.lanes, bf16[2,256,256]{2,1,0:T(8,128)(2,1)S(1)} %copy-done.10, bf16[2,256,512]{2,1,0:T(8,128)(2,1)S(1)} %copy-done.8, bf16[2,256,512]{2,1,0:T(8,128)(2,1)S(1)} %copy-done.7, ...), custom_call_target="tpu_custom_call" | custom-call | tf_op jit(solution)/shard_map/middle/pallas_call | solution.py:402
  44.0 0.0 collective-permute-done.3
  44.0 0.0 collective-permute-done.2
  44.0 5.0 %all-to-all-start.1 = ((f32[32,2,3,8,128]{4,3,2,1,0:T(8,128)}), f32[32,2,3,8,128]{4,3,2,1,0:T(8,128)S(1)}, u32[]{:S(2)}, u32[]{:S(2)}) async-start(f32[32,2,3,8,128]{4,3,2,1,0:T(8,128)} %middle.1), calls=%async_computation.1 | async-start | bytes 1572864 | tf_op jit(solution)/shard_map/all_to_all | solution.py:462
  49.0 0.1 copy.17.b1
  49.1 0.0 copy-done.16
  49.1 0.1 constant_dynamic-update-slice_fusion.11
  49.3 0.8 copy-done.14
  50.1 9.5 %velocity.1 = (bf16[10560,256]{1,0:T(8,128)(2,1)S(1)}, f32[9,64,8,128]{3,2,1,0:T(8,128)S(1)}) custom-call(f32[3,70,16,128]{3,2,1,0:T(8,128)S(1)} %constant_dynamic-update-slice_fusion.10.vel, bf16[320,512]{1,0:T(8,128)(2,1)S(1)} %copy-done.14, f32[320,1]{1,0:T(8,128)S(1)} %copy.17.b1), custom_call_target="tpu_custom_call" | custom-call | flops 2768240640 | bytes 12582912 | tf_op jit(solution)/shard_map/velocity/pallas_call | solution.py:240
  59.6 2.4 %copy-done = bf16[10560,256]{1,0:T(8,128)(2,1)} copy-done((bf16[10560,256]{1,0:T(8,128)(2,1)}, bf16[10560,256]{1,0:T(8,128)(2,1)S(1)}, u32[]{:S(2)}) %copy-start) | copy-done | bytes 5406744
  62.0 1.2 %copy-done.2 = f32[3,70,16,128]{3,2,1,0:T(8,128)} copy-done((f32[3,70,16,128]{3,2,1,0:T(8,128)}, f32[3,70,16,128]{3,2,1,0:T(8,128)S(1)}, u32[]{:S(2)}) %copy-start.2) | copy-done | bytes 1720344
  63.2 7.3 %all-to-all-done.1.got = f32[32,2,3,8,128]{4,3,2,1,0:T(8,128)S(1)} async-done(((f32[32,2,3,8,128]{4,3,2,1,0:T(8,128)}), f32[32,2,3,8,128]{4,3,2,1,0:T(8,128)S(1)}, u32[]{:S(2)}, u32[]{:S(2)}) %all-to-all-start.1) | async-done | bytes 786464 | tf_op jit(solution)/shard_map/all_to_all | solution.py:462
  70.5 1.5 %backward.1 = f32[3,64,8,128]{3,2,1,0:T(8,128)S(1)} custom-call(f32[32,2,3,8,128]{4,3,2,1,0:T(8,128)S(1)} %all-to-all-done.1.got, bf16[2,128,128]{2,1,0:T(8,128)(2,1)S(1)} %copy-done.11), custom_call_target="tpu_custom_call" | custom-call | tf_op jit(solution)/shard_map/backward/pallas_call | solution.py:402
  72.1 0.1 fusion.7
  72.2 0.2 collective-permute-start.4
  72.4 0.3 collective-permute-start.5
  72.8 5.0 %collective-permute-done.4 = f32[3,64,3,128]{3,2,1,0:T(4,128)S(1)} collective-permute-done((f32[3,64,3,128]{3,2,1,0:T(4,128)S(1)}, f32[3,64,3,128]{3,2,1,0:T(4,128)S(1)}, u32[]{:S(2)}, u32[]{:S(2)}) %collective-permute-start.4) | collective-permute-done | bytes 294944 | tf_op jit(solution)/shard_map/ppermute | solution.py:30
  77.7 4.7 %collective-permute-done.5 = f32[3,64,3,128]{3,2,1,0:T(4,128)S(1)} collective-permute-done((f32[3,64,3,128]{3,2,1,0:T(4,128)S(1)}, f32[3,64,3,128]{3,2,1,0:T(4,128)S(1)}, u32[]{:S(2)}, u32[]{:S(2)}) %collective-permute-start.5) | collective-permute-done | bytes 294944 | tf_op jit(solution)/shard_map/ppermute | solution.py:27
  82.4 0.3 fusion.1
  82.8 1.4 %collective-permute-start.6 = (f32[3,3,16,128]{3,2,1,0:T(8,128)S(1)}, f32[3,3,16,128]{3,2,1,0:T(8,128)S(1)}, u32[]{:S(2)}, u32[]{:S(2)}) collective-permute-start(f32[3,3,16,128]{3,2,1,0:T(8,128)S(1)} %get-tuple-element.59), channel_id=1, source_target_pairs={{0,16},{16,0},{1,17},{17,1},{2,18},{18,2},{3,19},{19,3},{4,20},{20... | collective-permute-start | bytes 221192 | tf_op jit(solution)/shard_map/ppermute | solution.py:27
  84.2 0.7 collective-permute-start.7
  84.9 3.0 %collective-permute-done.6 = f32[3,3,16,128]{3,2,1,0:T(8,128)S(1)} collective-permute-done((f32[3,3,16,128]{3,2,1,0:T(8,128)S(1)}, f32[3,3,16,128]{3,2,1,0:T(8,128)S(1)}, u32[]{:S(2)}, u32[]{:S(2)}) %collective-permute-start.6) | collective-permute-done | bytes 73760 | tf_op jit(solution)/shard_map/ppermute | solution.py:27
  87.9 1.6 %collective-permute-done.7 = f32[3,3,16,128]{3,2,1,0:T(8,128)S(1)} collective-permute-done((f32[3,3,16,128]{3,2,1,0:T(8,128)S(1)}, f32[3,3,16,128]{3,2,1,0:T(8,128)S(1)}, u32[]{:S(2)}, u32[]{:S(2)}) %collective-permute-start.7) | collective-permute-done | bytes 73760 | tf_op jit(solution)/shard_map/ppermute | solution.py:30
  89.4 0.3 pad_maximum_fusion.2.lam
  89.7 0.0 copy-done.6
  89.8 0.0 copy-done.1
  89.8 0.0 copy-done.3
  89.8 30.2 %closure.1 = f32[3,64,8,128]{3,2,1,0:T(8,128)} custom-call(f32[3,70,16,128]{3,2,1,0:T(8,128)S(1)} %copy-done.3, f32[3,70,16,128]{3,2,1,0:T(8,128)S(1)} %pad_maximum_fusion.2.lam, bf16[10560,256]{1,0:T(8,128)(2,1)S(1)} %copy-done.1, f32[9,64,8,128]{3,2,1,0:T(8,128)S(1)} %get-tuple-element.56.grads, bf16[320,896]{1,0:T(8,128)(2,1)S(1)} %copy-done.6, ...), custom_call_target="tpu_custom_call" | custom-call | tf_op jit(solution)/shard_map/closure/pallas_call | solution.py:263
  (57 shorter events, 0.4 us)
Async XLA Ops:
  0.0 1.1 copy-start.4
  1.1 0.8 copy-start.12
  2.0 10.7 %copy-start.19 = (f32[3,64,8,128]{3,2,1,0:T(8,128)S(1)}, f32[3,64,8,128]{3,2,1,0:T(8,128)}, u32[]{:S(2)}) copy-start(f32[3,64,8,128]{3,2,1,0:T(8,128)} %param.14) | copy-start | bytes 2359300
  5.4 12.5 %copy-start.23 = (bf16[32,3,3,3,3]{0,4,3,2,1:T(4,128)(2,1)S(1)}, bf16[32,3,3,3,3]{0,4,3,2,1:T(4,128)(2,1)}, u32[]{:S(2)}) copy-start(bf16[32,3,3,3,3]{0,4,3,2,1:T(4,128)(2,1)} %param.16) | copy-start | bytes 15556
  5.4 12.5 %copy-start.22 = (bf16[6,32,3,3,3]{1,4,3,2,0:T(4,128)(2,1)S(1)}, bf16[6,32,3,3,3]{1,4,3,2,0:T(4,128)(2,1)}, u32[]{:S(2)}) copy-start(bf16[6,32,3,3,3]{1,4,3,2,0:T(4,128)(2,1)} %param.18) | copy-start | bytes 31108
  5.4 12.7 %copy-start.20 = (bf16[81,5120]{1,0:T(8,128)(2,1)S(1)}, bf16[81,5120]{1,0:T(8,128)(2,1)}, u32[]{:S(2)}) copy-start(bf16[81,5120]{1,0:T(8,128)(2,1)} %constant.72.clone) | copy-start | bytes 2488324
  5.4 34.0 %all-to-all-start = ((f32[32,2,3,8,128]{4,3,2,1,0:T(8,128)}), f32[32,2,3,8,128]{4,3,2,1,0:T(8,128)S(1)}, u32[]{:S(2)}, u32[]{:S(2)}) async-start(f32[32,2,3,8,128]{4,3,2,1,0:T(8,128)} %forward.1), calls=%async_computation | async-start | bytes 1572864 | tf_op jit(solution)/shard_map/all_to_all | solution.py:431
  13.6 17.0 %collective-permute-start = (f32[3,64,3,128]{3,2,1,0:T(4,128)}, f32[3,64,3,128]{3,2,1,0:T(4,128)}, u32[]{:S(2)}, u32[]{:S(2)}) collective-permute-start(f32[3,64,3,128]{3,2,1,0:T(4,128)} %get-tuple-element.65), channel_id=1, source_target_pairs={{1,0},{2,1},{3,2},{4,3},{5,4},{6,5},{7,6},{8,7},{9,8},{10,9},{11,1... | collective-permute-start | bytes 884744 | tf_op jit(solution)/shard_map/ppermute | solution.py:30
  17.9 17.5 %collective-permute-start.1 = (f32[3,64,3,128]{3,2,1,0:T(4,128)S(1)}, f32[3,64,3,128]{3,2,1,0:T(4,128)}, u32[]{:S(2)}, u32[]{:S(2)}) collective-permute-start(f32[3,64,3,128]{3,2,1,0:T(4,128)S(1)} %get-tuple-element.66), channel_id=1, source_target_pairs={{0,1},{1,2},{2,3},{3,4},{4,5},{5,6},{6,7},{7,8},{8,9},{9,10},{10,1... | collective-permute-start | bytes 884744 | tf_op jit(solution)/shard_map/ppermute | solution.py:27
  18.5 0.7 copy-start.13
  19.3 2.8 %copy-start.21 = (bf16[81,2560]{1,0:T(8,128)(2,1)S(1)}, bf16[81,2560]{1,0:T(8,128)(2,1)}, u32[]{:S(2)}) copy-start(bf16[81,2560]{1,0:T(8,128)(2,1)} %constant.74.clone) | copy-start | bytes 1244164
  21.9 0.7 copy-start.24
  23.0 14.3 %copy-start.5 = (bf16[320,896]{1,0:T(8,128)(2,1)}, bf16[320,896]{1,0:T(8,128)(2,1)S(1)}, u32[]{:S(2)}) copy-start(bf16[320,896]{1,0:T(8,128)(2,1)S(1)} %slice_dynamic-update-slice_fusion.w2) | copy-start | bytes 1720324
  35.4 1.9 %copy-start.17 = (f32[3,64,2,128]{3,2,1,0:T(2,128)}, f32[3,64,2,128]{3,2,1,0:T(2,128)S(1)}, u32[]{:S(2)}) copy-start(f32[3,64,2,128]{3,2,1,0:T(2,128)S(1)} %broadcast.158) | copy-start | bytes 589828
  35.5 4.0 %copy-start.7 = (bf16[2,256,512]{2,1,0:T(8,128)(2,1)S(1)}, bf16[2,256,512]{2,1,0:T(8,128)(2,1)}, u32[]{:S(2)}) copy-start(bf16[2,256,512]{2,1,0:T(8,128)(2,1)} %constant.77.clone.bx) | copy-start | bytes 1572868
  35.5 4.0 %copy-start.8 = (bf16[2,256,512]{2,1,0:T(8,128)(2,1)S(1)}, bf16[2,256,512]{2,1,0:T(8,128)(2,1)}, u32[]{:S(2)}) copy-start(bf16[2,256,512]{2,1,0:T(8,128)(2,1)} %constant.76.clone.fx) | copy-start | bytes 1572868
  35.5 4.0 %copy-start.9 = (bf16[2,256,256]{2,1,0:T(8,128)(2,1)S(1)}, bf16[2,256,256]{2,1,0:T(8,128)(2,1)}, u32[]{:S(2)}) copy-start(bf16[2,256,256]{2,1,0:T(8,128)(2,1)} %constant.78.clone.by) | copy-start | bytes 786436
  35.5 4.0 %copy-start.10 = (bf16[2,256,256]{2,1,0:T(8,128)(2,1)S(1)}, bf16[2,256,256]{2,1,0:T(8,128)(2,1)}, u32[]{:S(2)}) copy-start(bf16[2,256,256]{2,1,0:T(8,128)(2,1)} %constant.75.clone.fy) | copy-start | bytes 786436
  37.3 2.1 %copy-start.15 = (f32[3,64,16,128]{3,2,1,0:T(8,128)}, f32[3,64,16,128]{3,2,1,0:T(8,128)S(1)}, u32[]{:S(2)}) copy-start(f32[3,64,16,128]{3,2,1,0:T(8,128)S(1)} %fusion) | copy-start | bytes 4718596
  37.4 6.6 %collective-permute-start.3 = (f32[3,3,16,128]{3,2,1,0:T(8,128)S(1)}, f32[3,3,16,128]{3,2,1,0:T(8,128)S(1)}, u32[]{:S(2)}, u32[]{:S(2)}) collective-permute-start(f32[3,3,16,128]{3,2,1,0:T(8,128)S(1)} %get-tuple-element.61), channel_id=1, source_target_pairs={{16,0},{0,16},{17,1},{1,17},{18,2},{2,18},{19,3},{3,19},{20,4},{4,... | collective-permute-start | bytes 221192 | tf_op jit(solution)/shard_map/ppermute | solution.py:30
  38.9 5.1 %collective-permute-start.2 = (f32[3,3,16,128]{3,2,1,0:T(8,128)S(1)}, f32[3,3,16,128]{3,2,1,0:T(8,128)S(1)}, u32[]{:S(2)}, u32[]{:S(2)}) collective-permute-start(f32[3,3,16,128]{3,2,1,0:T(8,128)S(1)} %get-tuple-element.62), channel_id=1, source_target_pairs={{0,16},{16,0},{1,17},{17,1},{2,18},{18,2},{3,19},{19,3},{4,20},{20... | collective-permute-start | bytes 221192 | tf_op jit(solution)/shard_map/ppermute | solution.py:27
  44.0 5.2 %copy-start.16 = (f32[3,64,16,128]{3,2,1,0:T(8,128)S(1)}, f32[3,64,16,128]{3,2,1,0:T(8,128)}, u32[]{:S(2)}) copy-start(f32[3,64,16,128]{3,2,1,0:T(8,128)} %copy-done.15) | copy-start | bytes 4718596
  44.0 26.5 %all-to-all-start.1 = ((f32[32,2,3,8,128]{4,3,2,1,0:T(8,128)}), f32[32,2,3,8,128]{4,3,2,1,0:T(8,128)S(1)}, u32[]{:S(2)}, u32[]{:S(2)}) async-start(f32[32,2,3,8,128]{4,3,2,1,0:T(8,128)} %middle.1), calls=%async_computation.1 | async-start | bytes 1572864 | tf_op jit(solution)/shard_map/all_to_all | solution.py:462
  49.1 1.0 copy-start.14
  50.1 20.4 %copy-start.11 = (bf16[2,128,128]{2,1,0:T(8,128)(2,1)S(1)}, bf16[2,128,128]{2,1,0:T(8,128)(2,1)}, u32[]{:S(2)}) copy-start(bf16[2,128,128]{2,1,0:T(8,128)(2,1)} %constant.79.clone.table) | copy-start | bytes 196612
  59.6 2.4 %copy-start = (bf16[10560,256]{1,0:T(8,128)(2,1)}, bf16[10560,256]{1,0:T(8,128)(2,1)S(1)}, u32[]{:S(2)}) copy-start(bf16[10560,256]{1,0:T(8,128)(2,1)S(1)} %get-tuple-element.55.slope) | copy-start | bytes 16220164
  62.0 1.2 %copy-start.2 = (f32[3,70,16,128]{3,2,1,0:T(8,128)}, f32[3,70,16,128]{3,2,1,0:T(8,128)S(1)}, u32[]{:S(2)}) copy-start(f32[3,70,16,128]{3,2,1,0:T(8,128)S(1)} %constant_dynamic-update-slice_fusion.10.vel) | copy-start | bytes 5160964
  70.5 11.9 %copy-start.18 = (f32[3,64,2,128]{3,2,1,0:T(2,128)S(1)}, f32[3,64,2,128]{3,2,1,0:T(2,128)}, u32[]{:S(2)}) copy-start(f32[3,64,2,128]{3,2,1,0:T(2,128)} %copy-done.17) | copy-start | bytes 589828
  72.1 17.7 %copy-start.6 = (bf16[320,896]{1,0:T(8,128)(2,1)S(1)}, bf16[320,896]{1,0:T(8,128)(2,1)}, u32[]{:S(2)}) copy-start(bf16[320,896]{1,0:T(8,128)(2,1)} %copy-done.5) | copy-start | bytes 1720324
  72.2 5.5 %collective-permute-start.4 = (f32[3,64,3,128]{3,2,1,0:T(4,128)S(1)}, f32[3,64,3,128]{3,2,1,0:T(4,128)S(1)}, u32[]{:S(2)}, u32[]{:S(2)}) collective-permute-start(f32[3,64,3,128]{3,2,1,0:T(4,128)S(1)} %get-tuple-element.63), channel_id=1, source_target_pairs={{1,0},{2,1},{3,2},{4,3},{5,4},{6,5},{7,6},{8,7},{9,8},{10,9},{11,1... | collective-permute-start | bytes 884744 | tf_op jit(solution)/shard_map/ppermute | solution.py:30
  72.4 10.0 %collective-permute-start.5 = (f32[3,64,3,128]{3,2,1,0:T(4,128)S(1)}, f32[3,64,3,128]{3,2,1,0:T(4,128)S(1)}, u32[]{:S(2)}, u32[]{:S(2)}) collective-permute-start(f32[3,64,3,128]{3,2,1,0:T(4,128)S(1)} %get-tuple-element.64), channel_id=1, source_target_pairs={{0,1},{1,2},{2,3},{3,4},{4,5},{5,6},{6,7},{7,8},{8,9},{9,10},{10,1... | collective-permute-start | bytes 884744 | tf_op jit(solution)/shard_map/ppermute | solution.py:27
  82.4 7.3 %copy-start.1 = (bf16[10560,256]{1,0:T(8,128)(2,1)S(1)}, bf16[10560,256]{1,0:T(8,128)(2,1)}, u32[]{:S(2)}) copy-start(bf16[10560,256]{1,0:T(8,128)(2,1)} %copy-done) | copy-start | bytes 16220164
  82.8 5.1 %collective-permute-start.6 = (f32[3,3,16,128]{3,2,1,0:T(8,128)S(1)}, f32[3,3,16,128]{3,2,1,0:T(8,128)S(1)}, u32[]{:S(2)}, u32[]{:S(2)}) collective-permute-start(f32[3,3,16,128]{3,2,1,0:T(8,128)S(1)} %get-tuple-element.59), channel_id=1, source_target_pairs={{0,16},{16,0},{1,17},{17,1},{2,18},{18,2},{3,19},{19,3},{4,20},{20... | collective-permute-start | bytes 221192 | tf_op jit(solution)/shard_map/ppermute | solution.py:27
  84.2 5.6 %copy-start.3 = (f32[3,70,16,128]{3,2,1,0:T(8,128)S(1)}, f32[3,70,16,128]{3,2,1,0:T(8,128)}, u32[]{:S(2)}) copy-start(f32[3,70,16,128]{3,2,1,0:T(8,128)} %copy-done.2) | copy-start | bytes 5160964
  84.2 5.2 %collective-permute-start.7 = (f32[3,3,16,128]{3,2,1,0:T(8,128)S(1)}, f32[3,3,16,128]{3,2,1,0:T(8,128)S(1)}, u32[]{:S(2)}, u32[]{:S(2)}) collective-permute-start(f32[3,3,16,128]{3,2,1,0:T(8,128)S(1)} %get-tuple-element.60), channel_id=1, source_target_pairs={{16,0},{0,16},{17,1},{1,17},{18,2},{2,18},{19,3},{3,19},{20,4},{4,... | collective-permute-start | bytes 221192 | tf_op jit(solution)/shard_map/ppermute | solution.py:30

commit v5 on v4

--- a/solution.py
+++ b/solution.py
@@ -13,6 +13,7 @@
 time_step = 0.005
 high = lax.Precision.HIGH
 LANES = 128
+SIDES = 4
 taps = ((1, 45.0), (2, -9.0), (3, 1.0))
 
 
@@ -40,10 +41,19 @@
     return jnp.concatenate(parts + [low], axis=2)
 
 
+def joined(low, wide, up):
+    nx = wide.shape[1]
+    extra = max(0, -(-(nx + 2) // SIDES) * SIDES - nx - 2)
+    parts = [low, wide, up]
+    if extra:
+        parts.append(jnp.zeros(wide.shape[:1] + (extra,) + wide.shape[2:], wide.dtype))
+    return jnp.concatenate(parts, axis=1)
+
+
 def bordered(block):
     wide = widened(block, *halo(block, "py", 2, 3))
     low, up = halo(wide, "px", 1, 3)
-    return jnp.concatenate([low, wide, up], axis=1)
+    return joined(low, wide, up)
 
 
 def zroll(value, shift):
@@ -51,21 +61,21 @@
 
 
 def many(count, size, run):
-    if count % size:
-        size = 1
-
     @pl.loop(0, count // size)
     def _(block):
         for piece in range(size):
             run(block * size + piece)
 
+    for last in range(count - count % size, count):
+        run(last)
+
 
 def velocity_kernel(sizes, vel, w1, b1, slope, grads, vs):
     nx, ny, rows, half, spacings = sizes
     vblock, out_rows = 9 * rows, w1.shape[0]
 
     def prepare(k):
-        for side in range(2):
+        for side in range(SIDES):
             v = vel[:, k + 1 + side * half].reshape(3 * rows, LANES)
             for t in range(3):
                 start = pl.multiple_of(k * vblock + t * 3 * rows, 16)
@@ -73,7 +83,7 @@
                     v, 1 - t
                 ).astype(jnp.bfloat16)
 
-    many(half + 2, 5, prepare)
+    many(half + 2, 2, prepare)
 
     def step(i):
         pre = jnp.dot(
@@ -86,7 +96,7 @@
             jnp.bfloat16
         )
 
-    many(half, 3, step)
+    many(half, 2, step)
 
     def gradient(x):
         e = x + 3
@@ -113,7 +123,7 @@
     inv2 = [1.0 / (2.0 * h) for h in spacings]
 
     def prepare(k):
-        for side in range(2):
+        for side in range(SIDES):
             e = k + 1 + side * half
             lanes = slice(side * LANES, (side + 1) * LANES)
             l = [lam[c, e] for c in range(3)]
@@ -131,7 +141,7 @@
                 ss[pl.ds(start, 6 * rows), lanes] = zroll(s, 1 - t).astype(jnp.bfloat16)
         acc[k] = jnp.zeros(acc.shape[1:], acc.dtype)
 
-    many(half + 2, 5, prepare)
+    many(half + 2, 2, prepare)
 
     def step(i):
         hid = jnp.dot(
@@ -145,10 +155,10 @@
         for d in range(3):
             acc[i + d] += c[d * 9 * ny : (d + 1) * 9 * ny]
 
-    many(half, 3, step)
+    many(half, 2, step)
 
     for d in range(2):
-        acc[half + d, :, :LANES] += acc[d, :, LANES:]
+        acc[half + d, :, : (SIDES - 1) * LANES] += acc[d, :, LANES:]
 
     def finish(x, idx, side):
         e = x + 3
@@ -174,8 +184,17 @@
                 total -= l0[a] * grads[3 * c + a, x]
             out[c, x] = l0[c] + time_step * total
 
-    many(half, 3, lambda x: finish(x, x + 2, 0))
-    many(nx - half, 2, lambda x: finish(x + half, x + 2, 1))
+    shared = nx - (SIDES - 1) * half
+
+    @pl.loop(0, shared)
+    def _(x):
+        for side in range(SIDES):
+            finish(x + side * half, x + 2, side)
+
+    @pl.loop(shared, half)
+    def _(x):
+        for side in range(SIDES - 1):
+            finish(x + side * half, x + 2, side)
 
 
 def lane_padded(size):
@@ -235,22 +254,22 @@
 
 def velocity_step(vel_ext, w1, bias, nx, ny, spacings):
     rows = vel_ext.shape[2]
-    half = (nx + 2) // 2
+    half = -(-(nx + 2) // SIDES)
     vm = pl.BlockSpec(memory_space=pltpu.VMEM)
     return pl.pallas_call(
         functools.partial(velocity_kernel, (nx, ny, rows, half, spacings)),
         out_shape=(
-            jax.ShapeDtypeStruct((half * w1.shape[0], 2 * LANES), jnp.bfloat16),
+            jax.ShapeDtypeStruct((half * w1.shape[0], SIDES * LANES), jnp.bfloat16),
             jax.ShapeDtypeStruct((9, nx, ny, LANES), jnp.float32),
         ),
         in_specs=[vm] * 3,
         out_specs=(vm, vm),
-        scratch_shapes=[pltpu.VMEM(((half + 2) * 9 * rows, 2 * LANES), jnp.bfloat16)],
+        scratch_shapes=[pltpu.VMEM(((half + 2) * 9 * rows, SIDES * LANES), jnp.bfloat16)],
         compiler_params=pltpu.CompilerParams(vmem_limit_bytes=20 * 2**20),
         cost_estimate=pl.CostEstimate(
-            flops=2 * half * w1.shape[0] * w1.shape[1] * 2 * LANES,
+            flops=2 * half * w1.shape[0] * w1.shape[1] * SIDES * LANES,
             bytes_accessed=12 * 2**20,
-            transcendentals=half * w1.shape[0] * 2 * LANES,
+            transcendentals=half * w1.shape[0] * SIDES * LANES,
         ),
         name="velocity",
     )(vel_ext, w1, bias)
@@ -258,7 +277,7 @@
 
 def closure_step(vel_ext, lam_ext, slope, grads, w2, w3, nx, ny, spacings):
     rows = vel_ext.shape[2]
-    half = (nx + 2) // 2
+    half = -(-(nx + 2) // SIDES)
     vm = pl.BlockSpec(memory_space=pltpu.VMEM)
     return pl.pallas_call(
         functools.partial(closure_kernel, (nx, ny, rows, half, spacings)),
@@ -266,8 +285,8 @@
         in_specs=[vm] * 6,
         out_specs=vm,
         scratch_shapes=[
-            pltpu.VMEM(((half + 2) * 18 * rows, 2 * LANES), jnp.bfloat16),
-            pltpu.VMEM((half + 2, 9 * ny, 2 * LANES), jnp.float32),
+            pltpu.VMEM(((half + 2) * 18 * rows, SIDES * LANES), jnp.bfloat16),
+            pltpu.VMEM((half + 2, 9 * ny, SIDES * LANES), jnp.float32),
         ],
         compiler_params=pltpu.CompilerParams(vmem_limit_bytes=28 * 2**20),
         name="closure",
@@ -535,7 +554,7 @@
     def beside_second(first, halo_first):
         w1, bias, w2, w3, wide = first
         low, up = halo_first
-        vel_ext = jnp.concatenate([low, wide, up], axis=1)
+        vel_ext = joined(low, wide, up)
         slope, grads = velocity_step(vel_ext, w1, bias, nx, ny, spacings)
         return vel_ext, slope, grads, w2, w3
 

time: 120 us -> 114 us (0.950)
  Pallas kernels: 49.1 us -> 39.4 us
  other arithmetic: 2.41 us -> 5.25 us
    pallas_call x1, Pallas kernels: 30.2 us -> 20.7 us  [closure_step(): pl.pallas_call(functools.partial(closure_kernel, (nx, ny, rows, half, spa...]
    slice x3, local copies, waits for them, and re-layouts: 1 us -> 2.69 us  [halo(): lax.slice_in_dim(block, 0, width, axis=dim)]
    concatenate x1 -> x2, other arithmetic: 0.3 us -> 1.95 us  [joined(): return jnp.concatenate(parts, axis=1)]
    unnamed x70 -> x62, local copies, waits for them, and re-layouts: 7.52 us -> 6.88 us
  transfers between devices with their start and end apart: 10 -> 10, of which waited for: 7 -> 7; matrix products, arithmetic and copies ran while one was open for 6% -> 10% of each run, Pallas kernels for 12% -> 12%
where the time goes in v5:
time: 114 us; the launch traced here: 113 us
  Pallas kernels  39.4 us (35%)
  waiting for transfers between devices  33 us (29%)
  starting transfers between devices  21.3 us (19%)
  local copies, waits for them, and re-layouts  10.4 us (9%)
  other arithmetic  5.25 us (5%)
  matrix products  3.37 us (3%)
    pallas_call x1, Pallas kernels, closure_step(): pl.pallas_call(functools.partial(closure_kernel, (nx, ny, rows, half, spa...  20.7 us
    ppermute x4, waiting for transfers between devices, halo(): lax.ppermute(lax.slice_in_dim(block, 0, width, axis=dim), axis, backward)  13.9 us
    ppermute x4, waiting for transfers between devices, halo(): lax.ppermute(lax.slice_in_dim(block, block.shape[dim] - width, None, axis...  12.7 us
    all_to_all x2, starting transfers between devices, projected_once(): got = lax.all_to_all(sent, ('px', 'py'), 0, 0, tiled=True)  12.3 us
    pallas_call x3, Pallas kernels, local_call(): pl.pallas_call(kernel, out_shape=jax.ShapeDtypeStruct(shape, jnp.float32)...  9.43 us
    pallas_call x1, Pallas kernels, velocity_step(): pl.pallas_call(functools.partial(velocity_kernel, (nx, ny, rows, half, sp...  9.28 us
    unnamed x62, local copies, waits for them, and re-layouts  6.88 us
    ppermute x4, starting transfers between devices, halo(): lax.ppermute(lax.slice_in_dim(block, 0, width, axis=dim), axis, backward)  6.75 us
  transfers between devices with their start and end apart: 10, of which 7 were waited for; matrix products, arithmetic and copies ran while one was open for 10% of the time, Pallas kernels for 12%

profile of v5, /device:TPU:0, one launch (start us, length us, event | category | flops | bytes accessed | tf_op | source)
XLA Modules:
  0.0 113.2 jit_solution(6254380933851919573)
XLA Ops:
  0.0 1.1 copy-done.4
  1.1 0.8 copy-done.10
  2.0 3.4 %forward.1 = f32[32,2,3,8,128]{4,3,2,1,0:T(8,128)} custom-call(f32[3,64,8,128]{3,2,1,0:T(8,128)S(1)} %copy-done.4, bf16[2,128,128]{2,1,0:T(8,128)(2,1)S(1)} %copy-done.10), custom_call_target="tpu_custom_call" | custom-call | tf_op jit(solution)/shard_map/forward/pallas_call | solution.py:421
  5.4 7.3 %all-to-all-start = ((f32[32,2,3,8,128]{4,3,2,1,0:T(8,128)}), f32[32,2,3,8,128]{4,3,2,1,0:T(8,128)S(1)}, u32[]{:S(2)}, u32[]{:S(2)}) async-start(f32[32,2,3,8,128]{4,3,2,1,0:T(8,128)} %forward.1), calls=%async_computation | async-start | bytes 1572864 | tf_op jit(solution)/shard_map/all_to_all | solution.py:450
  12.7 0.0 copy-done.13
  12.7 1.0 fusion.8
  13.7 4.3 %collective-permute-start = (f32[3,64,3,128]{3,2,1,0:T(4,128)}, f32[3,64,3,128]{3,2,1,0:T(4,128)}, u32[]{:S(2)}, u32[]{:S(2)}) collective-permute-start(f32[3,64,3,128]{3,2,1,0:T(4,128)} %get-tuple-element.65), channel_id=1, source_target_pairs={{1,0},{2,1},{3,2},{4,3},{5,4},{6,5},{7,6},{8,7},{9,8},{10,9},{11,1... | collective-permute-start | bytes 884744 | tf_op jit(solution)/shard_map/ppermute | solution.py:31
  18.0 0.0 collective-permute-start.1
  18.0 0.0 copy-done.20
  18.1 0.0 copy-done.19
  18.1 0.1 rev.4
  18.2 0.3 convolution_convert_fusion.1
  18.7 0.7 copy-done.11
  19.4 2.7 %convolution_convert_fusion = bf16[32,8960]{1,0:T(8,128)(2,1)S(1)} fusion(bf16[32,162]{0,1:T(8,128)(2,1)S(1)} %reshape.90, bf16[162,8960]{1,0:T(8,128)(2,1)} %constant.74.clone), kind=kOutput, calls=%fused_computation | convolution fusion | flops 93184000 | bytes 3486848 | tf_op jit(solution)/shard_map/dot_general | solution.py:232
  22.2 0.0 copy-done.17
  22.2 0.4 convolution_convert_fusion.2
  22.7 0.1 copy-done.21
  22.8 0.1 broadcast_in_dim_tile.3
  22.9 0.2 concatenate.23
  23.2 7.3 %collective-permute-done = f32[3,64,3,128]{3,2,1,0:T(4,128)} collective-permute-done((f32[3,64,3,128]{3,2,1,0:T(4,128)}, f32[3,64,3,128]{3,2,1,0:T(4,128)}, u32[]{:S(2)}, u32[]{:S(2)}) %collective-permute-start) | collective-permute-done | bytes 294944 | tf_op jit(solution)/shard_map/ppermute | solution.py:31
  30.5 4.8 %collective-permute-done.1 = f32[3,64,3,128]{3,2,1,0:T(4,128)} collective-permute-done((f32[3,64,3,128]{3,2,1,0:T(4,128)}, f32[3,64,3,128]{3,2,1,0:T(4,128)}, u32[]{:S(2)}, u32[]{:S(2)}) %collective-permute-start.1) | collective-permute-done | bytes 294944 | tf_op jit(solution)/shard_map/ppermute | solution.py:28
  35.4 0.1 broadcast.161
  35.5 0.0 copy-start.5
  35.5 0.0 copy-start.6
  35.5 0.0 copy-start.7
  35.5 0.0 copy-start.8
  35.5 3.0 %fusion = f32[3,64,16,128]{3,2,1,0:T(8,128)} fusion(f32[3,64,2,128]{3,2,1,0:T(2,128)S(1)} %broadcast.161, f32[3,64,3,128]{3,2,1,0:T(4,128)} %collective-permute-done.1, f32[3,64,3,128]{3,2,1,0:T(4,128)} %collective-permute-done, f32[3,64,8,128]{3,2,1,0:T(8,128)} %param.14), kind=kLoop, calls=%fused_computation.7 | loop fusion | flops 1179648 | bytes 3145728 | tf_op jit(solution)/shard_map/concatenate | solution.py:41
  38.5 1.6 %fusion.6 = (f32[3,3,16,128]{3,2,1,0:T(8,128)}, f32[3,3,16,128]{3,2,1,0:T(8,128)S(1)}) fusion(f32[3,64,16,128]{3,2,1,0:T(8,128)} %fusion), kind=kLoop, calls=%fused_computation.41 | loop fusion | bytes 294912 | tf_op jit(solution)/shard_map/slice | solution.py:31
  40.0 0.0 copy-done.14
  40.0 1.5 %collective-permute-start.3 = (f32[3,3,16,128]{3,2,1,0:T(8,128)}, f32[3,3,16,128]{3,2,1,0:T(8,128)S(1)}, u32[]{:S(2)}, u32[]{:S(2)}) collective-permute-start(f32[3,3,16,128]{3,2,1,0:T(8,128)} %get-tuple-element.61), channel_id=1, source_target_pairs={{16,0},{0,16},{17,1},{1,17},{18,2},{2,18},{19,3},{3,19},{20,4},{4,... | collective-permute-start | bytes 221192 | tf_op jit(solution)/shard_map/ppermute | solution.py:31
  41.5 0.5 collective-permute-start.2
  42.1 0.0 all-to-all-done.got
  42.1 0.0 copy-done.5
  42.1 0.0 copy-done.6
  42.1 0.0 copy-done.7
  42.1 0.0 copy-done.8
  42.1 4.5 %middle.1 = f32[32,2,3,8,128]{4,3,2,1,0:T(8,128)} custom-call(f32[32,2,3,8,128]{4,3,2,1,0:T(8,128)S(1)} %all-to-all-done.got, f32[3,256]{1,0:T(4,128)S(1)} %pad_maximum_fusion.2.lanes, bf16[2,256,256]{2,1,0:T(8,128)(2,1)S(1)} %copy-done.8, bf16[2,256,512]{2,1,0:T(8,128)(2,1)S(1)} %copy-done.6, bf16[2,256,512]{2,1,0:T(8,128)(2,1)S(1)} %copy-done.5, ...), custom_call_target="tpu_custom_call" | custom-call | tf_op jit(solution)/shard_map/middle/pallas_call | solution.py:421
  46.6 0.0 collective-permute-done.3
  46.6 0.0 collective-permute-done.2
  46.6 5.0 %all-to-all-start.1 = ((f32[32,2,3,8,128]{4,3,2,1,0:T(8,128)}), f32[32,2,3,8,128]{4,3,2,1,0:T(8,128)S(1)}, u32[]{:S(2)}, u32[]{:S(2)}) async-start(f32[32,2,3,8,128]{4,3,2,1,0:T(8,128)} %middle.1), calls=%async_computation.1 | async-start | bytes 1572864 | tf_op jit(solution)/shard_map/all_to_all | solution.py:481
  51.6 0.1 pad.14.clone
  51.7 0.1 copy.17.b1
  51.8 0.0 copy-start.12
  51.8 1.6 %maximum_maximum_fusion.vel = f32[3,72,16,128]{3,2,1,0:T(8,128)S(1)} fusion(f32[3,3,16,128]{3,2,1,0:T(8,128)S(1)} %collective-permute-done.3, f32[3,64,16,128]{3,2,1,0:T(8,128)} %fusion, f32[3,3,16,128]{3,2,1,0:T(8,128)} %copy-done.18, f32[72]{0:T(128)S(1)} %pad.14.clone), kind=kLoop, calls=%fused_computation.5 | loop fusion | flops 1327104 | bytes 3490080 | tf_op jit(solution)/shard_map/concatenate | solution.py:50
  53.5 0.0 copy-start.9
  53.5 9.3 %velocity.1 = (bf16[5440,512]{1,0:T(8,128)(2,1)S(1)}, f32[9,64,8,128]{3,2,1,0:T(8,128)S(1)}) custom-call(f32[3,72,16,128]{3,2,1,0:T(8,128)S(1)} %maximum_maximum_fusion.vel, bf16[320,512]{1,0:T(8,128)(2,1)S(1)} %copy-done.12, f32[320,1]{1,0:T(8,128)S(1)} %copy.17.b1), custom_call_target="tpu_custom_call" | custom-call | flops 2852126720 | bytes 12582912 | tf_op jit(solution)/shard_map/velocity/pallas_call | solution.py:259
  62.8 2.4 %copy-done = bf16[5440,512]{1,0:T(8,128)(2,1)} copy-done((bf16[5440,512]{1,0:T(8,128)(2,1)}, bf16[5440,512]{1,0:T(8,128)(2,1)S(1)}, u32[]{:S(2)}) %copy-start) | copy-done | bytes 5570584
  65.2 1.4 %copy-done.2 = f32[9,64,8,128]{3,2,1,0:T(8,128)} copy-done((f32[9,64,8,128]{3,2,1,0:T(8,128)}, f32[9,64,8,128]{3,2,1,0:T(8,128)S(1)}, u32[]{:S(2)}) %copy-start.2) | copy-done | bytes 2359320
  66.7 6.5 %all-to-all-done.1.got = f32[32,2,3,8,128]{4,3,2,1,0:T(8,128)S(1)} async-done(((f32[32,2,3,8,128]{4,3,2,1,0:T(8,128)}), f32[32,2,3,8,128]{4,3,2,1,0:T(8,128)S(1)}, u32[]{:S(2)}, u32[]{:S(2)}) %all-to-all-start.1) | async-done | bytes 786464 | tf_op jit(solution)/shard_map/all_to_all | solution.py:481
  73.1 1.5 %backward.1 = f32[3,64,8,128]{3,2,1,0:T(8,128)S(1)} custom-call(f32[32,2,3,8,128]{4,3,2,1,0:T(8,128)S(1)} %all-to-all-done.1.got, bf16[2,128,128]{2,1,0:T(8,128)(2,1)S(1)} %copy-done.9), custom_call_target="tpu_custom_call" | custom-call | tf_op jit(solution)/shard_map/backward/pallas_call | solution.py:421
  74.7 0.1 fusion.7
  74.8 0.2 collective-permute-start.4
  75.1 0.3 collective-permute-start.5
  75.4 5.0 %collective-permute-done.4 = f32[3,64,3,128]{3,2,1,0:T(4,128)S(1)} collective-permute-done((f32[3,64,3,128]{3,2,1,0:T(4,128)S(1)}, f32[3,64,3,128]{3,2,1,0:T(4,128)S(1)}, u32[]{:S(2)}, u32[]{:S(2)}) %collective-permute-start.4) | collective-permute-done | bytes 294944 | tf_op jit(solution)/shard_map/ppermute | solution.py:31
  80.3 4.8 %collective-permute-done.5 = f32[3,64,3,128]{3,2,1,0:T(4,128)S(1)} collective-permute-done((f32[3,64,3,128]{3,2,1,0:T(4,128)S(1)}, f32[3,64,3,128]{3,2,1,0:T(4,128)S(1)}, u32[]{:S(2)}, u32[]{:S(2)}) %collective-permute-start.5) | collective-permute-done | bytes 294944 | tf_op jit(solution)/shard_map/ppermute | solution.py:28
  85.1 0.3 fusion.1
  85.5 1.4 %collective-permute-start.6 = (f32[3,3,16,128]{3,2,1,0:T(8,128)S(1)}, f32[3,3,16,128]{3,2,1,0:T(8,128)S(1)}, u32[]{:S(2)}, u32[]{:S(2)}) collective-permute-start(f32[3,3,16,128]{3,2,1,0:T(8,128)S(1)} %get-tuple-element.59), channel_id=1, source_target_pairs={{0,16},{16,0},{1,17},{17,1},{2,18},{18,2},{3,19},{19,3},{4,20},{20... | collective-permute-start | bytes 221192 | tf_op jit(solution)/shard_map/ppermute | solution.py:28
  86.8 0.7 collective-permute-start.7
  87.5 3.1 %collective-permute-done.6 = f32[3,3,16,128]{3,2,1,0:T(8,128)S(1)} collective-permute-done((f32[3,3,16,128]{3,2,1,0:T(8,128)S(1)}, f32[3,3,16,128]{3,2,1,0:T(8,128)S(1)}, u32[]{:S(2)}, u32[]{:S(2)}) %collective-permute-start.6) | collective-permute-done | bytes 73760 | tf_op jit(solution)/shard_map/ppermute | solution.py:28
  90.6 1.6 %collective-permute-done.7 = f32[3,3,16,128]{3,2,1,0:T(8,128)S(1)} collective-permute-done((f32[3,3,16,128]{3,2,1,0:T(8,128)S(1)}, f32[3,3,16,128]{3,2,1,0:T(8,128)S(1)}, u32[]{:S(2)}, u32[]{:S(2)}) %collective-permute-start.7) | collective-permute-done | bytes 73760 | tf_op jit(solution)/shard_map/ppermute | solution.py:31
  92.2 0.3 maximum_maximum_fusion.1.lam
  92.5 0.0 copy-done.3
  92.5 0.0 copy-done.1
  92.5 20.7 %closure.1 = f32[3,64,8,128]{3,2,1,0:T(8,128)} custom-call(f32[3,72,16,128]{3,2,1,0:T(8,128)S(1)} %maximum_maximum_fusion.vel, f32[3,72,16,128]{3,2,1,0:T(8,128)S(1)} %maximum_maximum_fusion.1.lam, bf16[5440,512]{1,0:T(8,128)(2,1)S(1)} %copy-done.1, f32[9,64,8,128]{3,2,1,0:T(8,128)S(1)} %copy-done.3, bf16[320,896]{1,0:T(8,128)(2,1)S(1)} %slice_dynamic-update-slice_fusion.w2, ...), custom_call_target="tpu_custom_call" | custom-call | tf_op jit(solution)/shard_map/closure/pallas_call | solution.py:282
  (51 shorter events, 0.4 us)
Async XLA Ops:
  0.0 1.1 %copy-start.4 = (f32[3,64,8,128]{3,2,1,0:T(8,128)S(1)}, f32[3,64,8,128]{3,2,1,0:T(8,128)}, u32[]{:S(2)}) copy-start(f32[3,64,8,128]{3,2,1,0:T(8,128)} %cot.1) | copy-start | bytes 2359300
  1.1 0.8 copy-start.10
  2.0 10.7 %copy-start.13 = (f32[3,64,8,128]{3,2,1,0:T(8,128)S(1)}, f32[3,64,8,128]{3,2,1,0:T(8,128)}, u32[]{:S(2)}) copy-start(f32[3,64,8,128]{3,2,1,0:T(8,128)} %param.14) | copy-start | bytes 2359300
  5.4 12.6 %copy-start.20 = (bf16[32,3,3,3,3]{0,4,3,2,1:T(4,128)(2,1)S(1)}, bf16[32,3,3,3,3]{0,4,3,2,1:T(4,128)(2,1)}, u32[]{:S(2)}) copy-start(bf16[32,3,3,3,3]{0,4,3,2,1:T(4,128)(2,1)} %param.16) | copy-start | bytes 15556
  5.4 12.7 %copy-start.19 = (bf16[6,32,3,3,3]{1,4,3,2,0:T(4,128)(2,1)S(1)}, bf16[6,32,3,3,3]{1,4,3,2,0:T(4,128)(2,1)}, u32[]{:S(2)}) copy-start(bf16[6,32,3,3,3]{1,4,3,2,0:T(4,128)(2,1)} %param.18) | copy-start | bytes 31108
  5.4 12.8 %copy-start.16 = (bf16[81,5120]{1,0:T(8,128)(2,1)S(1)}, bf16[81,5120]{1,0:T(8,128)(2,1)}, u32[]{:S(2)}) copy-start(bf16[81,5120]{1,0:T(8,128)(2,1)} %constant.73.clone) | copy-start | bytes 2488324
  5.4 36.7 %all-to-all-start = ((f32[32,2,3,8,128]{4,3,2,1,0:T(8,128)}), f32[32,2,3,8,128]{4,3,2,1,0:T(8,128)S(1)}, u32[]{:S(2)}, u32[]{:S(2)}) async-start(f32[32,2,3,8,128]{4,3,2,1,0:T(8,128)} %forward.1), calls=%async_computation | async-start | bytes 1572864 | tf_op jit(solution)/shard_map/all_to_all | solution.py:450
  13.7 16.8 %collective-permute-start = (f32[3,64,3,128]{3,2,1,0:T(4,128)}, f32[3,64,3,128]{3,2,1,0:T(4,128)}, u32[]{:S(2)}, u32[]{:S(2)}) collective-permute-start(f32[3,64,3,128]{3,2,1,0:T(4,128)} %get-tuple-element.65), channel_id=1, source_target_pairs={{1,0},{2,1},{3,2},{4,3},{5,4},{6,5},{7,6},{8,7},{9,8},{10,9},{11,1... | collective-permute-start | bytes 884744 | tf_op jit(solution)/shard_map/ppermute | solution.py:31
  18.0 17.4 %collective-permute-start.1 = (f32[3,64,3,128]{3,2,1,0:T(4,128)}, f32[3,64,3,128]{3,2,1,0:T(4,128)}, u32[]{:S(2)}, u32[]{:S(2)}) collective-permute-start(f32[3,64,3,128]{3,2,1,0:T(4,128)} %get-tuple-element.66), channel_id=1, source_target_pairs={{0,1},{1,2},{2,3},{3,4},{4,5},{5,6},{6,7},{7,8},{8,9},{9,10},{10,1... | collective-permute-start | bytes 884744 | tf_op jit(solution)/shard_map/ppermute | solution.py:28
  18.7 0.8 copy-start.11
  19.4 2.8 %copy-start.17 = (bf16[81,2560]{1,0:T(8,128)(2,1)S(1)}, bf16[81,2560]{1,0:T(8,128)(2,1)}, u32[]{:S(2)}) copy-start(bf16[81,2560]{1,0:T(8,128)(2,1)} %constant.75.clone) | copy-start | bytes 1244164
  22.1 0.7 copy-start.21
  35.5 4.6 %copy-start.14 = (f32[3,64,2,128]{3,2,1,0:T(2,128)}, f32[3,64,2,128]{3,2,1,0:T(2,128)S(1)}, u32[]{:S(2)}) copy-start(f32[3,64,2,128]{3,2,1,0:T(2,128)S(1)} %broadcast.161) | copy-start | bytes 589828
  35.5 6.6 %copy-start.5 = (bf16[2,256,512]{2,1,0:T(8,128)(2,1)S(1)}, bf16[2,256,512]{2,1,0:T(8,128)(2,1)}, u32[]{:S(2)}) copy-start(bf16[2,256,512]{2,1,0:T(8,128)(2,1)} %constant.78.clone.bx) | copy-start | bytes 1572868
  35.5 6.6 %copy-start.6 = (bf16[2,256,512]{2,1,0:T(8,128)(2,1)S(1)}, bf16[2,256,512]{2,1,0:T(8,128)(2,1)}, u32[]{:S(2)}) copy-start(bf16[2,256,512]{2,1,0:T(8,128)(2,1)} %constant.77.clone.fx) | copy-start | bytes 1572868
  35.5 6.6 %copy-start.7 = (bf16[2,256,256]{2,1,0:T(8,128)(2,1)S(1)}, bf16[2,256,256]{2,1,0:T(8,128)(2,1)}, u32[]{:S(2)}) copy-start(bf16[2,256,256]{2,1,0:T(8,128)(2,1)} %constant.79.clone.by) | copy-start | bytes 786436
  35.5 6.6 %copy-start.8 = (bf16[2,256,256]{2,1,0:T(8,128)(2,1)S(1)}, bf16[2,256,256]{2,1,0:T(8,128)(2,1)}, u32[]{:S(2)}) copy-start(bf16[2,256,256]{2,1,0:T(8,128)(2,1)} %constant.76.clone.fy) | copy-start | bytes 786436
  40.0 6.5 %collective-permute-start.3 = (f32[3,3,16,128]{3,2,1,0:T(8,128)}, f32[3,3,16,128]{3,2,1,0:T(8,128)S(1)}, u32[]{:S(2)}, u32[]{:S(2)}) collective-permute-start(f32[3,3,16,128]{3,2,1,0:T(8,128)} %get-tuple-element.61), channel_id=1, source_target_pairs={{16,0},{0,16},{17,1},{1,17},{18,2},{2,18},{19,3},{3,19},{20,4},{4,... | collective-permute-start | bytes 221192 | tf_op jit(solution)/shard_map/ppermute | solution.py:31
  41.5 5.0 %collective-permute-start.2 = (f32[3,3,16,128]{3,2,1,0:T(8,128)S(1)}, f32[3,3,16,128]{3,2,1,0:T(8,128)S(1)}, u32[]{:S(2)}, u32[]{:S(2)}) collective-permute-start(f32[3,3,16,128]{3,2,1,0:T(8,128)S(1)} %get-tuple-element.62), channel_id=1, source_target_pairs={{0,16},{16,0},{1,17},{17,1},{2,18},{18,2},{3,19},{19,3},{4,20},{20... | collective-permute-start | bytes 221192 | tf_op jit(solution)/shard_map/ppermute | solution.py:28
  46.6 5.0 %copy-start.18 = (f32[3,3,16,128]{3,2,1,0:T(8,128)}, f32[3,3,16,128]{3,2,1,0:T(8,128)S(1)}, u32[]{:S(2)}) copy-start(f32[3,3,16,128]{3,2,1,0:T(8,128)S(1)} %collective-permute-done.2) | copy-start | bytes 221188
  46.6 26.5 %all-to-all-start.1 = ((f32[32,2,3,8,128]{4,3,2,1,0:T(8,128)}), f32[32,2,3,8,128]{4,3,2,1,0:T(8,128)S(1)}, u32[]{:S(2)}, u32[]{:S(2)}) async-start(f32[32,2,3,8,128]{4,3,2,1,0:T(8,128)} %middle.1), calls=%async_computation.1 | async-start | bytes 1572864 | tf_op jit(solution)/shard_map/all_to_all | solution.py:481
  51.8 1.7 %copy-start.12 = (bf16[320,512]{1,0:T(8,128)(2,1)S(1)}, bf16[320,512]{1,0:T(8,128)(2,1)}, u32[]{:S(2)}) copy-start(bf16[320,512]{1,0:T(8,128)(2,1)} %copy-done.11) | copy-start | bytes 983044
  53.5 19.6 %copy-start.9 = (bf16[2,128,128]{2,1,0:T(8,128)(2,1)S(1)}, bf16[2,128,128]{2,1,0:T(8,128)(2,1)}, u32[]{:S(2)}) copy-start(bf16[2,128,128]{2,1,0:T(8,128)(2,1)} %constant.80.clone.table) | copy-start | bytes 196612
  62.8 2.4 %copy-start = (bf16[5440,512]{1,0:T(8,128)(2,1)}, bf16[5440,512]{1,0:T(8,128)(2,1)S(1)}, u32[]{:S(2)}) copy-start(bf16[5440,512]{1,0:T(8,128)(2,1)S(1)} %get-tuple-element.55.slope) | copy-start | bytes 16711684
  65.2 1.4 %copy-start.2 = (f32[9,64,8,128]{3,2,1,0:T(8,128)}, f32[9,64,8,128]{3,2,1,0:T(8,128)S(1)}, u32[]{:S(2)}) copy-start(f32[9,64,8,128]{3,2,1,0:T(8,128)S(1)} %get-tuple-element.56.grads) | copy-start | bytes 7077892
  73.1 12.0 %copy-start.15 = (f32[3,64,2,128]{3,2,1,0:T(2,128)S(1)}, f32[3,64,2,128]{3,2,1,0:T(2,128)}, u32[]{:S(2)}) copy-start(f32[3,64,2,128]{3,2,1,0:T(2,128)} %copy-done.14) | copy-start | bytes 589828
  74.7 17.8 %copy-start.3 = (f32[9,64,8,128]{3,2,1,0:T(8,128)S(1)}, f32[9,64,8,128]{3,2,1,0:T(8,128)}, u32[]{:S(2)}) copy-start(f32[9,64,8,128]{3,2,1,0:T(8,128)} %copy-done.2) | copy-start | bytes 7077892
  74.8 5.5 %collective-permute-start.4 = (f32[3,64,3,128]{3,2,1,0:T(4,128)S(1)}, f32[3,64,3,128]{3,2,1,0:T(4,128)S(1)}, u32[]{:S(2)}, u32[]{:S(2)}) collective-permute-start(f32[3,64,3,128]{3,2,1,0:T(4,128)S(1)} %get-tuple-element.63), channel_id=1, source_target_pairs={{1,0},{2,1},{3,2},{4,3},{5,4},{6,5},{7,6},{8,7},{9,8},{10,9},{11,1... | collective-permute-start | bytes 884744 | tf_op jit(solution)/shard_map/ppermute | solution.py:31
  75.1 10.1 %collective-permute-start.5 = (f32[3,64,3,128]{3,2,1,0:T(4,128)S(1)}, f32[3,64,3,128]{3,2,1,0:T(4,128)S(1)}, u32[]{:S(2)}, u32[]{:S(2)}) collective-permute-start(f32[3,64,3,128]{3,2,1,0:T(4,128)S(1)} %get-tuple-element.64), channel_id=1, source_target_pairs={{0,1},{1,2},{2,3},{3,4},{4,5},{5,6},{6,7},{7,8},{8,9},{9,10},{10,1... | collective-permute-start | bytes 884744 | tf_op jit(solution)/shard_map/ppermute | solution.py:28
  85.1 7.4 %copy-start.1 = (bf16[5440,512]{1,0:T(8,128)(2,1)S(1)}, bf16[5440,512]{1,0:T(8,128)(2,1)}, u32[]{:S(2)}) copy-start(bf16[5440,512]{1,0:T(8,128)(2,1)} %copy-done) | copy-start | bytes 16711684
  85.5 5.2 %collective-permute-start.6 = (f32[3,3,16,128]{3,2,1,0:T(8,128)S(1)}, f32[3,3,16,128]{3,2,1,0:T(8,128)S(1)}, u32[]{:S(2)}, u32[]{:S(2)}) collective-permute-start(f32[3,3,16,128]{3,2,1,0:T(8,128)S(1)} %get-tuple-element.59), channel_id=1, source_target_pairs={{0,16},{16,0},{1,17},{17,1},{2,18},{18,2},{3,19},{19,3},{4,20},{20... | collective-permute-start | bytes 221192 | tf_op jit(solution)/shard_map/ppermute | solution.py:28
  86.8 5.4 %collective-permute-start.7 = (f32[3,3,16,128]{3,2,1,0:T(8,128)S(1)}, f32[3,3,16,128]{3,2,1,0:T(8,128)S(1)}, u32[]{:S(2)}, u32[]{:S(2)}) collective-permute-start(f32[3,3,16,128]{3,2,1,0:T(8,128)S(1)} %get-tuple-element.60), channel_id=1, source_target_pairs={{16,0},{0,16},{17,1},{1,17},{18,2},{2,18},{19,3},{3,19},{20,4},{4,... | collective-permute-start | bytes 221192 | tf_op jit(solution)/shard_map/ppermute | solution.py:31

commit v6 on v5

--- a/solution.py
+++ b/solution.py
@@ -13,7 +13,7 @@
 time_step = 0.005
 high = lax.Precision.HIGH
 LANES = 128
-SIDES = 4
+SIDES = 6
 taps = ((1, 45.0), (2, -9.0), (3, 1.0))
 
 
@@ -548,12 +548,12 @@
     def beside_first(velocity, weight_in, bias_in, weight_out):
         w1, bias = input_weights(weight_in, bias_in, ny, rows)
         w2, w3 = output_weights(weight_in, weight_out, ny, rows)
-        wide = widened(velocity, *halo(velocity, "py", 2, 3))
-        return (w1, bias, w2, w3, wide), halo(wide, "px", 1, 3)
+        return (w1, bias, w2, w3), (velocity,) + halo(velocity, "py", 2, 3)
 
     def beside_second(first, halo_first):
-        w1, bias, w2, w3, wide = first
-        low, up = halo_first
+        w1, bias, w2, w3 = first
+        wide = widened(*halo_first)
+        low, up = halo(wide, "px", 1, 3)
         vel_ext = joined(low, wide, up)
         slope, grads = velocity_step(vel_ext, w1, bias, nx, ny, spacings)
         return vel_ext, slope, grads, w2, w3

time: 114 us -> 114 us (level)
  local copies, waits for them, and re-layouts: 10.4 us -> 18.5 us
  waiting for transfers between devices: 33 us -> 25.3 us
  Pallas kernels: 39.4 us -> 37.3 us
  starting transfers between devices: 21.3 us -> 23.4 us
  other arithmetic: 5.25 us -> 3.93 us
    unnamed x62, local copies, waits for them, and re-layouts: 6.88 us -> 14.1 us
    ppermute x4, waiting for transfers between devices: 13.9 us -> 9.16 us  [halo(): lax.ppermute(lax.slice_in_dim(block, 0, width, axis=dim), axis, backward)]
    ppermute x4, starting transfers between devices: 6.75 us -> 11.1 us  [halo(): lax.ppermute(lax.slice_in_dim(block, 0, width, axis=dim), axis, backward)]
    all_to_all x2, waiting for transfers between devices: 6.47 us -> 4.2 us  [projected_once(): got = lax.all_to_all(sent, ('px', 'py'), 0, 0, tiled=True)]
    all_to_all x2, starting transfers between devices: 12.3 us -> 10.1 us  [projected_once(): got = lax.all_to_all(sent, ('px', 'py'), 0, 0, tiled=True)]
    concatenate x3, local copies, waits for them, and re-layouts: 0.27 us -> 2.03 us  [spread(): jnp.concatenate([wide[:, p * columns:(p + 1) * columns] for p in range(ta...]
    slice x3 -> x2, local copies, waits for them, and re-layouts: 2.69 us -> 1.13 us  [halo(): lax.slice_in_dim(block, 0, width, axis=dim)]
    concatenate x2, other arithmetic: 3.27 us -> 1.78 us  [widened(): return jnp.concatenate(parts + [low], axis=2)]
  transfers between devices with their start and end apart: 10 -> 10, of which waited for: 7 -> 7; matrix products, arithmetic and copies ran while one was open for 10% -> 17% of each run, Pallas kernels for 12% -> 11%
where the time goes in v6:
time: 114 us; the launch traced here: 113 us
  Pallas kernels  37.3 us (33%)
  waiting for transfers between devices  25.3 us (22%)
  starting transfers between devices  23.4 us (21%)
  local copies, waits for them, and re-layouts  18.5 us (16%)
  matrix products  4.2 us (4%)
  other arithmetic  3.93 us (3%)
    pallas_call x1, Pallas kernels, closure_step(): pl.pallas_call(functools.partial(closure_kernel, (nx, ny, rows, half, spa...  19.4 us
    unnamed x62, local copies, waits for them, and re-layouts  14.1 us
    ppermute x4, waiting for transfers between devices, halo(): lax.ppermute(lax.slice_in_dim(block, block.shape[dim] - width, None, axis...  11.9 us
    ppermute x4, starting transfers between devices, halo(): lax.ppermute(lax.slice_in_dim(block, 0, width, axis=dim), axis, backward)  11.1 us
    all_to_all x2, starting transfers between devices, projected_once(): got = lax.all_to_all(sent, ('px', 'py'), 0, 0, tiled=True)  10.1 us
    pallas_call x3, Pallas kernels, local_call(): pl.pallas_call(kernel, out_shape=jax.ShapeDtypeStruct(shape, jnp.float32)...  9.43 us
    ppermute x4, waiting for transfers between devices, halo(): lax.ppermute(lax.slice_in_dim(block, 0, width, axis=dim), axis, backward)  9.16 us
    pallas_call x1, Pallas kernels, velocity_step(): pl.pallas_call(functools.partial(velocity_kernel, (nx, ny, rows, half, sp...  8.49 us
  transfers between devices with their start and end apart: 10, of which 7 were waited for; matrix products, arithmetic and copies ran while one was open for 17% of the time, Pallas kernels for 11%

profile of v6, /device:TPU:0, one launch (start us, length us, event | category | flops | bytes accessed | tf_op | source)
XLA Modules:
  0.0 113.1 jit_solution(7723061519640277515)
XLA Ops:
  0.0 1.1 %copy-done.4 = f32[3,64,8,128]{3,2,1,0:T(8,128)S(1)} copy-done((f32[3,64,8,128]{3,2,1,0:T(8,128)S(1)}, f32[3,64,8,128]{3,2,1,0:T(8,128)}, u32[]{:S(2)}) %copy-start.4) | copy-done | bytes 786456
  1.1 0.8 copy-done.10
  2.0 3.4 %forward.1 = f32[32,2,3,8,128]{4,3,2,1,0:T(8,128)} custom-call(f32[3,64,8,128]{3,2,1,0:T(8,128)S(1)} %copy-done.4, bf16[2,128,128]{2,1,0:T(8,128)(2,1)S(1)} %copy-done.10), custom_call_target="tpu_custom_call" | custom-call | tf_op jit(solution)/shard_map/forward/pallas_call | solution.py:421
  5.4 7.3 %all-to-all-start = ((f32[32,2,3,8,128]{4,3,2,1,0:T(8,128)}), f32[32,2,3,8,128]{4,3,2,1,0:T(8,128)S(1)}, u32[]{:S(2)}, u32[]{:S(2)}) async-start(f32[32,2,3,8,128]{4,3,2,1,0:T(8,128)} %forward.1), calls=%async_computation | async-start | bytes 1572864 | tf_op jit(solution)/shard_map/all_to_all | solution.py:450
  12.7 0.0 copy-done.13
  12.7 1.0 fusion.14
  13.7 4.3 %collective-permute-start.1 = (f32[3,64,3,128]{3,2,1,0:T(4,128)}, f32[3,64,3,128]{3,2,1,0:T(4,128)}, u32[]{:S(2)}, u32[]{:S(2)}) collective-permute-start(f32[3,64,3,128]{3,2,1,0:T(4,128)} %get-tuple-element.63), channel_id=1, source_target_pairs={{1,0},{2,1},{3,2},{4,3},{5,4},{6,5},{7,6},{8,7},{9,8},{10,9},{11,1... | collective-permute-start | bytes 884744 | tf_op jit(solution)/shard_map/ppermute | solution.py:31
  18.0 0.0 collective-permute-start
  18.0 0.0 copy-done.20
  18.1 0.0 copy-done.19
  18.1 0.1 rev.4
  18.3 0.3 convolution_convert_fusion.1
  18.7 0.0 copy-start.11
  18.7 0.7 copy-done.11
  19.4 3.5 %convolution_convert_fusion = bf16[32,8960]{1,0:T(8,128)(2,1)} fusion(bf16[32,162]{0,1:T(8,128)(2,1)S(1)} %reshape.90, bf16[162,8960]{1,0:T(8,128)(2,1)} %constant.73.clone), kind=kOutput, calls=%fused_computation | convolution fusion | flops 93184000 | bytes 3486848 | tf_op jit(solution)/shard_map/dot_general | solution.py:232
  22.9 0.8 slice_dynamic-update-slice_fusion.9
  23.8 0.8 slice_dynamic-update-slice_fusion.8
  24.6 0.8 slice_dynamic-update-slice_fusion.7
  25.4 0.8 slice_dynamic-update-slice_fusion.6
  26.3 0.4 convolution_convert_fusion.2
  26.7 0.0 copy-start.5
  26.7 0.0 copy-start.6
  26.7 0.0 copy-start.7
  26.7 0.0 copy-start.8
  26.7 0.7 fusion.15
  27.5 0.1 broadcast_in_dim_tile.3
  27.5 1.2 %concatenate.23 = bf16[320,256]{0,1:T(8,128)(2,1)S(1)} concatenate(bf16[32,256]{0,1:T(8,128)(2,1)} %get-tuple-element.74, bf16[32,256]{0,1:T(8,128)(2,1)} %get-tuple-element.73, bf16[32,256]{0,1:T(8,128)(2,1)} %get-tuple-element.72, bf16[32,256]{0,1:T(8,128)(2,1)} %get-tuple-element.71, bf16[32,256]{0,1:T(8,128)(2,1)} %get-tuple-element.70, ...), dimensions={0} | concatenate | bytes 327680 | tf_op jit(solution)/shard_map/concatenate | solution.py:236
  28.8 0.8 slice_dynamic-update-slice_fusion.5
  29.6 0.8 slice_dynamic-update-slice_fusion.4
  30.4 0.8 slice_dynamic-update-slice_fusion.3
  31.3 0.8 slice_dynamic-update-slice_fusion.2
  32.1 0.8 slice_dynamic-update-slice_fusion.1
  32.9 0.8 slice_dynamic-update-slice_fusion.w2
  33.8 4.2 %all-to-all-done.got = f32[32,2,3,8,128]{4,3,2,1,0:T(8,128)S(1)} async-done(((f32[32,2,3,8,128]{4,3,2,1,0:T(8,128)}), f32[32,2,3,8,128]{4,3,2,1,0:T(8,128)S(1)}, u32[]{:S(2)}, u32[]{:S(2)}) %all-to-all-start) | async-done | bytes 786464 | tf_op jit(solution)/shard_map/all_to_all | solution.py:450
  38.0 4.5 %middle.1 = f32[32,2,3,8,128]{4,3,2,1,0:T(8,128)} custom-call(f32[32,2,3,8,128]{4,3,2,1,0:T(8,128)S(1)} %all-to-all-done.got, f32[3,256]{1,0:T(4,128)S(1)} %pad_maximum_fusion.4.lanes, bf16[2,256,256]{2,1,0:T(8,128)(2,1)S(1)} %copy-done.8, bf16[2,256,512]{2,1,0:T(8,128)(2,1)S(1)} %copy-done.6, bf16[2,256,512]{2,1,0:T(8,128)(2,1)S(1)} %copy-done.5, ...), custom_call_target="tpu_custom_call" | custom-call | tf_op jit(solution)/shard_map/middle/pallas_call | solution.py:421
  42.5 0.0 collective-permute-done.1
  42.5 0.0 collective-permute-done
  42.5 2.8 %all-to-all-start.1 = ((f32[32,2,3,8,128]{4,3,2,1,0:T(8,128)}), f32[32,2,3,8,128]{4,3,2,1,0:T(8,128)S(1)}, u32[]{:S(2)}, u32[]{:S(2)}) async-start(f32[32,2,3,8,128]{4,3,2,1,0:T(8,128)} %middle.1), calls=%async_computation.1 | async-start | bytes 1572864 | tf_op jit(solution)/shard_map/all_to_all | solution.py:481
  45.2 0.1 broadcast.160
  45.3 1.5 %fusion.6 = f32[3,64,16,128]{3,2,1,0:T(8,128)S(1)} fusion(f32[3,64,2,128]{3,2,1,0:T(2,128)S(1)} %broadcast.160, f32[3,64,3,128]{3,2,1,0:T(4,128)} %collective-permute-done, f32[3,64,3,128]{3,2,1,0:T(4,128)} %collective-permute-done.1, f32[3,64,8,128]{3,2,1,0:T(8,128)S(1)} %copy-done.14), kind=kLoop, calls=%fused_computation.13 | loop fusion | flops 1179648 | bytes 3145728 | tf_op jit(solution)/shard_map/concatenate | solution.py:41
  46.8 1.7 %collective-permute-start.2 = (f32[3,3,16,128]{3,2,1,0:T(8,128)S(1)}, f32[3,3,16,128]{3,2,1,0:T(8,128)S(1)}, u32[]{:S(2)}, u32[]{:S(2)}) collective-permute-start(f32[3,3,16,128]{3,2,1,0:T(8,128)S(1)} %get-tuple-element.59), channel_id=1, source_target_pairs={{0,16},{16,0},{1,17},{17,1},{2,18},{18,2},{3,19},{19,3},{4,20},{20... | collective-permute-start | bytes 221192 | tf_op jit(solution)/shard_map/ppermute | solution.py:28
  48.6 0.4 collective-permute-start.3
  48.9 0.1 copy.17.b1
  49.1 5.0 %collective-permute-done.2 = f32[3,3,16,128]{3,2,1,0:T(8,128)S(1)} collective-permute-done((f32[3,3,16,128]{3,2,1,0:T(8,128)S(1)}, f32[3,3,16,128]{3,2,1,0:T(8,128)S(1)}, u32[]{:S(2)}, u32[]{:S(2)}) %collective-permute-start.2) | collective-permute-done | bytes 73760 | tf_op jit(solution)/shard_map/ppermute | solution.py:28
  54.1 3.1 %collective-permute-done.3 = f32[3,3,16,128]{3,2,1,0:T(8,128)} collective-permute-done((f32[3,3,16,128]{3,2,1,0:T(8,128)S(1)}, f32[3,3,16,128]{3,2,1,0:T(8,128)}, u32[]{:S(2)}, u32[]{:S(2)}) %collective-permute-start.3) | collective-permute-done | bytes 73760 | tf_op jit(solution)/shard_map/ppermute | solution.py:31
  57.1 1.8 %fusion.2.vel = f32[3,70,16,128]{3,2,1,0:T(8,128)S(1)} fusion(f32[3,64,2,128]{3,2,1,0:T(2,128)} %copy-done.15, f32[3,3,16,128]{3,2,1,0:T(8,128)} %collective-permute-done.3, f32[3,64,3,128]{3,2,1,0:T(4,128)} %collective-permute-done, f32[3,64,3,128]{3,2,1,0:T(4,128)} %collective-permute-done.1, f32[3,64,8,128]{3,2,1,0:T(8,128)} %param.14, ...), kind=kLoop, calls=%fused_computation.9 | loop fusion | flops 2150400 | bytes 3440640 | tf_op jit(solution)/shard_map/concatenate | solution.py:50
  59.0 0.0 copy-start.9
  59.0 8.5 %velocity.1 = (bf16[3520,768]{1,0:T(8,128)(2,1)S(1)}, f32[9,64,8,128]{3,2,1,0:T(8,128)S(1)}) custom-call(f32[3,70,16,128]{3,2,1,0:T(8,128)S(1)} %fusion.2.vel, bf16[320,512]{1,0:T(8,128)(2,1)S(1)} %copy-done.12, f32[320,1]{1,0:T(8,128)S(1)} %copy.17.b1), custom_call_target="tpu_custom_call" | custom-call | flops 2768240640 | bytes 12582912 | tf_op jit(solution)/shard_map/velocity/pallas_call | solution.py:259
  67.5 2.4 %copy-done = bf16[3520,768]{1,0:T(8,128)(2,1)} copy-done((bf16[3520,768]{1,0:T(8,128)(2,1)}, bf16[3520,768]{1,0:T(8,128)(2,1)S(1)}, u32[]{:S(2)}) %copy-start) | copy-done | bytes 5406744
  69.9 1.4 %copy-done.2 = f32[9,64,8,128]{3,2,1,0:T(8,128)} copy-done((f32[9,64,8,128]{3,2,1,0:T(8,128)}, f32[9,64,8,128]{3,2,1,0:T(8,128)S(1)}, u32[]{:S(2)}) %copy-start.2) | copy-done | bytes 2359320
  71.3 0.0 all-to-all-done.1.got
  71.3 1.5 %backward.1 = f32[3,64,8,128]{3,2,1,0:T(8,128)S(1)} custom-call(f32[32,2,3,8,128]{4,3,2,1,0:T(8,128)S(1)} %all-to-all-done.1.got, bf16[2,128,128]{2,1,0:T(8,128)(2,1)S(1)} %copy-done.9), custom_call_target="tpu_custom_call" | custom-call | tf_op jit(solution)/shard_map/backward/pallas_call | solution.py:421
  72.9 0.1 fusion.13
  73.0 4.9 %collective-permute-start.4 = (f32[3,64,3,128]{3,2,1,0:T(4,128)S(1)}, f32[3,64,3,128]{3,2,1,0:T(4,128)S(1)}, u32[]{:S(2)}, u32[]{:S(2)}) collective-permute-start(f32[3,64,3,128]{3,2,1,0:T(4,128)S(1)} %get-tuple-element.61), channel_id=1, source_target_pairs={{1,0},{2,1},{3,2},{4,3},{5,4},{6,5},{7,6},{8,7},{9,8},{10,9},{11,1... | collective-permute-start | bytes 884744 | tf_op jit(solution)/shard_map/ppermute | solution.py:31
  77.9 0.0 collective-permute-start.5
  77.9 5.3 %collective-permute-done.4 = f32[3,64,3,128]{3,2,1,0:T(4,128)S(1)} collective-permute-done((f32[3,64,3,128]{3,2,1,0:T(4,128)S(1)}, f32[3,64,3,128]{3,2,1,0:T(4,128)S(1)}, u32[]{:S(2)}, u32[]{:S(2)}) %collective-permute-start.4) | collective-permute-done | bytes 294944 | tf_op jit(solution)/shard_map/ppermute | solution.py:31
  83.2 4.6 %collective-permute-done.5 = f32[3,64,3,128]{3,2,1,0:T(4,128)S(1)} collective-permute-done((f32[3,64,3,128]{3,2,1,0:T(4,128)S(1)}, f32[3,64,3,128]{3,2,1,0:T(4,128)S(1)}, u32[]{:S(2)}, u32[]{:S(2)}) %collective-permute-start.5) | collective-permute-done | bytes 294944 | tf_op jit(solution)/shard_map/ppermute | solution.py:28
  87.8 0.3 fusion.7
  88.1 0.5 collective-permute-start.6
  88.6 1.6 %collective-permute-start.7 = (f32[3,3,16,128]{3,2,1,0:T(8,128)S(1)}, f32[3,3,16,128]{3,2,1,0:T(8,128)S(1)}, u32[]{:S(2)}, u32[]{:S(2)}) collective-permute-start(f32[3,3,16,128]{3,2,1,0:T(8,128)S(1)} %get-tuple-element.58), channel_id=1, source_target_pairs={{16,0},{0,16},{17,1},{1,17},{18,2},{2,18},{19,3},{3,19},{20,4},{4,... | collective-permute-start | bytes 221192 | tf_op jit(solution)/shard_map/ppermute | solution.py:31
  90.2 2.3 %collective-permute-done.6 = f32[3,3,16,128]{3,2,1,0:T(8,128)S(1)} collective-permute-done((f32[3,3,16,128]{3,2,1,0:T(8,128)S(1)}, f32[3,3,16,128]{3,2,1,0:T(8,128)S(1)}, u32[]{:S(2)}, u32[]{:S(2)}) %collective-permute-start.6) | collective-permute-done | bytes 73760 | tf_op jit(solution)/shard_map/ppermute | solution.py:28
  92.5 0.8 collective-permute-done.7
  93.3 0.3 fusion.5.lam
  93.7 19.4 %closure.1 = f32[3,64,8,128]{3,2,1,0:T(8,128)} custom-call(f32[3,70,16,128]{3,2,1,0:T(8,128)S(1)} %fusion.2.vel, f32[3,70,16,128]{3,2,1,0:T(8,128)S(1)} %fusion.5.lam, bf16[3520,768]{1,0:T(8,128)(2,1)S(1)} %copy-done.1, f32[9,64,8,128]{3,2,1,0:T(8,128)S(1)} %copy-done.3, bf16[320,896]{1,0:T(8,128)(2,1)S(1)} %slice_dynamic-update-slice_fusion.w2, ...), custom_call_target="tpu_custom_call" | custom-call | tf_op jit(solution)/shard_map/closure/pallas_call | solution.py:282
  (49 shorter events, 0.2 us)
Async XLA Ops:
  0.0 1.1 %copy-start.4 = (f32[3,64,8,128]{3,2,1,0:T(8,128)S(1)}, f32[3,64,8,128]{3,2,1,0:T(8,128)}, u32[]{:S(2)}) copy-start(f32[3,64,8,128]{3,2,1,0:T(8,128)} %cot.1) | copy-start | bytes 2359300
  1.1 0.8 copy-start.10
  2.0 10.7 %copy-start.13 = (f32[3,64,8,128]{3,2,1,0:T(8,128)S(1)}, f32[3,64,8,128]{3,2,1,0:T(8,128)}, u32[]{:S(2)}) copy-start(f32[3,64,8,128]{3,2,1,0:T(8,128)} %param.14) | copy-start | bytes 2359300
  5.4 12.6 %copy-start.20 = (bf16[32,3,3,3,3]{0,4,3,2,1:T(4,128)(2,1)S(1)}, bf16[32,3,3,3,3]{0,4,3,2,1:T(4,128)(2,1)}, u32[]{:S(2)}) copy-start(bf16[32,3,3,3,3]{0,4,3,2,1:T(4,128)(2,1)} %param.16) | copy-start | bytes 15556
  5.4 12.7 %copy-start.19 = (bf16[6,32,3,3,3]{1,4,3,2,0:T(4,128)(2,1)S(1)}, bf16[6,32,3,3,3]{1,4,3,2,0:T(4,128)(2,1)}, u32[]{:S(2)}) copy-start(bf16[6,32,3,3,3]{1,4,3,2,0:T(4,128)(2,1)} %param.18) | copy-start | bytes 31108
  5.4 12.8 %copy-start.17 = (bf16[81,5120]{1,0:T(8,128)(2,1)S(1)}, bf16[81,5120]{1,0:T(8,128)(2,1)}, u32[]{:S(2)}) copy-start(bf16[81,5120]{1,0:T(8,128)(2,1)} %constant.72.clone) | copy-start | bytes 2488324
  5.4 32.6 %all-to-all-start = ((f32[32,2,3,8,128]{4,3,2,1,0:T(8,128)}), f32[32,2,3,8,128]{4,3,2,1,0:T(8,128)S(1)}, u32[]{:S(2)}, u32[]{:S(2)}) async-start(f32[32,2,3,8,128]{4,3,2,1,0:T(8,128)} %forward.1), calls=%async_computation | async-start | bytes 1572864 | tf_op jit(solution)/shard_map/all_to_all | solution.py:450
  13.7 28.7 %collective-permute-start.1 = (f32[3,64,3,128]{3,2,1,0:T(4,128)}, f32[3,64,3,128]{3,2,1,0:T(4,128)}, u32[]{:S(2)}, u32[]{:S(2)}) collective-permute-start(f32[3,64,3,128]{3,2,1,0:T(4,128)} %get-tuple-element.63), channel_id=1, source_target_pairs={{1,0},{2,1},{3,2},{4,3},{5,4},{6,5},{7,6},{8,7},{9,8},{10,9},{11,1... | collective-permute-start | bytes 884744 | tf_op jit(solution)/shard_map/ppermute | solution.py:31
  18.0 24.4 %collective-permute-start = (f32[3,64,3,128]{3,2,1,0:T(4,128)}, f32[3,64,3,128]{3,2,1,0:T(4,128)}, u32[]{:S(2)}, u32[]{:S(2)}) collective-permute-start(f32[3,64,3,128]{3,2,1,0:T(4,128)} %get-tuple-element.64), channel_id=1, source_target_pairs={{0,1},{1,2},{2,3},{3,4},{4,5},{5,6},{6,7},{7,8},{8,9},{9,10},{10,1... | collective-permute-start | bytes 884744 | tf_op jit(solution)/shard_map/ppermute | solution.py:28
  18.7 0.7 copy-start.11
  19.4 6.8 %copy-start.18 = (bf16[81,2560]{1,0:T(8,128)(2,1)S(1)}, bf16[81,2560]{1,0:T(8,128)(2,1)}, u32[]{:S(2)}) copy-start(bf16[81,2560]{1,0:T(8,128)(2,1)} %constant.74.clone) | copy-start | bytes 1244164
  22.9 4.5 %copy-start.21 = (f32[32]{0:T(128)S(1)}, f32[32]{0:T(128)}, u32[]{:S(2)}) copy-start(f32[32]{0:T(128)} %param.17) | copy-start | bytes 388
  26.7 11.3 %copy-start.5 = (bf16[2,256,512]{2,1,0:T(8,128)(2,1)S(1)}, bf16[2,256,512]{2,1,0:T(8,128)(2,1)}, u32[]{:S(2)}) copy-start(bf16[2,256,512]{2,1,0:T(8,128)(2,1)} %constant.77.clone.bx) | copy-start | bytes 1572868
  26.7 11.3 %copy-start.6 = (bf16[2,256,512]{2,1,0:T(8,128)(2,1)S(1)}, bf16[2,256,512]{2,1,0:T(8,128)(2,1)}, u32[]{:S(2)}) copy-start(bf16[2,256,512]{2,1,0:T(8,128)(2,1)} %constant.76.clone.fx) | copy-start | bytes 1572868
  26.7 11.3 %copy-start.7 = (bf16[2,256,256]{2,1,0:T(8,128)(2,1)S(1)}, bf16[2,256,256]{2,1,0:T(8,128)(2,1)}, u32[]{:S(2)}) copy-start(bf16[2,256,256]{2,1,0:T(8,128)(2,1)} %constant.78.clone.by) | copy-start | bytes 786436
  26.7 11.3 %copy-start.8 = (bf16[2,256,256]{2,1,0:T(8,128)(2,1)S(1)}, bf16[2,256,256]{2,1,0:T(8,128)(2,1)}, u32[]{:S(2)}) copy-start(bf16[2,256,256]{2,1,0:T(8,128)(2,1)} %constant.75.clone.fy) | copy-start | bytes 786436
  42.5 2.9 %copy-start.14 = (f32[3,64,8,128]{3,2,1,0:T(8,128)S(1)}, f32[3,64,8,128]{3,2,1,0:T(8,128)}, u32[]{:S(2)}) copy-start(f32[3,64,8,128]{3,2,1,0:T(8,128)} %param.14) | copy-start | bytes 2359300
  42.5 28.8 %all-to-all-start.1 = ((f32[32,2,3,8,128]{4,3,2,1,0:T(8,128)}), f32[32,2,3,8,128]{4,3,2,1,0:T(8,128)S(1)}, u32[]{:S(2)}, u32[]{:S(2)}) async-start(f32[32,2,3,8,128]{4,3,2,1,0:T(8,128)} %middle.1), calls=%async_computation.1 | async-start | bytes 1572864 | tf_op jit(solution)/shard_map/all_to_all | solution.py:481
  45.3 8.7 %copy-start.15 = (f32[3,64,2,128]{3,2,1,0:T(2,128)}, f32[3,64,2,128]{3,2,1,0:T(2,128)S(1)}, u32[]{:S(2)}) copy-start(f32[3,64,2,128]{3,2,1,0:T(2,128)S(1)} %broadcast.160) | copy-start | bytes 589828
  46.8 7.2 %collective-permute-start.2 = (f32[3,3,16,128]{3,2,1,0:T(8,128)S(1)}, f32[3,3,16,128]{3,2,1,0:T(8,128)S(1)}, u32[]{:S(2)}, u32[]{:S(2)}) collective-permute-start(f32[3,3,16,128]{3,2,1,0:T(8,128)S(1)} %get-tuple-element.59), channel_id=1, source_target_pairs={{0,16},{16,0},{1,17},{17,1},{2,18},{18,2},{3,19},{19,3},{4,20},{20... | collective-permute-start | bytes 221192 | tf_op jit(solution)/shard_map/ppermute | solution.py:28
  48.6 8.6 %collective-permute-start.3 = (f32[3,3,16,128]{3,2,1,0:T(8,128)S(1)}, f32[3,3,16,128]{3,2,1,0:T(8,128)}, u32[]{:S(2)}, u32[]{:S(2)}) collective-permute-start(f32[3,3,16,128]{3,2,1,0:T(8,128)S(1)} %get-tuple-element.60), channel_id=1, source_target_pairs={{16,0},{0,16},{17,1},{1,17},{18,2},{2,18},{19,3},{3,19},{20,4},{4,... | collective-permute-start | bytes 221192 | tf_op jit(solution)/shard_map/ppermute | solution.py:31
  49.1 9.9 %copy-start.12 = (bf16[320,512]{1,0:T(8,128)(2,1)S(1)}, bf16[320,512]{1,0:T(8,128)(2,1)}, u32[]{:S(2)}) copy-start(bf16[320,512]{1,0:T(8,128)(2,1)} %copy-done.11) | copy-start | bytes 983044
  59.0 12.3 %copy-start.9 = (bf16[2,128,128]{2,1,0:T(8,128)(2,1)S(1)}, bf16[2,128,128]{2,1,0:T(8,128)(2,1)}, u32[]{:S(2)}) copy-start(bf16[2,128,128]{2,1,0:T(8,128)(2,1)} %constant.79.clone.table) | copy-start | bytes 196612
  67.5 2.4 %copy-start = (bf16[3520,768]{1,0:T(8,128)(2,1)}, bf16[3520,768]{1,0:T(8,128)(2,1)S(1)}, u32[]{:S(2)}) copy-start(bf16[3520,768]{1,0:T(8,128)(2,1)S(1)} %get-tuple-element.53.slope) | copy-start | bytes 16220164
  69.9 1.4 %copy-start.2 = (f32[9,64,8,128]{3,2,1,0:T(8,128)}, f32[9,64,8,128]{3,2,1,0:T(8,128)S(1)}, u32[]{:S(2)}) copy-start(f32[9,64,8,128]{3,2,1,0:T(8,128)S(1)} %get-tuple-element.54.grads) | copy-start | bytes 7077892
  71.3 16.5 %copy-start.16 = (f32[3,64,2,128]{3,2,1,0:T(2,128)S(1)}, f32[3,64,2,128]{3,2,1,0:T(2,128)}, u32[]{:S(2)}) copy-start(f32[3,64,2,128]{3,2,1,0:T(2,128)} %copy-done.15) | copy-start | bytes 589828
  72.9 20.8 %copy-start.3 = (f32[9,64,8,128]{3,2,1,0:T(8,128)S(1)}, f32[9,64,8,128]{3,2,1,0:T(8,128)}, u32[]{:S(2)}) copy-start(f32[9,64,8,128]{3,2,1,0:T(8,128)} %copy-done.2) | copy-start | bytes 7077892
  73.0 10.2 %collective-permute-start.4 = (f32[3,64,3,128]{3,2,1,0:T(4,128)S(1)}, f32[3,64,3,128]{3,2,1,0:T(4,128)S(1)}, u32[]{:S(2)}, u32[]{:S(2)}) collective-permute-start(f32[3,64,3,128]{3,2,1,0:T(4,128)S(1)} %get-tuple-element.61), channel_id=1, source_target_pairs={{1,0},{2,1},{3,2},{4,3},{5,4},{6,5},{7,6},{8,7},{9,8},{10,9},{11,1... | collective-permute-start | bytes 884744 | tf_op jit(solution)/shard_map/ppermute | solution.py:31
  77.9 9.9 %collective-permute-start.5 = (f32[3,64,3,128]{3,2,1,0:T(4,128)S(1)}, f32[3,64,3,128]{3,2,1,0:T(4,128)S(1)}, u32[]{:S(2)}, u32[]{:S(2)}) collective-permute-start(f32[3,64,3,128]{3,2,1,0:T(4,128)S(1)} %get-tuple-element.62), channel_id=1, source_target_pairs={{0,1},{1,2},{2,3},{3,4},{4,5},{5,6},{6,7},{7,8},{8,9},{9,10},{10,1... | collective-permute-start | bytes 884744 | tf_op jit(solution)/shard_map/ppermute | solution.py:28
  87.8 5.9 %copy-start.1 = (bf16[3520,768]{1,0:T(8,128)(2,1)S(1)}, bf16[3520,768]{1,0:T(8,128)(2,1)}, u32[]{:S(2)}) copy-start(bf16[3520,768]{1,0:T(8,128)(2,1)} %copy-done) | copy-start | bytes 16220164
  88.1 4.4 %collective-permute-start.6 = (f32[3,3,16,128]{3,2,1,0:T(8,128)S(1)}, f32[3,3,16,128]{3,2,1,0:T(8,128)S(1)}, u32[]{:S(2)}, u32[]{:S(2)}) collective-permute-start(f32[3,3,16,128]{3,2,1,0:T(8,128)S(1)} %get-tuple-element.57), channel_id=1, source_target_pairs={{0,16},{16,0},{1,17},{17,1},{2,18},{18,2},{3,19},{19,3},{4,20},{20... | collective-permute-start | bytes 221192 | tf_op jit(solution)/shard_map/ppermute | solution.py:28
  88.6 4.7 %collective-permute-start.7 = (f32[3,3,16,128]{3,2,1,0:T(8,128)S(1)}, f32[3,3,16,128]{3,2,1,0:T(8,128)S(1)}, u32[]{:S(2)}, u32[]{:S(2)}) collective-permute-start(f32[3,3,16,128]{3,2,1,0:T(8,128)S(1)} %get-tuple-element.58), channel_id=1, source_target_pairs={{16,0},{0,16},{17,1},{1,17},{18,2},{2,18},{19,3},{3,19},{20,4},{4,... | collective-permute-start | bytes 221192 | tf_op jit(solution)/shard_map/ppermute | solution.py:31
